TPU v7x, 32 devices: a whole 2x2x4 slice. The times are simulated.
32 devices in a mesh: dp: 4 (over y, x), proto: 8 (over z, core).
Axes of the slice: x: 2, y: 2, z: 4, core: 2. Of those that a mesh axis runs over, the one named last changes fastest.
Arguments:
- first_view: bfloat16 [2048, 128], P('dp'), may hold values from -6 to 6
- alternate_augmentation: bfloat16 [2048, 128], P('dp'), may hold values from -6 to 6
- prototypes: bfloat16 [32768, 128], P('proto'), may hold values from -6 to 6
Outputs:
- proto_grad: float32 [32768, 128], P('proto')
- token_grad: float32 [2048, 128], P('dp')
All inputs are finite; a program needn't handle non-finite values.
Results may differ from a plain program's by a relative error of at most 0.0003.
The roundings to bfloat16 on the way count: a program that leaves them out, or rounds other values in their place, can miss the bound.
Values may be sent and summed in bfloat16 or wider, within the bound.
No kernel may reach another device: no remote copies, remote signals or barrier semaphores. Data moves between devices by JAX's collectives and lax.ppermute only.
A program may use at most 64 MiB of HBM per device.

v0:
```python
import jax
import jax.numpy as jnp
from jax import lax
from jax.sharding import PartitionSpec as P

BALANCING_PASSES = 3


CODE_TEMP = 0.05
PRED_TEMP = 0.1


def normalize(values):
    floats = values.astype(jnp.float32)
    mean_square = jnp.mean(floats * floats, axis=-1, keepdims=True)
    inverse_root = lax.rsqrt(mean_square + 1e-06)
    return (floats * inverse_root).astype(jnp.bfloat16)


def exponential_piece(row_slice, centroid_block, softness_level):
    return jnp.exp(
        jnp.dot(row_slice, centroid_block.T, preferred_element_type=jnp.float32)
        / row_slice.shape[1]
        / softness_level
    )


def logit_grads(
    anchors,
    soft_labels,
    token_scale,
    divisor_value,
    centroid_block,
    cluster_center_factor,
    proto_total,
):
    assigned = (
        exponential_piece(anchors, centroid_block, CODE_TEMP)
        * cluster_center_factor[None, :]
        * token_scale[:, None]
    )
    predicted = exponential_piece(soft_labels, centroid_block, PRED_TEMP) / divisor_value[:, None]
    return (proto_total * (predicted - assigned)).astype(jnp.bfloat16)


def predicted_divisors(soft_labels, partition_pieces):
    return sum(
        [
            jnp.sum(exponential_piece(soft_labels, centroid_block, PRED_TEMP), axis=1)
            for centroid_block in partition_pieces
        ]
    )


def local(first_view, alternate_augmentation, prototypes):
    anchors = normalize(first_view)
    soft_labels = normalize(alternate_augmentation)
    centres = normalize(prototypes)
    tok_rows = anchors.shape[0]
    proto_rows = centres.shape[0]
    feature_count = anchors.shape[1]
    tile_cols = min(1024, proto_rows)
    piece_quantity = proto_rows // tile_cols
    protos_all = proto_rows * lax.axis_size("proto")
    tokens_all = tok_rows * lax.axis_size("dp")
    partition_pieces = [
        centres[piece_position * tile_cols : (piece_position + 1) * tile_cols]
        for piece_position in range(piece_quantity)
    ]
    token_scale = jnp.ones((tok_rows,), jnp.float32)
    cluster_center_factor = jnp.ones((proto_rows,), jnp.float32)
    for iteration_number in range(BALANCING_PASSES):
        nearby_matrix_cols = jnp.concatenate(
            [
                jnp.sum(
                    exponential_piece(anchors, centroid_block, CODE_TEMP) * token_scale[:, None],
                    axis=0,
                )
                for centroid_block in partition_pieces
            ]
        )
        prototype_marginals = lax.psum(nearby_matrix_cols, "dp")
        cluster_center_factor = 1.0 / (protos_all * prototype_marginals)
        kept_matrix_lines = sum(
            [
                jnp.sum(
                    exponential_piece(anchors, partition_pieces[piece_position], CODE_TEMP)
                    * cluster_center_factor[
                        piece_position * tile_cols : (piece_position + 1) * tile_cols
                    ][None, :],
                    axis=1,
                )
                for piece_position in range(piece_quantity)
            ]
        )
        if iteration_number == 0:
            row_total = lax.psum(kept_matrix_lines, "proto")
        else:
            row_total = lax.psum(kept_matrix_lines, "proto")
        token_scale = 1.0 / row_total
    divisor_value = lax.psum(predicted_divisors(soft_labels, partition_pieces), "proto")
    token_sum = jnp.zeros((tok_rows, feature_count), jnp.float32)
    grad_tiles = []
    for piece_position in range(piece_quantity):
        block_scale = cluster_center_factor[
            piece_position * tile_cols : (piece_position + 1) * tile_cols
        ]
        logit_grad = logit_grads(
            anchors,
            soft_labels,
            token_scale,
            divisor_value,
            partition_pieces[piece_position],
            block_scale,
            protos_all,
        )
        token_sum = token_sum + jnp.dot(
            logit_grad, partition_pieces[piece_position], preferred_element_type=jnp.float32
        )
        grad_tiles.append(logit_grad)
    local_protos = jnp.concatenate(
        [
            jnp.dot(logit_grad.T, soft_labels, preferred_element_type=jnp.float32)
            for logit_grad in grad_tiles
        ],
        axis=0,
    )
    proto_total = lax.psum(local_protos, "dp")
    token_count_sum = lax.psum(token_sum, "proto")
    return (proto_total * tokens_all ** (-0.5), token_count_sum * protos_all ** (-0.5))


def solution(mesh):
    return jax.shard_map(
        local,
        mesh=mesh,
        in_specs=(P("dp", None), P("dp", None), P("proto", None)),
        out_specs=(P("proto", None), P("dp", None)),
        check_vma=False,
    )
```

profile of v0, /device:TPU:0, one launch (start us, length us, event | category | flops | bytes accessed | tf_op | source)
XLA Modules:
  0.0 274.8 jit_solution(3370033439990803510)
XLA Ops:
  8.3 1.8 fusion
  10.2 1.7 fusion.1
  11.9 1.8 fusion.5
  13.8 1.9 fusion.4
  15.7 1.8 fusion.3
  17.5 1.8 fusion.2
  20.0 1.8 fusion.48
  21.8 1.8 fusion.47
  23.6 1.8 fusion.46
  25.4 17.5 %psum.64 = f32[4096]{0:T(1024)S(1)} all-reduce(f32[4096]{0:T(1024)S(1)} %pad_maximum_fusion.1), channel_id=1, replica_groups=mesh['dp'=4,'proto'=8] {'dp'}, use_global_device_ids=true, to_apply=%region_12.0 | all-reduce | flops 4096 | bytes 32768 | tf_op jit(solution)/shard_map/psum | solution.py:82
  43.0 2.1 multiply_reduce_fusion.14
  46.2 13.6 %psum.65 = f32[512]{0:T(512)S(1)} all-reduce(f32[512]{0:T(512)S(1)} %add_add_fusion.2), channel_id=1, replica_groups=mesh['dp'=4,'proto'=8] {'proto'}, use_global_device_ids=true, to_apply=%region_17.0 | all-reduce | flops 512 | bytes 4096 | tf_op jit(solution)/shard_map/psum | solution.py:97
  59.8 4.0 %multiply_reduce_fusion.11 = (f32[1024]{0:T(1024)S(1)}, f32[1024]{0:T(1024)S(1)}, f32[1024]{0:T(1024)S(1)}, f32[1024]{0:T(1024)S(1)}) fusion(f32[512,1024]{1,0:T(8,128)S(1)} %get-tuple-element.35, f32[512]{0:T(512)S(1)} %broadcast_divide_fusion.2, f32[512,1024]{1,0:T(8,128)} %get-tuple-element.33, f32[512,1024]{1,0:T(8,128)} %get-tuple-element.31, ...), kind=kLoop, calls=%fused_computation.20 | loop fusion | flops 4190208 | bytes 8407040 | tf_op jit(solution)/shard_map/reduce_sum | solution.py:75
  63.8 13.7 %psum.66 = f32[4096]{0:T(1024)S(1)} all-reduce(f32[4096]{0:T(1024)S(1)} %pad_maximum_fusion.2), channel_id=1, replica_groups=mesh['dp'=4,'proto'=8] {'dp'}, use_global_device_ids=true, to_apply=%region_22.0 | all-reduce | flops 4096 | bytes 32768 | tf_op jit(solution)/shard_map/psum | solution.py:82
  77.6 2.0 multiply_reduce_fusion.6
  80.8 13.6 %psum.67 = f32[512]{0:T(512)S(1)} all-reduce(f32[512]{0:T(512)S(1)} %add_add_fusion.1), channel_id=1, replica_groups=mesh['dp'=4,'proto'=8] {'proto'}, use_global_device_ids=true, to_apply=%region_27.0 | all-reduce | flops 512 | bytes 4096 | tf_op jit(solution)/shard_map/psum | solution.py:99
  94.4 4.0 %multiply_reduce_fusion.3 = (f32[1024]{0:T(1024)S(1)}, f32[1024]{0:T(1024)S(1)}, f32[1024]{0:T(1024)S(1)}, f32[1024]{0:T(1024)S(1)}) fusion(f32[512,1024]{1,0:T(8,128)S(1)} %get-tuple-element.35, f32[512]{0:T(512)S(1)} %broadcast_divide_fusion.1, f32[512,1024]{1,0:T(8,128)} %get-tuple-element.33, f32[512,1024]{1,0:T(8,128)} %get-tuple-element.31, ...), kind=kLoop, calls=%fused_computation.12 | loop fusion | flops 4190208 | bytes 8407040 | tf_op jit(solution)/shard_map/reduce_sum | solution.py:75
  98.5 15.4 %psum.68 = f32[4096]{0:T(1024)S(1)} all-reduce(f32[4096]{0:T(1024)S(1)} %pad_maximum_fusion.3), channel_id=1, replica_groups=mesh['dp'=4,'proto'=8] {'dp'}, use_global_device_ids=true, to_apply=%region_32.0 | all-reduce | flops 4096 | bytes 32768 | tf_op jit(solution)/shard_map/psum | solution.py:82
  113.9 2.0 multiply_reduce_fusion.18
  117.2 13.8 %all-reduce = (f32[512]{0:T(512)S(1)}, f32[512]{0:T(512)S(1)}) all-reduce(f32[512]{0:T(512)S(1)} %add_add_fusion, f32[512]{0:T(512)S(1)} %add_add_fusion.3), channel_id=1, replica_groups=mesh['dp'=4,'proto'=8] {'proto'}, use_global_device_ids=true, to_apply=%region_37.0 | all-reduce | flops 1024 | bytes 8192 | tf_op jit(solution)/shard_map/psum | solution.py:99
  131.0 6.6 %multiply_convert_fusion.3 = (bf16[512,1024]{1,0:T(8,128)(2,1)S(1)}, bf16[512,1024]{1,0:T(8,128)(2,1)S(1)}, bf16[512,1024]{1,0:T(8,128)(2,1)S(1)}, bf16[512,1024]{1,0:T(8,128)(2,1)S(1)}) fusion(f32[512,1024]{1,0:T(8,128)S(1)} %get-tuple-element.35, f32[512,1024]{1,0:T(8,128)} %get-tuple-element.41, f32[512]{0:T(512)S(1)} %broadcast_divide_fusion, ...), kind=kLoop, calls=%fused_computation.8 | loop fusion | flops 14680064 | bytes 20992000 | tf_op jit(solution)/shard_map/convert_element_type | solution.py:43
  144.8 47.4 %all-reduce.6.cloned.1.call-done = f32[512,128]{1,0:T(8,128)} async-done(((f32[512,128]{1,0:T(8,128)}), f32[512,128]{1,0:T(8,128)}) %all-reduce.6.cloned.1.call-update) | async-done | bytes 262160 | tf_op jit(solution)/shard_map/psum | solution.py:129
  193.9 71.0 %all-reduce.4.cloned.1.call-done = f32[4096,128]{1,0:T(8,128)} async-done(((f32[4096,128]{1,0:T(8,128)}), f32[4096,128]{1,0:T(8,128)}) %all-reduce.4.cloned.1.call-update) | async-done | bytes 2097168 | tf_op jit(solution)/shard_map/psum | solution.py:128
  264.9 3.1 %broadcast_multiply_fusion = f32[4096,128]{1,0:T(8,128)} fusion(f32[4096,128]{1,0:T(8,128)} %all-reduce.4.cloned.1.call-done), kind=kLoop, calls=%fused_computation.44 | loop fusion | flops 524288 | bytes 4194304 | tf_op jit(solution)/shard_map/mul | solution.py:130
  (75 shorter events, 14.3 us)
Async XLA Ops:
  7.2 4.8 %copy-start.6 = (bf16[512,128]{1,0:T(8,128)(2,1)S(1)}, bf16[512,128]{1,0:T(8,128)(2,1)}, u32[]{:S(2)}) copy-start(bf16[512,128]{1,0:T(8,128)(2,1)} %param.4) | copy-start | bytes 393220
  7.2 185.0 %all-reduce.6.cloned.1.call-start = ((), (), s32[]{:S(2)}) async-start(), calls=%async_computation.1 | async-start | bytes 524288 | tf_op jit(solution)/shard_map/psum | solution.py:129
  15.7 3.6 %copy-start.15 = (bf16[512,128]{1,0:T(8,128)(2,1)S(1)}, bf16[512,128]{1,0:T(8,128)(2,1)}, u32[]{:S(2)}) copy-start(bf16[512,128]{1,0:T(8,128)(2,1)} %param.3) | copy-start | bytes 393220
  42.9 2.2 copy-start
  42.9 2.8 %copy-start.3 = (f32[512,1024]{1,0:T(8,128)S(1)}, f32[512,1024]{1,0:T(8,128)}, u32[]{:S(2)}) copy-start(f32[512,1024]{1,0:T(8,128)} %get-tuple-element.29) | copy-start | bytes 6291460
  77.5 2.2 copy-start.4
  77.5 2.8 %copy-start.1 = (f32[512,1024]{1,0:T(8,128)S(1)}, f32[512,1024]{1,0:T(8,128)}, u32[]{:S(2)}) copy-start(f32[512,1024]{1,0:T(8,128)} %get-tuple-element.31) | copy-start | bytes 6291460
  113.9 2.2 copy-start.5
  113.9 2.8 %copy-start.2 = (f32[512,1024]{1,0:T(8,128)S(1)}, f32[512,1024]{1,0:T(8,128)}, u32[]{:S(2)}) copy-start(f32[512,1024]{1,0:T(8,128)} %get-tuple-element.31) | copy-start | bytes 6291460
  137.6 1.4 copy-start.7
  137.6 1.4 copy-start.11
  137.6 1.6 copy-start.13
  137.6 2.0 copy-start.9
  139.6 1.2 copy-start.14
  139.6 1.8 copy-start.12
  140.7 1.3 copy-start.10
  140.8 124.1 %all-reduce.4.cloned.1.call-start = ((), (), s32[]{:S(2)}) async-start(), calls=%async_computation | async-start | bytes 4194304 | tf_op jit(solution)/shard_map/psum | solution.py:128
  141.4 1.3 copy-start.8
Sparse Core Ops, SparseCore 0:
  140.9 51.2 all-reduce.5
  196.2 68.6 all-reduce.3
where the time goes:
time: 275 us
  waiting for transfers between devices  118 us (43%)
  blocking collectives  87.6 us (32%)
  other arithmetic  33.4 us (12%)
  matrix products  18.1 us (7%)
  between operations  14.3 us (5%)
  local copies, waits for them, and re-layouts  2.86 us (1%)
    psum x1, waiting for transfers between devices, local(): proto_total = lax.psum(local_protos, 'dp')  71 us
    psum x1, waiting for transfers between devices, local(): token_count_sum = lax.psum(token_sum, 'proto')  47.4 us
    psum x3, blocking collectives, local(): prototype_marginals = lax.psum(nearby_matrix_cols, 'dp')  46.6 us
    psum x3, blocking collectives, local(): row_total = lax.psum(kept_matrix_lines, 'proto')  41 us
    dot_general x8, matrix products, exponential_piece(): jnp.dot(row_slice, centroid_block.T, preferred_element_type=jnp.float32)  13.3 us
    reduce_sum x2, other arithmetic, local(): jnp.sum(exponential_piece(anchors, centroid_block, CODE_TEMP) * token_sca...  8.03 us
    reduce_sum x10, other arithmetic, local(): jnp.sum(exponential_piece(anchors, partition_pieces[piece_position], CODE...  7.65 us
    convert_element_type x1, other arithmetic, logit_grads(): return (proto_total * (predicted - assigned)).astype(jnp.bfloat16)  6.59 us
  transfers between devices with their start and end apart: 2, of which 2 were waited for; matrix products, arithmetic and copies ran while one was open for 2% of the time, Pallas kernels for 0%

commit v1 on v0

v1 whole, which is shorter than its diff:
```python
import functools
import math

import jax
import jax.numpy as jnp
from jax import lax
from jax.experimental import pallas as pl
from jax.experimental.pallas import tpu as pltpu
from jax.sharding import PartitionSpec as P

CODE_TEMP = 0.05
PRED_TEMP = 0.1
F32 = jnp.float32
BF16 = jnp.bfloat16
VMEM_LIMIT = 20 << 20


def vmem_spec():
    return pl.BlockSpec(memory_space=pltpu.VMEM)


def shape(*dims, dtype=F32):
    return jax.ShapeDtypeStruct(dims, dtype)


def normalize(values):
    floats = values.astype(F32)
    mean_square = jnp.mean(floats * floats, axis=-1, keepdims=True)
    return (floats * lax.rsqrt(mean_square + 1e-06)).astype(BF16)


def rows(i, size):
    return pl.ds(pl.multiple_of(i * size, size), size)


def similarity(a, b):
    return lax.dot_general(a, b, (((1,), (1,)), ((), ())), preferred_element_type=F32)


def sublane_sums(block):
    return jnp.sum(block.reshape(block.shape[0] // 8, 8, block.shape[1]), axis=0)


def first_pass(*refs, parts, block, scale, total):
    proto_ref, token_refs = refs[0], refs[1 : 1 + parts]
    code_ref, centre_ref, out_ref, tok, acc = refs[1 + parts :]
    n = token_refs[0].shape[0]
    for i, t in enumerate(token_refs):
        tok[i * n : (i + 1) * n, :] = normalize(t[...])
    acc[...] = jnp.zeros_like(acc)

    def step(i, carry):
        at = rows(i, block)
        centre = normalize(proto_ref[at, :])
        centre_ref[at, :] = centre
        code = jnp.exp2(similarity(centre, tok[...]) * scale)
        code_ref[at, :] = code
        factor = 1.0 / (total * jnp.sum(code, axis=1, keepdims=True))
        acc[...] += sublane_sums(code * factor)
        return carry

    lax.fori_loop(0, proto_ref.shape[0] // block, step, 0)
    out_ref[...] = jnp.sum(acc[...], axis=0, keepdims=True)


def denominators(*refs, parts, block, scale):
    centre_ref, token_refs = refs[0], refs[1 : 1 + parts]
    tok, out_ref, acc = refs[1 + parts :]
    n = token_refs[0].shape[0]
    for i, t in enumerate(token_refs):
        tok[i * n : (i + 1) * n, :] = normalize(t[...])
    acc[...] = jnp.zeros_like(acc)

    def step(i, carry):
        centre = centre_ref[rows(i, block), :]
        acc[...] += sublane_sums(jnp.exp2(similarity(centre, tok[...]) * scale))
        return carry

    lax.fori_loop(0, centre_ref.shape[0] // block, step, 0)
    out_ref[...] = jnp.sum(acc[...], axis=0, keepdims=True)


def middle_pass(*refs, parts, block, total, extra):
    code_ref, sum_refs = refs[0], refs[1 : 1 + parts]
    if extra:
        extra_ref, out_ref, factor_ref, acc = refs[1 + parts :]
    else:
        out_ref, factor_ref, acc = refs[1 + parts :]
    sums = sum_refs[0][0:1, :]
    for s in sum_refs[1:]:
        sums = sums + s[0:1, :]
    token_scale = 1.0 / sums
    acc[...] = jnp.zeros_like(acc)

    def step(i, carry):
        at = rows(i, block)
        code = code_ref[at, :]
        factor = 1.0 / (total * jnp.sum(code * token_scale, axis=1, keepdims=True))
        factor_ref[at, :] = factor
        acc[...] += sublane_sums(code * factor)
        return carry

    lax.fori_loop(0, code_ref.shape[0] // block, step, 0)
    out_ref[0:1, :] = jnp.sum(acc[...], axis=0, keepdims=True)
    if extra:
        out_ref[1:2, :] = extra_ref[...]


def token_part(*refs, parts, block, scale, total, own):
    code_ref, centre_ref, tok_ref, factor_ref = refs[:4]
    sum_refs, den_refs = refs[4 : 4 + parts], refs[4 + parts : 4 + 2 * parts]
    grad_ref, logit_ref, scales_ref, acc = refs[4 + 2 * parts :]
    sums, den = sum_refs[0][0:1, :], den_refs[0][1:2, :]
    for s in sum_refs[1:]:
        sums = sums + s[0:1, :]
    for d in den_refs[1:]:
        den = den + d[1:2, :]
    scales_ref[0:1, :] = total / sums
    scales_ref[1:2, :] = total / den
    acc[...] = jnp.zeros_like(acc)
    token_scale, weight = scales_ref[0:1, :own], scales_ref[1:2, :own]

    def step(i, carry):
        at = rows(i, block)
        centre = centre_ref[at, :]
        pred = jnp.exp2(similarity(centre, tok_ref[:own, :]) * scale)
        code = code_ref[at, :own]
        logit = (pred * weight - code * factor_ref[at, :] * token_scale).astype(BF16)
        logit_ref[at, :] = logit
        acc[...] += lax.dot_general(
            centre, logit, (((0,), (0,)), ((), ())), preferred_element_type=F32
        )
        return carry

    lax.fori_loop(0, code_ref.shape[0] // block, step, 0)
    grad_ref[...] = acc[...].T * total ** (-0.5)


def proto_part(
    code_ref, centre_ref, tok_ref, factor_ref, scales_ref, logit_ref, out_ref, *, block, scale, own
):
    tokens = code_ref.shape[1]
    token_scale, weight = scales_ref[0:1, own:], scales_ref[1:2, own:]

    def step(i, carry):
        at = rows(i, block)
        pred = jnp.exp2(similarity(centre_ref[at, :], tok_ref[own:, :]) * scale)
        code = code_ref[at, own:]
        logit = (pred * weight - code * factor_ref[at, :] * token_scale).astype(BF16)
        grad = jnp.dot(logit, tok_ref[own:, :], preferred_element_type=F32)
        grad += jnp.dot(logit_ref[at, :], tok_ref[:own, :], preferred_element_type=F32)
        out_ref[at, :] = grad * tokens ** (-0.5)
        return carry

    lax.fori_loop(0, code_ref.shape[0] // block, step, 0)


def shifted(x, axis):
    n = lax.axis_size(axis)
    return [x] + [
        lax.ppermute(x, axis, [(i, (i + s) % n) for i in range(n)]) for s in range(1, n)
    ]


def swapped(x, axis, mask):
    return lax.ppermute(x, axis, [(i, i ^ mask) for i in range(lax.axis_size(axis))])


def proto_terms(x):
    n = lax.axis_size("proto")
    x = x + swapped(x, "proto", 1)
    terms, unit = [x], 2
    while unit < n:
        group = min(4, n // unit)
        if unit > 2:
            terms = [sum(terms)]
        terms = [terms[0]] + [swapped(terms[0], "proto", unit * m) for m in range(1, group)]
        unit *= group
    return terms


def proto_sum(x):
    n = lax.axis_size("proto")
    core = lax.rem(lax.axis_index("proto"), 2)
    half = x.shape[0] // 2
    mine = lax.dynamic_slice_in_dim(x, core * half, half)
    other = lax.dynamic_slice_in_dim(x, (1 - core) * half, half)
    mine = mine + swapped(other, "proto", 1)
    unit = 2
    while unit < n:
        group = min(4, n // unit)
        mine = sum([swapped(mine, "proto", unit * m) for m in range(1, group)], mine)
        unit *= group
    other = swapped(mine, "proto", 1)
    return jnp.where(
        core == 0, jnp.concatenate([mine, other]), jnp.concatenate([other, mine])
    )


def local(first_view, alternate_augmentation, prototypes):
    own, d = first_view.shape
    k = prototypes.shape[0]
    tokens = own * lax.axis_size("dp")
    total = float(k * lax.axis_size("proto"))
    log2e = math.log2(math.e)
    code_scale = log2e / d / CODE_TEMP
    pred_scale = log2e / d / PRED_TEMP
    views = shifted(first_view, "dp")
    others = shifted(alternate_augmentation, "dp")
    dp = len(views)
    block = min(512, k)

    def run(body, outs, args, scratch, resident=(), keep=(), us=1.0):
        shapes = tuple(pltpu.VMEM(s.shape, s.dtype) if i in keep else s for i, s in enumerate(outs))
        args = [
            pltpu.with_memory_space_constraint(a, pltpu.VMEM) if i in resident else a
            for i, a in enumerate(args)
        ]
        return pl.pallas_call(
            body,
            out_shape=shapes,
            in_specs=[vmem_spec()] * len(args),
            out_specs=tuple(vmem_spec() for _ in outs),
            scratch_shapes=scratch,
            compiler_params=pltpu.CompilerParams(vmem_limit_bytes=VMEM_LIMIT),
            cost_estimate=pl.CostEstimate(
                flops=int(us * 1e9), bytes_accessed=1 << 20, transcendentals=0
            ),
        )(*args)

    acc = pltpu.VMEM((8, tokens), F32)
    code, centres, sums = run(
        functools.partial(first_pass, parts=dp, block=block, scale=code_scale, total=total),
        [shape(k, tokens), shape(k, d, dtype=BF16), shape(1, tokens)],
        [prototypes] + views,
        [pltpu.VMEM((tokens, d), BF16), acc],
        keep=(0, 1),
        us=8,
    )
    terms = proto_terms(sums)
    tok, den = run(
        functools.partial(denominators, parts=dp, block=block, scale=pred_scale),
        [shape(tokens, d, dtype=BF16), shape(1, tokens)],
        [centres] + others,
        [acc],
        resident=(0,),
        keep=(0,),
        us=6,
    )
    sums, _ = run(
        functools.partial(middle_pass, parts=len(terms), block=block, total=total, extra=True),
        [shape(2, tokens), shape(k, 1)],
        [code] + terms + [den],
        [acc],
        resident=(0,),
        keep=(1,),
        us=5,
    )
    den_terms = proto_terms(sums)
    sums, factor = run(
        functools.partial(
            middle_pass, parts=len(den_terms), block=block, total=total, extra=False
        ),
        [shape(1, tokens), shape(k, 1)],
        [code] + den_terms,
        [acc],
        resident=(0,),
        keep=(1,),
        us=5,
    )
    terms = proto_terms(sums)
    token_grad, logit, scales = run(
        functools.partial(
            token_part, parts=len(terms), block=block, scale=pred_scale, total=total, own=own
        ),
        [shape(own, d), shape(k, own, dtype=BF16), shape(2, tokens)],
        [code, centres, tok, factor] + terms + den_terms,
        [pltpu.VMEM((d, own), F32)],
        resident=(0, 1, 2, 3),
        keep=(1, 2),
        us=4,
    )
    (proto_grad,) = run(
        functools.partial(proto_part, block=block, scale=pred_scale, own=own),
        [shape(k, d)],
        [code, centres, tok, factor, scales, logit],
        [],
        resident=(0, 1, 2, 3, 4, 5),
        us=10,
    )
    return proto_grad, proto_sum(token_grad)


def solution(mesh):
    return jax.shard_map(
        local,
        mesh=mesh,
        in_specs=(P("dp", None), P("dp", None), P("proto", None)),
        out_specs=(P("proto", None), P("dp", None)),
        check_vma=False,
    )
```

time: 275 us -> 157 us (0.57)
  waiting for transfers between devices: 118 us -> 25 us
  blocking collectives: 87.6 us -> 0 us
  local copies, waits for them, and re-layouts: 2.86 us -> 54.1 us
  Pallas kernels: 0 us -> 45.5 us
  other arithmetic: 33.4 us -> 4.02 us
  starting transfers between devices: 0.08 us -> 27.1 us
  matrix products: 18.1 us -> 0 us
  between operations: 14.3 us -> 0.83 us
    psum x2 -> x0, waiting for transfers between devices: 118 us -> none  [the longest x1 71 us: local(): proto_total = lax.psum(local_protos, 'dp')]
    psum x6 -> x0, blocking collectives: 87.6 us -> none  [the longest x3 46.6 us: local(): prototype_marginals = lax.psum(nearby_matrix_cols, 'dp')]
    unnamed x32 -> x48, local copies, waits for them, and re-layouts: 2.84 us -> 53.1 us
    pallas_call x0 -> x6, Pallas kernels: none -> 45.5 us  [run(): pl.pallas_call(body, out_shape=shapes, in_specs=[vmem_spec()] * len(args)...]
    ppermute x0 -> x23, starting transfers between devices: none -> 27.1 us  [the longest x17 18 us: swapped(): lax.ppermute(x, axis, [(i, i ^ mask) for i in range(lax.axis_size(axis))])]
    ppermute x0 -> x23, waiting for transfers between devices: none -> 25 us  [the longest x17 22.2 us: swapped(): lax.ppermute(x, axis, [(i, i ^ mask) for i in range(lax.axis_size(axis))])]
    reduce_sum x15 -> x0, other arithmetic: 18.7 us -> none  [the longest x2 8.03 us: local(): jnp.sum(exponential_piece(anchors, centroid_block, CODE_TEMP) * token_sca...]
    dot_general x16 -> x0, matrix products: 18.1 us -> none  [the longest x8 13.3 us: exponential_piece(): jnp.dot(row_slice, centroid_block.T, preferred_element_type=jnp.float32)]
  transfers between devices with their start and end apart: 2 -> 23, of which waited for: 2 -> 13; matrix products, arithmetic and copies ran while one was open for 2% -> 0% of each run, Pallas kernels for 0% -> 17%
where the time goes in v1:
time: 157 us; the launch traced here: 156 us
  local copies, waits for them, and re-layouts  54.1 us (34%)
  Pallas kernels  45.5 us (29%)
  starting transfers between devices  27.1 us (17%)
  waiting for transfers between devices  25 us (16%)
  other arithmetic  4.02 us (3%)
    unnamed x48, local copies, waits for them, and re-layouts  53.1 us
    pallas_call x6, Pallas kernels, run(): pl.pallas_call(body, out_shape=shapes, in_specs=[vmem_spec()] * len(args)...  45.5 us
    ppermute x17, waiting for transfers between devices, swapped(): lax.ppermute(x, axis, [(i, i ^ mask) for i in range(lax.axis_size(axis))])  22.2 us
    ppermute x17, starting transfers between devices, swapped(): lax.ppermute(x, axis, [(i, i ^ mask) for i in range(lax.axis_size(axis))])  18 us
    ppermute x6, starting transfers between devices, shifted(): lax.ppermute(x, axis, [(i, (i + s) % n) for i in range(n)])  9.1 us
  transfers between devices with their start and end apart: 23, of which 13 were waited for; matrix products, arithmetic and copies ran while one was open for 0% of the time, Pallas kernels for 17%

profile of v1, /device:TPU:0, one launch (start us, length us, event | category | flops | bytes accessed | tf_op | source)
XLA Modules:
  0.0 156.4 jit_solution(3196702376614831746)
XLA Ops:
  0.6 3.0 %collective-permute-start = (bf16[512,128]{1,0:T(8,128)(2,1)}, bf16[512,128]{1,0:T(8,128)(2,1)S(1)}, u32[]{:S(2)}, u32[]{:S(2)}) collective-permute-start(bf16[512,128]{1,0:T(8,128)(2,1)} %refs_1_.2), channel_id=1, source_target_pairs={{0,8},{8,16},{16,24},{24,0},{1,9},{9,17},{17,25},{25,1},{2,10},{10... | collective-permute-start | bytes 393224 | tf_op jit(solution)/shard_map/ppermute | solution.py:161
  9.1 2.1 %collective-permute-start.5 = (bf16[512,128]{1,0:T(8,128)(2,1)}, bf16[512,128]{1,0:T(8,128)(2,1)S(1)}, u32[]{:S(2)}, u32[]{:S(2)}) collective-permute-start(bf16[512,128]{1,0:T(8,128)(2,1)} %refs_1_.3), channel_id=1, source_target_pairs={{0,24},{8,0},{16,8},{24,16},{1,25},{9,1},{17,9},{25,17},{2,26},{10... | collective-permute-start | bytes 393224 | tf_op jit(solution)/shard_map/ppermute | solution.py:161
  13.4 10.5 %shard_map.50 = (f32[4096,2048]{1,0:T(8,128)S(1)}, bf16[4096,128]{1,0:T(8,128)(2,1)S(1)}, f32[1,2048]{1,0:T(1,128)S(1)}) custom-call(bf16[4096,128]{1,0:T(8,128)(2,1)} %refs_0_.1, bf16[512,128]{1,0:T(8,128)(2,1)S(1)} %copy-done.10, bf16[512,128]{1,0:T(8,128)(2,1)S(1)} %collective-permute-done.refs_2_, bf16[512,128]{1,0:T(8,128)(2,1)S(1)} %collective-permute-done.1.refs_3_, ...), custom_call_target="tpu_custom_call" | custom-call | flops 8000000000 | bytes 1048576 | tf_op jit(solution)/shard_map/pallas_call | solution.py:219
  23.9 11.1 %copy-done = f32[4096,2048]{1,0:T(8,128)} copy-done((f32[4096,2048]{1,0:T(8,128)}, f32[4096,2048]{1,0:T(8,128)S(1)}, u32[]{:S(2)}) %copy-start) | copy-done | bytes 33554456
  36.2 1.7 %collective-permute-start.7 = (f32[1,2048]{1,0:T(1,128)S(1)}, f32[1,2048]{1,0:T(1,128)S(1)}, u32[]{:S(2)}, u32[]{:S(2)}) collective-permute-start(f32[1,2048]{1,0:T(1,128)S(1)} %add.27.refs_1_), channel_id=1, source_target_pairs={{0,2},{1,3},{2,0},{3,1},{4,6},{5,7},{6,4},{7,5},{8,10},{9,11},{10,... | collective-permute-start | bytes 24584 | tf_op jit(solution)/shard_map/ppermute | solution.py:166
  37.9 2.6 %collective-permute-start.8 = (f32[1,2048]{1,0:T(1,128)S(1)}, f32[1,2048]{1,0:T(1,128)S(1)}, u32[]{:S(2)}, u32[]{:S(2)}) collective-permute-start(f32[1,2048]{1,0:T(1,128)S(1)} %add.27.refs_1_), channel_id=1, source_target_pairs={{0,4},{1,5},{2,6},{3,7},{4,0},{5,1},{6,2},{7,3},{8,12},{9,13},{10,... | collective-permute-start | bytes 24584 | tf_op jit(solution)/shard_map/ppermute | solution.py:166
  40.6 6.1 %shard_map.51 = (bf16[2048,128]{1,0:T(8,128)(2,1)S(1)}, f32[1,2048]{1,0:T(1,128)S(1)}) custom-call(bf16[4096,128]{1,0:T(8,128)(2,1)S(1)} %get-tuple-element.14.refs_0_.refs_1_.centre_ref, bf16[512,128]{1,0:T(8,128)(2,1)S(1)} %copy-done.11, bf16[512,128]{1,0:T(8,128)(2,1)S(1)} %collective-permute-done.3.refs_2_, ...), custom_call_target="tpu_custom_call" | custom-call | flops 6000000000 | bytes 1048576 | tf_op jit(solution)/shard_map/pallas_call | solution.py:219
  48.8 10.5 %copy-done.1 = f32[4096,2048]{1,0:T(8,128)S(1)} copy-done((f32[4096,2048]{1,0:T(8,128)S(1)}, f32[4096,2048]{1,0:T(8,128)}, u32[]{:S(2)}) %copy-start.1) | copy-done | bytes 33554456
  59.3 6.6 %shard_map.52 = (f32[2,2048]{1,0:T(2,128)}, f32[4096,1]{1,0:T(8,128)}) custom-call(f32[4096,2048]{1,0:T(8,128)S(1)} %copy-done.1, f32[1,2048]{1,0:T(1,128)} %copy-done.17, f32[1,2048]{1,0:T(1,128)} %copy-done.21, f32[1,2048]{1,0:T(1,128)} %copy-done.22, f32[1,2048]{1,0:T(1,128)} %copy-done.23, f32[1,2048]{1,0:T(1,128)} %copy-done.9), custom_call_target="tpu_custom_call" | custom-call | flops 5000000000 | bytes 1048576 | tf_op jit(solution)/shard_map/pallas_call | solution.py:219
  68.8 3.5 %collective-permute-start.12 = (f32[2,2048]{1,0:T(2,128)S(1)}, f32[2,2048]{1,0:T(2,128)S(1)}, u32[]{:S(2)}, u32[]{:S(2)}) collective-permute-start(f32[2,2048]{1,0:T(2,128)S(1)} %add.28.refs_1_.refs_8_), channel_id=1, source_target_pairs={{0,4},{1,5},{2,6},{3,7},{4,0},{5,1},{6,2},{7,3},{8,12},{9,13},{10,... | collective-permute-start | bytes 49160 | tf_op jit(solution)/shard_map/ppermute | solution.py:166
  72.5 1.6 collective-permute-done.12.refs_3_.refs_10_
  74.0 3.8 %collective-permute-done.13.refs_4_.refs_11_ = f32[2,2048]{1,0:T(2,128)S(1)} collective-permute-done((f32[2,2048]{1,0:T(2,128)S(1)}, f32[2,2048]{1,0:T(2,128)S(1)}, u32[]{:S(2)}, u32[]{:S(2)}) %collective-permute-start.13) | collective-permute-done | bytes 16416 | tf_op jit(solution)/shard_map/ppermute | solution.py:166
  78.4 5.9 %shard_map.53 = (f32[1,2048]{1,0:T(1,128)}, f32[4096,1]{1,0:T(8,128)S(1)}) custom-call(f32[4096,2048]{1,0:T(8,128)S(1)} %copy-done.1, f32[2,2048]{1,0:T(2,128)} %copy-done.12, f32[2,2048]{1,0:T(2,128)} %copy-done.13, f32[2,2048]{1,0:T(2,128)} %copy-done.14, f32[2,2048]{1,0:T(2,128)} %copy-done.15), custom_call_target="tpu_custom_call" | custom-call | flops 5000000000 | bytes 1048576 | tf_op jit(solution)/shard_map/pallas_call | solution.py:219
  87.3 3.6 %collective-permute-start.17 = (f32[1,2048]{1,0:T(1,128)S(1)}, f32[1,2048]{1,0:T(1,128)S(1)}, u32[]{:S(2)}, u32[]{:S(2)}) collective-permute-start(f32[1,2048]{1,0:T(1,128)S(1)} %add.29.refs_4_), channel_id=1, source_target_pairs={{0,6},{1,7},{2,4},{3,5},{4,2},{5,3},{6,0},{7,1},{8,14},{9,15},{10,... | collective-permute-start | bytes 24584 | tf_op jit(solution)/shard_map/ppermute | solution.py:166
  91.2 1.6 collective-permute-done.17.refs_7_
  93.3 10.5 %copy-done.2 = f32[4096,2048]{1,0:T(8,128)S(1)} copy-done((f32[4096,2048]{1,0:T(8,128)S(1)}, f32[4096,2048]{1,0:T(8,128)}, u32[]{:S(2)}) %copy-start.2) | copy-done | bytes 33554456
  104.9 6.1 %shard_map.54 = (f32[512,128]{1,0:T(8,128)}, bf16[4096,512]{1,0:T(8,128)(2,1)S(1)}, f32[2,2048]{1,0:T(2,128)S(1)}) custom-call(f32[4096,2048]{1,0:T(8,128)S(1)} %copy-done.2, bf16[4096,128]{1,0:T(8,128)(2,1)S(1)} %get-tuple-element.14.refs_0_.refs_1_.centre_ref, bf16[2048,128]{1,0:T(8,128)(2,1)S(1)} %copy-done.7, ...), custom_call_target="tpu_custom_call" | custom-call | flops 4000000000 | bytes 1048576 | tf_op jit(solution)/shard_map/pallas_call | solution.py:219
  111.0 2.1 %copy-done.4 = bf16[4096,512]{1,0:T(8,128)(2,1)} copy-done((bf16[4096,512]{1,0:T(8,128)(2,1)}, bf16[4096,512]{1,0:T(8,128)(2,1)S(1)}, u32[]{:S(2)}) %copy-start.4) | copy-done | bytes 4194328
  116.8 3.8 %collective-permute-start.20 = (f32[256,128]{1,0:T(8,128)S(1)}, f32[256,128]{1,0:T(8,128)S(1)}, u32[]{:S(2)}, u32[]{:S(2)}) collective-permute-start(f32[256,128]{1,0:T(8,128)S(1)} %dynamic-slice_add_fusion), channel_id=1, source_target_pairs={{0,4},{1,5},{2,6},{3,7},{4,0},{5,1},{6,2},{7,3},{8,12},{9,13},{10,... | collective-permute-start | bytes 393224 | tf_op jit(solution)/shard_map/ppermute | solution.py:166
  120.8 3.4 %collective-permute-done.19 = f32[256,128]{1,0:T(8,128)S(1)} collective-permute-done((f32[256,128]{1,0:T(8,128)S(1)}, f32[256,128]{1,0:T(8,128)S(1)}, u32[]{:S(2)}, u32[]{:S(2)}) %collective-permute-start.19) | collective-permute-done | bytes 131104 | tf_op jit(solution)/shard_map/ppermute | solution.py:166
  124.2 6.4 %collective-permute-done.20 = f32[256,128]{1,0:T(8,128)S(1)} collective-permute-done((f32[256,128]{1,0:T(8,128)S(1)}, f32[256,128]{1,0:T(8,128)S(1)}, u32[]{:S(2)}, u32[]{:S(2)}) %collective-permute-start.20) | collective-permute-done | bytes 131104 | tf_op jit(solution)/shard_map/ppermute | solution.py:166
  131.6 10.5 %copy-done.3 = f32[4096,2048]{1,0:T(8,128)S(1)} copy-done((f32[4096,2048]{1,0:T(8,128)S(1)}, f32[4096,2048]{1,0:T(8,128)}, u32[]{:S(2)}) %copy-start.3) | copy-done | bytes 33554456
  142.2 2.2 %copy-done.5 = bf16[4096,512]{1,0:T(8,128)(2,1)S(1)} copy-done((bf16[4096,512]{1,0:T(8,128)(2,1)S(1)}, bf16[4096,512]{1,0:T(8,128)(2,1)}, u32[]{:S(2)}) %copy-start.5) | copy-done | bytes 4194328
  145.4 10.3 %shard_map.55 = f32[4096,128]{1,0:T(8,128)} custom-call(f32[4096,2048]{1,0:T(8,128)S(1)} %copy-done.3, bf16[4096,128]{1,0:T(8,128)(2,1)S(1)} %get-tuple-element.14.refs_0_.refs_1_.centre_ref, bf16[2048,128]{1,0:T(8,128)(2,1)S(1)} %copy-done.8, f32[4096,1]{1,0:T(8,128)S(1)} %get-tuple-element.19.refs_3_.factor_ref, ...), custom_call_target="tpu_custom_call" | custom-call | flops 10000000000 | bytes 1048576 | tf_op jit(solution)/shard_map/pallas_call | solution.py:219
  (83 shorter events, 26.2 us)
Async XLA Ops:
  0.6 8.5 %collective-permute-start = (bf16[512,128]{1,0:T(8,128)(2,1)}, bf16[512,128]{1,0:T(8,128)(2,1)S(1)}, u32[]{:S(2)}, u32[]{:S(2)}) collective-permute-start(bf16[512,128]{1,0:T(8,128)(2,1)} %refs_1_.2), channel_id=1, source_target_pairs={{0,8},{8,16},{16,24},{24,0},{1,9},{9,17},{17,25},{25,1},{2,10},{10... | collective-permute-start | bytes 393224 | tf_op jit(solution)/shard_map/ppermute | solution.py:161
  3.6 8.4 %collective-permute-start.1 = (bf16[512,128]{1,0:T(8,128)(2,1)}, bf16[512,128]{1,0:T(8,128)(2,1)S(1)}, u32[]{:S(2)}, u32[]{:S(2)}) collective-permute-start(bf16[512,128]{1,0:T(8,128)(2,1)} %refs_1_.2), channel_id=1, source_target_pairs={{0,16},{8,24},{16,0},{24,8},{1,17},{9,25},{17,1},{25,9},{2,18},{10... | collective-permute-start | bytes 393224 | tf_op jit(solution)/shard_map/ppermute | solution.py:161
  5.1 7.3 %collective-permute-start.2 = (bf16[512,128]{1,0:T(8,128)(2,1)}, bf16[512,128]{1,0:T(8,128)(2,1)S(1)}, u32[]{:S(2)}, u32[]{:S(2)}) collective-permute-start(bf16[512,128]{1,0:T(8,128)(2,1)} %refs_1_.2), channel_id=1, source_target_pairs={{0,24},{8,0},{16,8},{24,16},{1,25},{9,1},{17,9},{25,17},{2,26},{10... | collective-permute-start | bytes 393224 | tf_op jit(solution)/shard_map/ppermute | solution.py:161
  6.6 33.9 %collective-permute-start.3 = (bf16[512,128]{1,0:T(8,128)(2,1)}, bf16[512,128]{1,0:T(8,128)(2,1)S(1)}, u32[]{:S(2)}, u32[]{:S(2)}) collective-permute-start(bf16[512,128]{1,0:T(8,128)(2,1)} %refs_1_.3), channel_id=1, source_target_pairs={{0,8},{8,16},{16,24},{24,0},{1,9},{9,17},{17,25},{25,1},{2,10},{10... | collective-permute-start | bytes 393224 | tf_op jit(solution)/shard_map/ppermute | solution.py:161
  7.2 33.5 %collective-permute-start.4 = (bf16[512,128]{1,0:T(8,128)(2,1)}, bf16[512,128]{1,0:T(8,128)(2,1)S(1)}, u32[]{:S(2)}, u32[]{:S(2)}) collective-permute-start(bf16[512,128]{1,0:T(8,128)(2,1)} %refs_1_.3), channel_id=1, source_target_pairs={{0,16},{8,24},{16,0},{24,8},{1,17},{9,25},{17,1},{25,9},{2,18},{10... | collective-permute-start | bytes 393224 | tf_op jit(solution)/shard_map/ppermute | solution.py:161
  9.1 31.5 %collective-permute-start.5 = (bf16[512,128]{1,0:T(8,128)(2,1)}, bf16[512,128]{1,0:T(8,128)(2,1)S(1)}, u32[]{:S(2)}, u32[]{:S(2)}) collective-permute-start(bf16[512,128]{1,0:T(8,128)(2,1)} %refs_1_.3), channel_id=1, source_target_pairs={{0,24},{8,0},{16,8},{24,16},{1,25},{9,1},{17,9},{25,17},{2,26},{10... | collective-permute-start | bytes 393224 | tf_op jit(solution)/shard_map/ppermute | solution.py:161
  13.4 27.2 %copy-start.11 = (bf16[512,128]{1,0:T(8,128)(2,1)S(1)}, bf16[512,128]{1,0:T(8,128)(2,1)}, u32[]{:S(2)}) copy-start(bf16[512,128]{1,0:T(8,128)(2,1)} %refs_1_.3) | copy-start | bytes 393220
  35.0 1.2 collective-permute-start.6
  36.2 12.0 %collective-permute-start.7 = (f32[1,2048]{1,0:T(1,128)S(1)}, f32[1,2048]{1,0:T(1,128)S(1)}, u32[]{:S(2)}, u32[]{:S(2)}) collective-permute-start(f32[1,2048]{1,0:T(1,128)S(1)} %add.27.refs_1_), channel_id=1, source_target_pairs={{0,2},{1,3},{2,0},{3,1},{4,6},{5,7},{6,4},{7,5},{8,10},{9,11},{10,... | collective-permute-start | bytes 24584 | tf_op jit(solution)/shard_map/ppermute | solution.py:166
  37.9 10.3 %collective-permute-start.8 = (f32[1,2048]{1,0:T(1,128)S(1)}, f32[1,2048]{1,0:T(1,128)S(1)}, u32[]{:S(2)}, u32[]{:S(2)}) collective-permute-start(f32[1,2048]{1,0:T(1,128)S(1)} %add.27.refs_1_), channel_id=1, source_target_pairs={{0,4},{1,5},{2,6},{3,7},{4,0},{5,1},{6,2},{7,3},{8,12},{9,13},{10,... | collective-permute-start | bytes 24584 | tf_op jit(solution)/shard_map/ppermute | solution.py:166
  40.5 7.7 %collective-permute-start.9 = (f32[1,2048]{1,0:T(1,128)S(1)}, f32[1,2048]{1,0:T(1,128)S(1)}, u32[]{:S(2)}, u32[]{:S(2)}) collective-permute-start(f32[1,2048]{1,0:T(1,128)S(1)} %add.27.refs_1_), channel_id=1, source_target_pairs={{0,6},{1,7},{2,4},{3,5},{4,2},{5,3},{6,0},{7,1},{8,14},{9,15},{10,... | collective-permute-start | bytes 24584 | tf_op jit(solution)/shard_map/ppermute | solution.py:166
  65.9 1.4 collective-permute-start.10
  68.0 4.5 %collective-permute-start.11 = (f32[2,2048]{1,0:T(2,128)S(1)}, f32[2,2048]{1,0:T(2,128)S(1)}, u32[]{:S(2)}, u32[]{:S(2)}) collective-permute-start(f32[2,2048]{1,0:T(2,128)S(1)} %add.28.refs_1_.refs_8_), channel_id=1, source_target_pairs={{0,2},{1,3},{2,0},{3,1},{4,6},{5,7},{6,4},{7,5},{8,10},{9,11},{10,... | collective-permute-start | bytes 49160 | tf_op jit(solution)/shard_map/ppermute | solution.py:166
  68.8 5.2 %collective-permute-start.12 = (f32[2,2048]{1,0:T(2,128)S(1)}, f32[2,2048]{1,0:T(2,128)S(1)}, u32[]{:S(2)}, u32[]{:S(2)}) collective-permute-start(f32[2,2048]{1,0:T(2,128)S(1)} %add.28.refs_1_.refs_8_), channel_id=1, source_target_pairs={{0,4},{1,5},{2,6},{3,7},{4,0},{5,1},{6,2},{7,3},{8,12},{9,13},{10,... | collective-permute-start | bytes 49160 | tf_op jit(solution)/shard_map/ppermute | solution.py:166
  72.3 5.5 %collective-permute-start.13 = (f32[2,2048]{1,0:T(2,128)S(1)}, f32[2,2048]{1,0:T(2,128)S(1)}, u32[]{:S(2)}, u32[]{:S(2)}) collective-permute-start(f32[2,2048]{1,0:T(2,128)S(1)} %add.28.refs_1_.refs_8_), channel_id=1, source_target_pairs={{0,6},{1,7},{2,4},{3,5},{4,2},{5,3},{6,0},{7,1},{8,14},{9,15},{10,... | collective-permute-start | bytes 49160 | tf_op jit(solution)/shard_map/ppermute | solution.py:166
  84.4 1.4 collective-permute-start.14
  86.5 4.5 %collective-permute-start.15 = (f32[1,2048]{1,0:T(1,128)S(1)}, f32[1,2048]{1,0:T(1,128)S(1)}, u32[]{:S(2)}, u32[]{:S(2)}) collective-permute-start(f32[1,2048]{1,0:T(1,128)S(1)} %add.29.refs_4_), channel_id=1, source_target_pairs={{0,2},{1,3},{2,0},{3,1},{4,6},{5,7},{6,4},{7,5},{8,10},{9,11},{10,... | collective-permute-start | bytes 24584 | tf_op jit(solution)/shard_map/ppermute | solution.py:166
  86.5 4.6 %collective-permute-start.16 = (f32[1,2048]{1,0:T(1,128)S(1)}, f32[1,2048]{1,0:T(1,128)S(1)}, u32[]{:S(2)}, u32[]{:S(2)}) collective-permute-start(f32[1,2048]{1,0:T(1,128)S(1)} %add.29.refs_4_), channel_id=1, source_target_pairs={{0,4},{1,5},{2,6},{3,7},{4,0},{5,1},{6,2},{7,3},{8,12},{9,13},{10,... | collective-permute-start | bytes 24584 | tf_op jit(solution)/shard_map/ppermute | solution.py:166
  87.3 5.4 %collective-permute-start.17 = (f32[1,2048]{1,0:T(1,128)S(1)}, f32[1,2048]{1,0:T(1,128)S(1)}, u32[]{:S(2)}, u32[]{:S(2)}) collective-permute-start(f32[1,2048]{1,0:T(1,128)S(1)} %add.29.refs_4_), channel_id=1, source_target_pairs={{0,6},{1,7},{2,4},{3,5},{4,2},{5,3},{6,0},{7,1},{8,14},{9,15},{10,... | collective-permute-start | bytes 24584 | tf_op jit(solution)/shard_map/ppermute | solution.py:166
  114.0 1.4 collective-permute-start.18
  116.3 7.8 %collective-permute-start.19 = (f32[256,128]{1,0:T(8,128)S(1)}, f32[256,128]{1,0:T(8,128)S(1)}, u32[]{:S(2)}, u32[]{:S(2)}) collective-permute-start(f32[256,128]{1,0:T(8,128)S(1)} %dynamic-slice_add_fusion), channel_id=1, source_target_pairs={{0,2},{1,3},{2,0},{3,1},{4,6},{5,7},{6,4},{7,5},{8,10},{9,11},{10,... | collective-permute-start | bytes 393224 | tf_op jit(solution)/shard_map/ppermute | solution.py:166
  116.8 13.8 %collective-permute-start.20 = (f32[256,128]{1,0:T(8,128)S(1)}, f32[256,128]{1,0:T(8,128)S(1)}, u32[]{:S(2)}, u32[]{:S(2)}) collective-permute-start(f32[256,128]{1,0:T(8,128)S(1)} %dynamic-slice_add_fusion), channel_id=1, source_target_pairs={{0,4},{1,5},{2,6},{3,7},{4,0},{5,1},{6,2},{7,3},{8,12},{9,13},{10,... | collective-permute-start | bytes 393224 | tf_op jit(solution)/shard_map/ppermute | solution.py:166
  120.6 10.0 %collective-permute-start.21 = (f32[256,128]{1,0:T(8,128)S(1)}, f32[256,128]{1,0:T(8,128)}, u32[]{:S(2)}, u32[]{:S(2)}) collective-permute-start(f32[256,128]{1,0:T(8,128)S(1)} %dynamic-slice_add_fusion), channel_id=1, source_target_pairs={{0,6},{1,7},{2,4},{3,5},{4,2},{5,3},{6,0},{7,1},{8,14},{9,15},{10,... | collective-permute-start | bytes 393224 | tf_op jit(solution)/shard_map/ppermute | solution.py:166
  131.5 24.2 %collective-permute-start.22 = (f32[256,128]{1,0:T(8,128)S(1)}, f32[256,128]{1,0:T(8,128)S(1)}, u32[]{:S(2)}, u32[]{:S(2)}) collective-permute-start(f32[256,128]{1,0:T(8,128)S(1)} %add_add_fusion), channel_id=1, source_target_pairs={{0,1},{1,0},{2,3},{3,2},{4,5},{5,4},{6,7},{7,6},{8,9},{9,8},{10,11... | collective-permute-start | bytes 393224 | tf_op jit(solution)/shard_map/ppermute | solution.py:166
  (23 other events, 93.6 us)

commit v2 on v1

--- a/solution.py
+++ b/solution.py
@@ -12,7 +12,7 @@
 PRED_TEMP = 0.1
 F32 = jnp.float32
 BF16 = jnp.bfloat16
-VMEM_LIMIT = 20 << 20
+VMEM_LIMIT = 24 << 20
 
 
 def vmem_spec():
@@ -64,8 +64,8 @@
 
 
 def denominators(*refs, parts, block, scale):
-    centre_ref, token_refs = refs[0], refs[1 : 1 + parts]
-    tok, out_ref, acc = refs[1 + parts :]
+    centre_ref, token_refs = refs[1], refs[2 : 2 + parts]
+    _, tok, out_ref, acc = refs[2 + parts :]
     n = token_refs[0].shape[0]
     for i, t in enumerate(token_refs):
         tok[i * n : (i + 1) * n, :] = normalize(t[...])
@@ -83,9 +83,9 @@
 def middle_pass(*refs, parts, block, total, extra):
     code_ref, sum_refs = refs[0], refs[1 : 1 + parts]
     if extra:
-        extra_ref, out_ref, factor_ref, acc = refs[1 + parts :]
+        extra_ref, _, out_ref, factor_ref, acc = refs[1 + parts :]
     else:
-        out_ref, factor_ref, acc = refs[1 + parts :]
+        _, out_ref, factor_ref, acc = refs[1 + parts :]
     sums = sum_refs[0][0:1, :]
     for s in sum_refs[1:]:
         sums = sums + s[0:1, :]
@@ -108,8 +108,9 @@
 
 def token_part(*refs, parts, block, scale, total, own):
     code_ref, centre_ref, tok_ref, factor_ref = refs[:4]
+    core = lax.rem(lax.axis_index("proto"), 2)
     sum_refs, den_refs = refs[4 : 4 + parts], refs[4 + parts : 4 + 2 * parts]
-    grad_ref, logit_ref, scales_ref, acc = refs[4 + 2 * parts :]
+    _, mine_ref, other_ref, scales_ref, acc = refs[4 + 2 * parts :]
     sums, den = sum_refs[0][0:1, :], den_refs[0][1:2, :]
     for s in sum_refs[1:]:
         sums = sums + s[0:1, :]
@@ -126,29 +127,31 @@
         pred = jnp.exp2(similarity(centre, tok_ref[:own, :]) * scale)
         code = code_ref[at, :own]
         logit = (pred * weight - code * factor_ref[at, :] * token_scale).astype(BF16)
-        logit_ref[at, :] = logit
         acc[...] += lax.dot_general(
             centre, logit, (((0,), (0,)), ((), ())), preferred_element_type=F32
         )
         return carry
 
     lax.fori_loop(0, code_ref.shape[0] // block, step, 0)
-    grad_ref[...] = acc[...].T * total ** (-0.5)
-
-
-def proto_part(
-    code_ref, centre_ref, tok_ref, factor_ref, scales_ref, logit_ref, out_ref, *, block, scale, own
-):
+    acc[...] = acc[...] * total ** (-0.5)
+    half = own // 2
+    for c in range(2):
+
+        @pl.when(core == c)
+        def _():
+            mine_ref[...] = acc[:, c * half : (c + 1) * half].T
+            other_ref[...] = acc[:, (1 - c) * half : (2 - c) * half].T
+
+
+def proto_part(code_ref, centre_ref, tok_ref, factor_ref, scales_ref, out_ref, *, block, scale):
     tokens = code_ref.shape[1]
-    token_scale, weight = scales_ref[0:1, own:], scales_ref[1:2, own:]
+    token_scale, weight = scales_ref[0:1, :], scales_ref[1:2, :]
 
     def step(i, carry):
         at = rows(i, block)
-        pred = jnp.exp2(similarity(centre_ref[at, :], tok_ref[own:, :]) * scale)
-        code = code_ref[at, own:]
-        logit = (pred * weight - code * factor_ref[at, :] * token_scale).astype(BF16)
-        grad = jnp.dot(logit, tok_ref[own:, :], preferred_element_type=F32)
-        grad += jnp.dot(logit_ref[at, :], tok_ref[:own, :], preferred_element_type=F32)
+        pred = jnp.exp2(similarity(centre_ref[at, :], tok_ref[...]) * scale)
+        logit = (pred * weight - code_ref[at, :] * factor_ref[at, :] * token_scale).astype(BF16)
+        grad = jnp.dot(logit, tok_ref[...], preferred_element_type=F32)
         out_ref[at, :] = grad * tokens ** (-0.5)
         return carry
 
@@ -179,22 +182,13 @@
     return terms
 
 
-def proto_sum(x):
-    n = lax.axis_size("proto")
-    core = lax.rem(lax.axis_index("proto"), 2)
-    half = x.shape[0] // 2
-    mine = lax.dynamic_slice_in_dim(x, core * half, half)
-    other = lax.dynamic_slice_in_dim(x, (1 - core) * half, half)
-    mine = mine + swapped(other, "proto", 1)
-    unit = 2
+def chip_sum(x):
+    n, unit = lax.axis_size("proto"), 2
     while unit < n:
         group = min(4, n // unit)
-        mine = sum([swapped(mine, "proto", unit * m) for m in range(1, group)], mine)
+        x = sum([swapped(x, "proto", unit * m) for m in range(1, group)], x)
         unit *= group
-    other = swapped(mine, "proto", 1)
-    return jnp.where(
-        core == 0, jnp.concatenate([mine, other]), jnp.concatenate([other, mine])
-    )
+    return x
 
 
 def local(first_view, alternate_augmentation, prototypes):
@@ -210,7 +204,9 @@
     dp = len(views)
     block = min(512, k)
 
-    def run(body, outs, args, scratch, resident=(), keep=(), us=1.0):
+    def run(body, outs, args, scratch, resident=(), keep=(), us=1.0, thread=False):
+        if thread:
+            outs, keep = [shape(*args[0].shape, dtype=args[0].dtype)] + outs, [0] + [i + 1 for i in keep]
         shapes = tuple(pltpu.VMEM(s.shape, s.dtype) if i in keep else s for i, s in enumerate(outs))
         args = [
             pltpu.with_memory_space_constraint(a, pltpu.VMEM) if i in resident else a
@@ -222,6 +218,7 @@
             in_specs=[vmem_spec()] * len(args),
             out_specs=tuple(vmem_spec() for _ in outs),
             scratch_shapes=scratch,
+            input_output_aliases={0: 0} if thread else {},
             compiler_params=pltpu.CompilerParams(vmem_limit_bytes=VMEM_LIMIT),
             cost_estimate=pl.CostEstimate(
                 flops=int(us * 1e9), bytes_accessed=1 << 20, transcendentals=0
@@ -238,26 +235,28 @@
         us=8,
     )
     terms = proto_terms(sums)
-    tok, den = run(
+    code, tok, den = run(
         functools.partial(denominators, parts=dp, block=block, scale=pred_scale),
         [shape(tokens, d, dtype=BF16), shape(1, tokens)],
-        [centres] + others,
+        [code, centres] + others,
         [acc],
-        resident=(0,),
+        resident=(0, 1),
         keep=(0,),
+        thread=True,
         us=6,
     )
-    sums, _ = run(
+    code, sums, _ = run(
         functools.partial(middle_pass, parts=len(terms), block=block, total=total, extra=True),
         [shape(2, tokens), shape(k, 1)],
         [code] + terms + [den],
         [acc],
         resident=(0,),
         keep=(1,),
+        thread=True,
         us=5,
     )
     den_terms = proto_terms(sums)
-    sums, factor = run(
+    code, sums, factor = run(
         functools.partial(
             middle_pass, parts=len(den_terms), block=block, total=total, extra=False
         ),
@@ -266,29 +265,38 @@
         [acc],
         resident=(0,),
         keep=(1,),
+        thread=True,
         us=5,
     )
     terms = proto_terms(sums)
-    token_grad, logit, scales = run(
+    code, mine, other, scales = run(
         functools.partial(
             token_part, parts=len(terms), block=block, scale=pred_scale, total=total, own=own
         ),
-        [shape(own, d), shape(k, own, dtype=BF16), shape(2, tokens)],
+        [shape(own // 2, d), shape(own // 2, d), shape(2, tokens)],
         [code, centres, tok, factor] + terms + den_terms,
         [pltpu.VMEM((d, own), F32)],
         resident=(0, 1, 2, 3),
-        keep=(1, 2),
+        keep=(2,),
+        thread=True,
         us=4,
     )
+    mine = chip_sum(mine + swapped(other, "proto", 1))
     (proto_grad,) = run(
-        functools.partial(proto_part, block=block, scale=pred_scale, own=own),
+        functools.partial(proto_part, block=block, scale=pred_scale),
         [shape(k, d)],
-        [code, centres, tok, factor, scales, logit],
+        [code, centres, tok, factor, scales],
         [],
-        resident=(0, 1, 2, 3, 4, 5),
+        resident=(0, 1, 2, 3, 4),
         us=10,
     )
-    return proto_grad, proto_sum(token_grad)
+    mine, proto_grad = lax.optimization_barrier((mine, proto_grad))
+    other = swapped(mine, "proto", 1)
+    first = lax.rem(lax.axis_index("proto"), 2) == 0
+    token_grad = jnp.where(
+        first, jnp.concatenate([mine, other]), jnp.concatenate([other, mine])
+    )
+    return proto_grad, token_grad
 
 
 def solution(mesh):

time: 157 us -> 103 us (0.66)
  local copies, waits for them, and re-layouts: 54.1 us -> 3.29 us
  waiting for transfers between devices: 25 us -> 17.1 us
  Pallas kernels: 45.5 us -> 49.7 us
    unnamed x48 -> x36, local copies, waits for them, and re-layouts: 53.1 us -> 3.29 us
    ppermute x17, waiting for transfers between devices: 22.2 us -> 14.3 us  [swapped(): lax.ppermute(x, axis, [(i, i ^ mask) for i in range(lax.axis_size(axis))])]
    pallas_call x6, Pallas kernels: 45.5 us -> 49.7 us  [run(): pl.pallas_call(body, out_shape=shapes, in_specs=[vmem_spec()] * len(args)...]
  transfers between devices with their start and end apart: 23 -> 23, of which waited for: 13 -> 12; matrix products, arithmetic and copies ran while one was open for 0% -> 1% of each run, Pallas kernels for 17% -> 31%
where the time goes in v2:
time: 103 us; the launch traced here: 102 us
  Pallas kernels  49.7 us (48%)
  starting transfers between devices  27.3 us (27%)
  waiting for transfers between devices  17.1 us (17%)
  other arithmetic  3.81 us (4%)
  local copies, waits for them, and re-layouts  3.29 us (3%)
    pallas_call x6, Pallas kernels, run(): pl.pallas_call(body, out_shape=shapes, in_specs=[vmem_spec()] * len(args)...  49.7 us
    ppermute x17, starting transfers between devices, swapped(): lax.ppermute(x, axis, [(i, i ^ mask) for i in range(lax.axis_size(axis))])  18.2 us
    ppermute x17, waiting for transfers between devices, swapped(): lax.ppermute(x, axis, [(i, i ^ mask) for i in range(lax.axis_size(axis))])  14.3 us
    ppermute x6, starting transfers between devices, shifted(): lax.ppermute(x, axis, [(i, (i + s) % n) for i in range(n)])  9.1 us
    unnamed x36, local copies, waits for them, and re-layouts  3.29 us
    ppermute x6, waiting for transfers between devices, shifted(): lax.ppermute(x, axis, [(i, (i + s) % n) for i in range(n)])  2.76 us
    add x3, other arithmetic, proto_terms(): x = x + swapped(x, 'proto', 1)  2.14 us
  transfers between devices with their start and end apart: 23, of which 12 were waited for; matrix products, arithmetic and copies ran while one was open for 1% of the time, Pallas kernels for 31%

profile of v2, /device:TPU:0, one launch (start us, length us, event | category | flops | bytes accessed | tf_op | source)
XLA Modules:
  0.0 102.0 jit_solution(17503729506141852355)
XLA Ops:
  0.6 3.0 %collective-permute-start = (bf16[512,128]{1,0:T(8,128)(2,1)}, bf16[512,128]{1,0:T(8,128)(2,1)S(1)}, u32[]{:S(2)}, u32[]{:S(2)}) collective-permute-start(bf16[512,128]{1,0:T(8,128)(2,1)} %refs_1_.1), channel_id=1, source_target_pairs={{0,8},{8,16},{16,24},{24,0},{1,9},{9,17},{17,25},{25,1},{2,10},{10... | collective-permute-start | bytes 393224 | tf_op jit(solution)/shard_map/ppermute | solution.py:164
  3.6 1.5 %collective-permute-start.1 = (bf16[512,128]{1,0:T(8,128)(2,1)}, bf16[512,128]{1,0:T(8,128)(2,1)S(1)}, u32[]{:S(2)}, u32[]{:S(2)}) collective-permute-start(bf16[512,128]{1,0:T(8,128)(2,1)} %refs_1_.1), channel_id=1, source_target_pairs={{0,16},{8,24},{16,0},{24,8},{1,17},{9,25},{17,1},{25,9},{2,18},{10... | collective-permute-start | bytes 393224 | tf_op jit(solution)/shard_map/ppermute | solution.py:164
  5.1 1.4 %collective-permute-start.2 = (bf16[512,128]{1,0:T(8,128)(2,1)}, bf16[512,128]{1,0:T(8,128)(2,1)S(1)}, u32[]{:S(2)}, u32[]{:S(2)}) collective-permute-start(bf16[512,128]{1,0:T(8,128)(2,1)} %refs_1_.1), channel_id=1, source_target_pairs={{0,24},{8,0},{16,8},{24,16},{1,25},{9,1},{17,9},{25,17},{2,26},{10... | collective-permute-start | bytes 393224 | tf_op jit(solution)/shard_map/ppermute | solution.py:164
  7.7 1.4 %collective-permute-done.refs_2_ = bf16[512,128]{1,0:T(8,128)(2,1)S(1)} collective-permute-done((bf16[512,128]{1,0:T(8,128)(2,1)}, bf16[512,128]{1,0:T(8,128)(2,1)S(1)}, u32[]{:S(2)}, u32[]{:S(2)}) %collective-permute-start) | collective-permute-done | bytes 131104 | tf_op jit(solution)/shard_map/ppermute | solution.py:164
  9.1 2.1 %collective-permute-start.5 = (bf16[512,128]{1,0:T(8,128)(2,1)}, bf16[512,128]{1,0:T(8,128)(2,1)S(1)}, u32[]{:S(2)}, u32[]{:S(2)}) collective-permute-start(bf16[512,128]{1,0:T(8,128)(2,1)} %refs_2_.1), channel_id=1, source_target_pairs={{0,24},{8,0},{16,8},{24,16},{1,25},{9,1},{17,9},{25,17},{2,26},{10... | collective-permute-start | bytes 393224 | tf_op jit(solution)/shard_map/ppermute | solution.py:164
  13.3 11.2 %shard_map.50 = (f32[4096,2048]{1,0:T(8,128)S(1)}, bf16[4096,128]{1,0:T(8,128)(2,1)S(1)}, f32[1,2048]{1,0:T(1,128)}) custom-call(bf16[4096,128]{1,0:T(8,128)(2,1)} %refs_0_.1, bf16[512,128]{1,0:T(8,128)(2,1)} %refs_1_.1, bf16[512,128]{1,0:T(8,128)(2,1)} %copy-done.15, bf16[512,128]{1,0:T(8,128)(2,1)} %copy-done.16, bf16[512,128]{1,0:T(8,128)(2,1)} %copy-done.17), custom_call_target="tpu_custom_call" | custom-call | flops 8000000000 | bytes 1048576 | tf_op jit(solution)/shard_map/pallas_call | solution.py:215
  24.6 1.4 %collective-permute-done.6 = f32[1,2048]{1,0:T(1,128)S(1)} collective-permute-done((f32[1,2048]{1,0:T(1,128)}, f32[1,2048]{1,0:T(1,128)S(1)}, u32[]{:S(2)}, u32[]{:S(2)}) %collective-permute-start.6) | collective-permute-done | bytes 8224 | tf_op jit(solution)/shard_map/ppermute | solution.py:169
  26.7 2.2 %collective-permute-start.7 = (f32[1,2048]{1,0:T(1,128)S(1)}, f32[1,2048]{1,0:T(1,128)S(1)}, u32[]{:S(2)}, u32[]{:S(2)}) collective-permute-start(f32[1,2048]{1,0:T(1,128)S(1)} %add.21.refs_1_), channel_id=1, source_target_pairs={{0,2},{1,3},{2,0},{3,1},{4,6},{5,7},{6,4},{7,5},{8,10},{9,11},{10,... | collective-permute-start | bytes 24584 | tf_op jit(solution)/shard_map/ppermute | solution.py:169
  28.8 2.6 %collective-permute-start.8 = (f32[1,2048]{1,0:T(1,128)S(1)}, f32[1,2048]{1,0:T(1,128)S(1)}, u32[]{:S(2)}, u32[]{:S(2)}) collective-permute-start(f32[1,2048]{1,0:T(1,128)S(1)} %add.21.refs_1_), channel_id=1, source_target_pairs={{0,4},{1,5},{2,6},{3,7},{4,0},{5,1},{6,2},{7,3},{8,12},{9,13},{10,... | collective-permute-start | bytes 24584 | tf_op jit(solution)/shard_map/ppermute | solution.py:169
  32.2 7.8 %shard_map.51 = (f32[4096,2048]{1,0:T(8,128)S(1)}, bf16[2048,128]{1,0:T(8,128)(2,1)S(1)}, f32[1,2048]{1,0:T(1,128)}) custom-call(f32[4096,2048]{1,0:T(8,128)S(1)} %get-tuple-element.19.refs_0_, bf16[4096,128]{1,0:T(8,128)(2,1)S(1)} %get-tuple-element.20.refs_1_.centre_ref, bf16[512,128]{1,0:T(8,128)(2,1)} %refs_2_.1, ...), custom_call_target="tpu_custom_call", output_to_operand_aliasing={{0}: (0, {})} | custom-call | flops 6000000000 | bytes 1048576 | tf_op jit(solution)/shard_map/pallas_call | solution.py:215
  40.5 6.6 %shard_map.52 = (f32[4096,2048]{1,0:T(8,128)S(1)}, f32[2,2048]{1,0:T(2,128)}, f32[4096,1]{1,0:T(8,128)}) custom-call(f32[4096,2048]{1,0:T(8,128)S(1)} %get-tuple-element.21.refs_0_, f32[1,2048]{1,0:T(1,128)} %copy-done.7, f32[1,2048]{1,0:T(1,128)} %copy-done.9, f32[1,2048]{1,0:T(1,128)} %copy-done.10, ...), custom_call_target="tpu_custom_call", output_to_operand_aliasing={{0}: (0, {})} | custom-call | flops 5000000000 | bytes 1048576 | tf_op jit(solution)/shard_map/pallas_call | solution.py:215
  47.1 1.4 %collective-permute-done.10 = f32[2,2048]{1,0:T(2,128)S(1)} collective-permute-done((f32[2,2048]{1,0:T(2,128)}, f32[2,2048]{1,0:T(2,128)S(1)}, u32[]{:S(2)}, u32[]{:S(2)}) %collective-permute-start.10) | collective-permute-done | bytes 16416 | tf_op jit(solution)/shard_map/ppermute | solution.py:169
  50.1 3.5 %collective-permute-start.12 = (f32[2,2048]{1,0:T(2,128)S(1)}, f32[2,2048]{1,0:T(2,128)S(1)}, u32[]{:S(2)}, u32[]{:S(2)}) collective-permute-start(f32[2,2048]{1,0:T(2,128)S(1)} %add.22.refs_1_.refs_8_), channel_id=1, source_target_pairs={{0,4},{1,5},{2,6},{3,7},{4,0},{5,1},{6,2},{7,3},{8,12},{9,13},{10,... | collective-permute-start | bytes 49160 | tf_op jit(solution)/shard_map/ppermute | solution.py:169
  53.7 1.8 %collective-permute-done.12.refs_3_.refs_10_ = f32[2,2048]{1,0:T(2,128)S(1)} collective-permute-done((f32[2,2048]{1,0:T(2,128)S(1)}, f32[2,2048]{1,0:T(2,128)S(1)}, u32[]{:S(2)}, u32[]{:S(2)}) %collective-permute-start.12) | collective-permute-done | bytes 16416 | tf_op jit(solution)/shard_map/ppermute | solution.py:169
  55.5 3.6 %collective-permute-done.13.refs_4_.refs_11_ = f32[2,2048]{1,0:T(2,128)S(1)} collective-permute-done((f32[2,2048]{1,0:T(2,128)S(1)}, f32[2,2048]{1,0:T(2,128)S(1)}, u32[]{:S(2)}, u32[]{:S(2)}) %collective-permute-start.13) | collective-permute-done | bytes 16416 | tf_op jit(solution)/shard_map/ppermute | solution.py:169
  59.8 5.9 %shard_map.53 = (f32[4096,2048]{1,0:T(8,128)S(1)}, f32[1,2048]{1,0:T(1,128)}, f32[4096,1]{1,0:T(8,128)S(1)}) custom-call(f32[4096,2048]{1,0:T(8,128)S(1)} %get-tuple-element.24.refs_0_, f32[2,2048]{1,0:T(2,128)} %copy-done, f32[2,2048]{1,0:T(2,128)} %copy-done.4, f32[2,2048]{1,0:T(2,128)} %copy-done.5, ...), custom_call_target="tpu_custom_call", output_to_operand_aliasing={{0}: (0, {})} | custom-call | flops 5000000000 | bytes 1048576 | tf_op jit(solution)/shard_map/pallas_call | solution.py:215
  65.7 1.4 %collective-permute-done.14 = f32[1,2048]{1,0:T(1,128)S(1)} collective-permute-done((f32[1,2048]{1,0:T(1,128)}, f32[1,2048]{1,0:T(1,128)S(1)}, u32[]{:S(2)}, u32[]{:S(2)}) %collective-permute-start.14) | collective-permute-done | bytes 8224 | tf_op jit(solution)/shard_map/ppermute | solution.py:169
  68.6 3.6 %collective-permute-start.17 = (f32[1,2048]{1,0:T(1,128)S(1)}, f32[1,2048]{1,0:T(1,128)S(1)}, u32[]{:S(2)}, u32[]{:S(2)}) collective-permute-start(f32[1,2048]{1,0:T(1,128)S(1)} %add.23.refs_4_), channel_id=1, source_target_pairs={{0,6},{1,7},{2,4},{3,5},{4,2},{5,3},{6,0},{7,1},{8,14},{9,15},{10,... | collective-permute-start | bytes 24584 | tf_op jit(solution)/shard_map/ppermute | solution.py:169
  72.5 1.6 %collective-permute-done.17.refs_7_ = f32[1,2048]{1,0:T(1,128)S(1)} collective-permute-done((f32[1,2048]{1,0:T(1,128)S(1)}, f32[1,2048]{1,0:T(1,128)S(1)}, u32[]{:S(2)}, u32[]{:S(2)}) %collective-permute-start.17) | collective-permute-done | bytes 8224 | tf_op jit(solution)/shard_map/ppermute | solution.py:169
  74.6 5.9 %shard_map.54 = (f32[4096,2048]{1,0:T(8,128)S(1)}, f32[256,128]{1,0:T(8,128)}, f32[256,128]{1,0:T(8,128)}, f32[2,2048]{1,0:T(2,128)S(1)}) custom-call(f32[4096,2048]{1,0:T(8,128)S(1)} %get-tuple-element.26.refs_0_, bf16[4096,128]{1,0:T(8,128)(2,1)S(1)} %get-tuple-element.20.refs_1_.centre_ref, ...), custom_call_target="tpu_custom_call", output_to_operand_aliasing={{0}: (0, {})} | custom-call | flops 4000000000 | bytes 1048576 | tf_op jit(solution)/shard_map/pallas_call | solution.py:215
  80.6 1.6 %collective-permute-done.18 = f32[256,128]{1,0:T(8,128)S(1)} collective-permute-done((f32[256,128]{1,0:T(8,128)}, f32[256,128]{1,0:T(8,128)S(1)}, u32[]{:S(2)}, u32[]{:S(2)}) %collective-permute-start.18) | collective-permute-done | bytes 131104 | tf_op jit(solution)/shard_map/ppermute | solution.py:169
  83.5 3.8 %collective-permute-start.20 = (f32[256,128]{1,0:T(8,128)S(1)}, f32[256,128]{1,0:T(8,128)S(1)}, u32[]{:S(2)}, u32[]{:S(2)}) collective-permute-start(f32[256,128]{1,0:T(8,128)S(1)} %add.24), channel_id=1, source_target_pairs={{0,4},{1,5},{2,6},{3,7},{4,0},{5,1},{6,2},{7,3},{8,12},{9,13},{10,... | collective-permute-start | bytes 393224 | tf_op jit(solution)/shard_map/ppermute | solution.py:169
  87.5 12.3 %shard_map.55 = f32[4096,128]{1,0:T(8,128)} custom-call(f32[4096,2048]{1,0:T(8,128)S(1)} %get-tuple-element.32.code_ref, bf16[4096,128]{1,0:T(8,128)(2,1)S(1)} %get-tuple-element.20.refs_1_.centre_ref, bf16[2048,128]{1,0:T(8,128)(2,1)S(1)} %get-tuple-element.27.refs_2_.tok_ref, f32[4096,1]{1,0:T(8,128)S(1)} %get-tuple-element.28.refs_3_.factor_ref, ...), custom_call_target="tpu_custom_call" | custom-call | flops 10000000000 | bytes 1048576 | tf_op jit(solution)/shard_map/pallas_call | solution.py:215
  99.9 1.3 %collective-permute-done.22 = f32[256,128]{1,0:T(8,128)S(1)} collective-permute-done((f32[256,128]{1,0:T(8,128)S(1)}, f32[256,128]{1,0:T(8,128)S(1)}, u32[]{:S(2)}, u32[]{:S(2)}) %collective-permute-start.22) | collective-permute-done | bytes 131104 | tf_op jit(solution)/shard_map/ppermute | solution.py:169
  (70 shorter events, 12.2 us)
Async XLA Ops:
  0.6 8.5 %collective-permute-start = (bf16[512,128]{1,0:T(8,128)(2,1)}, bf16[512,128]{1,0:T(8,128)(2,1)S(1)}, u32[]{:S(2)}, u32[]{:S(2)}) collective-permute-start(bf16[512,128]{1,0:T(8,128)(2,1)} %refs_1_.1), channel_id=1, source_target_pairs={{0,8},{8,16},{16,24},{24,0},{1,9},{9,17},{17,25},{25,1},{2,10},{10... | collective-permute-start | bytes 393224 | tf_op jit(solution)/shard_map/ppermute | solution.py:164
  3.6 8.4 %collective-permute-start.1 = (bf16[512,128]{1,0:T(8,128)(2,1)}, bf16[512,128]{1,0:T(8,128)(2,1)S(1)}, u32[]{:S(2)}, u32[]{:S(2)}) collective-permute-start(bf16[512,128]{1,0:T(8,128)(2,1)} %refs_1_.1), channel_id=1, source_target_pairs={{0,16},{8,24},{16,0},{24,8},{1,17},{9,25},{17,1},{25,9},{2,18},{10... | collective-permute-start | bytes 393224 | tf_op jit(solution)/shard_map/ppermute | solution.py:164
  5.1 7.3 %collective-permute-start.2 = (bf16[512,128]{1,0:T(8,128)(2,1)}, bf16[512,128]{1,0:T(8,128)(2,1)S(1)}, u32[]{:S(2)}, u32[]{:S(2)}) collective-permute-start(bf16[512,128]{1,0:T(8,128)(2,1)} %refs_1_.1), channel_id=1, source_target_pairs={{0,24},{8,0},{16,8},{24,16},{1,25},{9,1},{17,9},{25,17},{2,26},{10... | collective-permute-start | bytes 393224 | tf_op jit(solution)/shard_map/ppermute | solution.py:164
  6.6 24.8 %collective-permute-start.3 = (bf16[512,128]{1,0:T(8,128)(2,1)}, bf16[512,128]{1,0:T(8,128)(2,1)S(1)}, u32[]{:S(2)}, u32[]{:S(2)}) collective-permute-start(bf16[512,128]{1,0:T(8,128)(2,1)} %refs_2_.1), channel_id=1, source_target_pairs={{0,8},{8,16},{16,24},{24,0},{1,9},{9,17},{17,25},{25,1},{2,10},{10... | collective-permute-start | bytes 393224 | tf_op jit(solution)/shard_map/ppermute | solution.py:164
  7.2 24.3 %collective-permute-start.4 = (bf16[512,128]{1,0:T(8,128)(2,1)}, bf16[512,128]{1,0:T(8,128)(2,1)S(1)}, u32[]{:S(2)}, u32[]{:S(2)}) collective-permute-start(bf16[512,128]{1,0:T(8,128)(2,1)} %refs_2_.1), channel_id=1, source_target_pairs={{0,16},{8,24},{16,0},{24,8},{1,17},{9,25},{17,1},{25,9},{2,18},{10... | collective-permute-start | bytes 393224 | tf_op jit(solution)/shard_map/ppermute | solution.py:164
  9.1 22.3 %collective-permute-start.5 = (bf16[512,128]{1,0:T(8,128)(2,1)}, bf16[512,128]{1,0:T(8,128)(2,1)S(1)}, u32[]{:S(2)}, u32[]{:S(2)}) collective-permute-start(bf16[512,128]{1,0:T(8,128)(2,1)} %refs_2_.1), channel_id=1, source_target_pairs={{0,24},{8,0},{16,8},{24,16},{1,25},{9,1},{17,9},{25,17},{2,26},{10... | collective-permute-start | bytes 393224 | tf_op jit(solution)/shard_map/ppermute | solution.py:164
  24.6 1.4 %collective-permute-start.6 = (f32[1,2048]{1,0:T(1,128)}, f32[1,2048]{1,0:T(1,128)S(1)}, u32[]{:S(2)}, u32[]{:S(2)}) collective-permute-start(f32[1,2048]{1,0:T(1,128)} %get-tuple-element.22), channel_id=1, source_target_pairs={{0,1},{1,0},{2,3},{3,2},{4,5},{5,4},{6,7},{7,6},{8,9},{9,8},{10,11... | collective-permute-start | bytes 24584 | tf_op jit(solution)/shard_map/ppermute | solution.py:169
  26.7 13.3 %copy-start.7 = (f32[1,2048]{1,0:T(1,128)}, f32[1,2048]{1,0:T(1,128)S(1)}, u32[]{:S(2)}) copy-start(f32[1,2048]{1,0:T(1,128)S(1)} %add.21.refs_1_) | copy-start | bytes 24580
  26.7 13.2 %collective-permute-start.7 = (f32[1,2048]{1,0:T(1,128)S(1)}, f32[1,2048]{1,0:T(1,128)S(1)}, u32[]{:S(2)}, u32[]{:S(2)}) collective-permute-start(f32[1,2048]{1,0:T(1,128)S(1)} %add.21.refs_1_), channel_id=1, source_target_pairs={{0,2},{1,3},{2,0},{3,1},{4,6},{5,7},{6,4},{7,5},{8,10},{9,11},{10,... | collective-permute-start | bytes 24584 | tf_op jit(solution)/shard_map/ppermute | solution.py:169
  28.8 11.1 %collective-permute-start.8 = (f32[1,2048]{1,0:T(1,128)S(1)}, f32[1,2048]{1,0:T(1,128)S(1)}, u32[]{:S(2)}, u32[]{:S(2)}) collective-permute-start(f32[1,2048]{1,0:T(1,128)S(1)} %add.21.refs_1_), channel_id=1, source_target_pairs={{0,4},{1,5},{2,6},{3,7},{4,0},{5,1},{6,2},{7,3},{8,12},{9,13},{10,... | collective-permute-start | bytes 24584 | tf_op jit(solution)/shard_map/ppermute | solution.py:169
  31.4 8.5 %collective-permute-start.9 = (f32[1,2048]{1,0:T(1,128)S(1)}, f32[1,2048]{1,0:T(1,128)S(1)}, u32[]{:S(2)}, u32[]{:S(2)}) collective-permute-start(f32[1,2048]{1,0:T(1,128)S(1)} %add.21.refs_1_), channel_id=1, source_target_pairs={{0,6},{1,7},{2,4},{3,5},{4,2},{5,3},{6,0},{7,1},{8,14},{9,15},{10,... | collective-permute-start | bytes 24584 | tf_op jit(solution)/shard_map/ppermute | solution.py:169
  47.1 1.4 %collective-permute-start.10 = (f32[2,2048]{1,0:T(2,128)}, f32[2,2048]{1,0:T(2,128)S(1)}, u32[]{:S(2)}, u32[]{:S(2)}) collective-permute-start(f32[2,2048]{1,0:T(2,128)} %get-tuple-element.25), channel_id=1, source_target_pairs={{0,1},{1,0},{2,3},{3,2},{4,5},{5,4},{6,7},{7,6},{8,9},{9,8},{10,11... | collective-permute-start | bytes 49160 | tf_op jit(solution)/shard_map/ppermute | solution.py:169
  49.2 4.5 %collective-permute-start.11 = (f32[2,2048]{1,0:T(2,128)S(1)}, f32[2,2048]{1,0:T(2,128)S(1)}, u32[]{:S(2)}, u32[]{:S(2)}) collective-permute-start(f32[2,2048]{1,0:T(2,128)S(1)} %add.22.refs_1_.refs_8_), channel_id=1, source_target_pairs={{0,2},{1,3},{2,0},{3,1},{4,6},{5,7},{6,4},{7,5},{8,10},{9,11},{10,... | collective-permute-start | bytes 49160 | tf_op jit(solution)/shard_map/ppermute | solution.py:169
  50.1 5.4 %collective-permute-start.12 = (f32[2,2048]{1,0:T(2,128)S(1)}, f32[2,2048]{1,0:T(2,128)S(1)}, u32[]{:S(2)}, u32[]{:S(2)}) collective-permute-start(f32[2,2048]{1,0:T(2,128)S(1)} %add.22.refs_1_.refs_8_), channel_id=1, source_target_pairs={{0,4},{1,5},{2,6},{3,7},{4,0},{5,1},{6,2},{7,3},{8,12},{9,13},{10,... | collective-permute-start | bytes 49160 | tf_op jit(solution)/shard_map/ppermute | solution.py:169
  53.6 5.5 %collective-permute-start.13 = (f32[2,2048]{1,0:T(2,128)S(1)}, f32[2,2048]{1,0:T(2,128)S(1)}, u32[]{:S(2)}, u32[]{:S(2)}) collective-permute-start(f32[2,2048]{1,0:T(2,128)S(1)} %add.22.refs_1_.refs_8_), channel_id=1, source_target_pairs={{0,6},{1,7},{2,4},{3,5},{4,2},{5,3},{6,0},{7,1},{8,14},{9,15},{10,... | collective-permute-start | bytes 49160 | tf_op jit(solution)/shard_map/ppermute | solution.py:169
  65.7 1.4 %collective-permute-start.14 = (f32[1,2048]{1,0:T(1,128)}, f32[1,2048]{1,0:T(1,128)S(1)}, u32[]{:S(2)}, u32[]{:S(2)}) collective-permute-start(f32[1,2048]{1,0:T(1,128)} %get-tuple-element.29), channel_id=1, source_target_pairs={{0,1},{1,0},{2,3},{3,2},{4,5},{5,4},{6,7},{7,6},{8,9},{9,8},{10,11... | collective-permute-start | bytes 24584 | tf_op jit(solution)/shard_map/ppermute | solution.py:169
  67.8 4.5 %collective-permute-start.15 = (f32[1,2048]{1,0:T(1,128)S(1)}, f32[1,2048]{1,0:T(1,128)S(1)}, u32[]{:S(2)}, u32[]{:S(2)}) collective-permute-start(f32[1,2048]{1,0:T(1,128)S(1)} %add.23.refs_4_), channel_id=1, source_target_pairs={{0,2},{1,3},{2,0},{3,1},{4,6},{5,7},{6,4},{7,5},{8,10},{9,11},{10,... | collective-permute-start | bytes 24584 | tf_op jit(solution)/shard_map/ppermute | solution.py:169
  67.9 4.6 %collective-permute-start.16 = (f32[1,2048]{1,0:T(1,128)S(1)}, f32[1,2048]{1,0:T(1,128)S(1)}, u32[]{:S(2)}, u32[]{:S(2)}) collective-permute-start(f32[1,2048]{1,0:T(1,128)S(1)} %add.23.refs_4_), channel_id=1, source_target_pairs={{0,4},{1,5},{2,6},{3,7},{4,0},{5,1},{6,2},{7,3},{8,12},{9,13},{10,... | collective-permute-start | bytes 24584 | tf_op jit(solution)/shard_map/ppermute | solution.py:169
  68.6 5.4 %collective-permute-start.17 = (f32[1,2048]{1,0:T(1,128)S(1)}, f32[1,2048]{1,0:T(1,128)S(1)}, u32[]{:S(2)}, u32[]{:S(2)}) collective-permute-start(f32[1,2048]{1,0:T(1,128)S(1)} %add.23.refs_4_), channel_id=1, source_target_pairs={{0,6},{1,7},{2,4},{3,5},{4,2},{5,3},{6,0},{7,1},{8,14},{9,15},{10,... | collective-permute-start | bytes 24584 | tf_op jit(solution)/shard_map/ppermute | solution.py:169
  80.6 1.6 %collective-permute-start.18 = (f32[256,128]{1,0:T(8,128)}, f32[256,128]{1,0:T(8,128)S(1)}, u32[]{:S(2)}, u32[]{:S(2)}) collective-permute-start(f32[256,128]{1,0:T(8,128)} %get-tuple-element.31), channel_id=1, source_target_pairs={{0,1},{1,0},{2,3},{3,2},{4,5},{5,4},{6,7},{7,6},{8,9},{9,8},{10,11... | collective-permute-start | bytes 393224 | tf_op jit(solution)/shard_map/ppermute | solution.py:169
  83.1 16.7 %collective-permute-start.19 = (f32[256,128]{1,0:T(8,128)S(1)}, f32[256,128]{1,0:T(8,128)S(1)}, u32[]{:S(2)}, u32[]{:S(2)}) collective-permute-start(f32[256,128]{1,0:T(8,128)S(1)} %add.24), channel_id=1, source_target_pairs={{0,2},{1,3},{2,0},{3,1},{4,6},{5,7},{6,4},{7,5},{8,10},{9,11},{10,... | collective-permute-start | bytes 393224 | tf_op jit(solution)/shard_map/ppermute | solution.py:169
  83.5 16.3 %collective-permute-start.20 = (f32[256,128]{1,0:T(8,128)S(1)}, f32[256,128]{1,0:T(8,128)S(1)}, u32[]{:S(2)}, u32[]{:S(2)}) collective-permute-start(f32[256,128]{1,0:T(8,128)S(1)} %add.24), channel_id=1, source_target_pairs={{0,4},{1,5},{2,6},{3,7},{4,0},{5,1},{6,2},{7,3},{8,12},{9,13},{10,... | collective-permute-start | bytes 393224 | tf_op jit(solution)/shard_map/ppermute | solution.py:169
  87.3 12.4 %collective-permute-start.21 = (f32[256,128]{1,0:T(8,128)S(1)}, f32[256,128]{1,0:T(8,128)S(1)}, u32[]{:S(2)}, u32[]{:S(2)}) collective-permute-start(f32[256,128]{1,0:T(8,128)S(1)} %add.24), channel_id=1, source_target_pairs={{0,6},{1,7},{2,4},{3,5},{4,2},{5,3},{6,0},{7,1},{8,14},{9,15},{10,... | collective-permute-start | bytes 393224 | tf_op jit(solution)/shard_map/ppermute | solution.py:169
  99.8 1.4 %collective-permute-start.22 = (f32[256,128]{1,0:T(8,128)S(1)}, f32[256,128]{1,0:T(8,128)S(1)}, u32[]{:S(2)}, u32[]{:S(2)}) collective-permute-start(f32[256,128]{1,0:T(8,128)S(1)} %add_add_fusion), channel_id=1, source_target_pairs={{0,1},{1,0},{2,3},{3,2},{4,5},{5,4},{6,7},{7,6},{8,9},{9,8},{10,11... | collective-permute-start | bytes 393224 | tf_op jit(solution)/shard_map/ppermute | solution.py:169
  (17 other events, 38.4 us)

commit v3 on v2

v3 whole, which is shorter than its diff:
```python
import functools
import math

import jax
import jax.numpy as jnp
from jax import lax
from jax.experimental import pallas as pl
from jax.experimental.pallas import tpu as pltpu
from jax.sharding import PartitionSpec as P

CODE_TEMP = 0.05
PRED_TEMP = 0.1
F32 = jnp.float32
BF16 = jnp.bfloat16
VMEM_LIMIT = 20 << 20
BLOCKS = {"own": 1024, "first": 512, "den": 512, "middle": 512, "token": 1024, "proto": 512}


def vmem_spec():
    return pl.BlockSpec(memory_space=pltpu.VMEM)


def shape(*dims, dtype=F32):
    return jax.ShapeDtypeStruct(dims, dtype)


def run(body, outs, args, scratch, resident=(), keep=(), us=1.0, thread=False):
    if thread:
        outs = [shape(*args[0].shape, dtype=args[0].dtype)] + outs
        keep = [0] + [i + 1 for i in keep]
        resident = [0] + list(resident)
    return pl.pallas_call(
        body,
        out_shape=tuple(pltpu.VMEM(s.shape, s.dtype) if i in keep else s for i, s in enumerate(outs)),
        in_specs=[vmem_spec()] * len(args),
        out_specs=tuple(vmem_spec() for _ in outs),
        scratch_shapes=scratch,
        input_output_aliases={0: 0} if thread else {},
        compiler_params=pltpu.CompilerParams(vmem_limit_bytes=VMEM_LIMIT),
        cost_estimate=pl.CostEstimate(flops=int(us * 1e9), bytes_accessed=1 << 20, transcendentals=0),
    )(
        *[
            pltpu.with_memory_space_constraint(a, pltpu.VMEM) if i in resident else a
            for i, a in enumerate(args)
        ]
    )


def normalize(values):
    floats = values.astype(F32)
    mean_square = jnp.mean(floats * floats, axis=-1, keepdims=True)
    return (floats * lax.rsqrt(mean_square + 1e-06)).astype(BF16)


def steps(name, size, step):
    block = min(BLOCKS[name], size)

    def body(i, carry):
        step(pl.ds(pl.multiple_of(i * block, block), block))
        return carry

    lax.fori_loop(0, size // block, body, 0)


def similarity(a, b):
    return lax.dot_general(a, b, (((1,), (1,)), ((), ())), preferred_element_type=F32)


def sublane_sums(block):
    return jnp.sum(block.reshape(block.shape[0] // 8, 8, block.shape[1]), axis=0)


def own_codes(proto_ref, token_ref, code_ref, centre_ref, column_ref, *, scale):
    own = token_ref.shape[0]
    tok = normalize(token_ref[...])

    def step(at):
        centre = normalize(proto_ref[at, :])
        centre_ref[at, :] = centre
        code = jnp.exp2(similarity(centre, tok) * scale)
        code_ref[at, :own] = code
        column_ref[at, :] = jnp.sum(code, axis=1, keepdims=True)

    steps("own", proto_ref.shape[0], step)


def first_pass(*refs, parts, scale, total):
    (own_ref, centre_ref, column_ref), token_refs = refs[:3], refs[3 : 3 + parts]
    code_ref, out_ref, tok, acc = refs[3 + parts :]
    n = token_refs[0].shape[0]
    for i, t in enumerate(token_refs):
        tok[i * n : (i + 1) * n, :] = normalize(t[...])
    acc[...] = jnp.zeros_like(acc)

    def step(at):
        code = jnp.exp2(similarity(centre_ref[at, :], tok[...]) * scale)
        code_ref[at, n:] = code
        factor = 1.0 / (total * (column_ref[at, :] + jnp.sum(code, axis=1, keepdims=True)))
        acc[:, n:] += sublane_sums(code * factor)
        acc[:, :n] += sublane_sums(own_ref[at, :n] * factor)

    steps("first", centre_ref.shape[0], step)
    out_ref[...] = jnp.sum(acc[...], axis=0, keepdims=True)


def denominators(code_in, centre_ref, tok_ref, code_ref, out_ref, acc, *, scale, first, last):
    acc[...] = jnp.zeros_like(acc)
    block = min(BLOCKS["den"], centre_ref.shape[0] // 2)
    tok = tok_ref[...]

    def body(i, carry):
        centre = centre_ref[pl.ds(pl.multiple_of(i * block, block), block), :]
        acc[...] += sublane_sums(jnp.exp2(similarity(centre, tok) * scale))
        return carry

    lax.fori_loop(first // block, last // block, body, 0)
    out_ref[...] = jnp.sum(acc[...], axis=0, keepdims=True)


def target_rows(code_in, *refs):
    *token_refs, code_ref, tok = refs
    n = token_refs[0].shape[0]
    for i, t in enumerate(token_refs):
        tok[i * n : (i + 1) * n, :] = normalize(t[...])


def middle_pass(*refs, parts, extras, total):
    code_ref, sum_refs, extra_refs = refs[0], refs[1 : 1 + parts], refs[1 + parts : 1 + parts + extras]
    _, out_ref, factor_ref, acc = refs[1 + parts + extras :]
    sums = sum_refs[0][0:1, :]
    for s in sum_refs[1:]:
        sums = sums + s[0:1, :]
    token_scale = 1.0 / sums
    acc[...] = jnp.zeros_like(acc)

    def step(at):
        code = code_ref[at, :]
        factor = 1.0 / (total * jnp.sum(code * token_scale, axis=1, keepdims=True))
        factor_ref[at, :] = factor
        acc[...] += sublane_sums(code * factor)

    steps("middle", code_ref.shape[0], step)
    out_ref[0:1, :] = jnp.sum(acc[...], axis=0, keepdims=True)
    if extras:
        extra = extra_refs[0][...]
        for e in extra_refs[1:]:
            extra = extra + e[...]
        out_ref[1:2, :] = extra


def token_part(*refs, parts, scale, total, own):
    code_ref, centre_ref, tok_ref, factor_ref = refs[:4]
    sum_refs = refs[4 : 4 + parts]
    _, mine_ref, other_ref, scales_ref, acc = refs[4 + parts :]
    core = lax.rem(lax.axis_index("proto"), 2)
    sums = sum_refs[0][...]
    for s in sum_refs[1:]:
        sums = sums + s[...]
    scales_ref[...] = total / sums
    acc[...] = jnp.zeros_like(acc)
    token_scale, weight = scales_ref[0:1, :own], scales_ref[1:2, :own]

    def step(at):
        centre = centre_ref[at, :]
        pred = jnp.exp2(similarity(centre, tok_ref[:own, :]) * scale)
        logit = (pred * weight - code_ref[at, :own] * factor_ref[at, :] * token_scale).astype(BF16)
        acc[...] += lax.dot_general(
            centre, logit, (((0,), (0,)), ((), ())), preferred_element_type=F32
        )

    steps("token", code_ref.shape[0], step)
    acc[...] = acc[...] * total ** (-0.5)
    half = own // 2
    for c in range(2):

        @pl.when(core == c)
        def _():
            mine_ref[...] = acc[:, c * half : (c + 1) * half].T
            other_ref[...] = acc[:, (1 - c) * half : (2 - c) * half].T


def proto_part(code_ref, centre_ref, tok_ref, factor_ref, scales_ref, out_ref, *, scale):
    tokens = code_ref.shape[1]
    token_scale, weight = scales_ref[0:1, :], scales_ref[1:2, :]

    def step(at):
        pred = jnp.exp2(similarity(centre_ref[at, :], tok_ref[...]) * scale)
        logit = (pred * weight - code_ref[at, :] * factor_ref[at, :] * token_scale).astype(BF16)
        grad = jnp.dot(logit, tok_ref[...], preferred_element_type=F32)
        out_ref[at, :] = grad * tokens ** (-0.5)

    steps("proto", code_ref.shape[0], step)


def shifted(x, axis):
    n = lax.axis_size(axis)
    return [lax.ppermute(x, axis, [(i, (i + s) % n) for i in range(n)]) for s in range(1, n)]


def swapped(x, axis, mask):
    return lax.ppermute(x, axis, [(i, i ^ mask) for i in range(lax.axis_size(axis))])


def proto_terms(x):
    n = lax.axis_size("proto")
    x = x + swapped(x, "proto", 1)
    terms, unit = [x], 2
    while unit < n:
        group = min(4, n // unit)
        if unit > 2:
            terms = [sum(terms)]
        terms = [terms[0]] + [swapped(terms[0], "proto", unit * m) for m in range(1, group)]
        unit *= group
    return terms


def chip_sum(x):
    n, unit = lax.axis_size("proto"), 2
    while unit < n:
        group = min(4, n // unit)
        x = sum([swapped(x, "proto", unit * m) for m in range(1, group)], x)
        unit *= group
    return x


def local(first_view, alternate_augmentation, prototypes):
    own, d = first_view.shape
    k = prototypes.shape[0]
    tokens = own * lax.axis_size("dp")
    total = float(k * lax.axis_size("proto"))
    log2e = math.log2(math.e)
    code_scale = log2e / d / CODE_TEMP
    pred_scale = log2e / d / PRED_TEMP
    acc = pltpu.VMEM((8, tokens), F32)

    views = shifted(first_view, "dp")
    code, centres, columns = run(
        functools.partial(own_codes, scale=code_scale),
        [shape(k, tokens), shape(k, d, dtype=BF16), shape(k, 1)],
        [prototypes, first_view],
        [],
        keep=(0, 1, 2),
        us=3,
    )
    alternate_augmentation, columns = lax.optimization_barrier((alternate_augmentation, columns))
    others = shifted(alternate_augmentation, "dp")
    code, sums = run(
        functools.partial(first_pass, parts=len(views), scale=code_scale, total=total),
        [shape(1, tokens)],
        [code, centres, columns] + views,
        [pltpu.VMEM((tokens - own, d), BF16), acc],
        resident=list(range(1, 3 + len(views))),
        keep=[0],
        thread=True,
        us=7,
    )
    terms = proto_terms(sums)
    code, tok = run(
        target_rows,
        [shape(tokens, d, dtype=BF16)],
        [code, alternate_augmentation] + others,
        [],
        keep=[0],
        thread=True,
        us=1,
    )
    dens = []
    for i in range(2):
        code, den = run(
            functools.partial(
                denominators, scale=pred_scale, first=i * k // 2, last=(i + 1) * k // 2
            ),
            [shape(1, tokens)],
            [code, centres, tok],
            [acc],
            resident=[1, 2],
            keep=[0],
            thread=True,
            us=3,
        )
        dens.append(den)
        code, sums, factor = run(
            functools.partial(
                middle_pass, parts=len(terms), extras=2 * i, total=total
            ),
            [shape(1 + i, tokens), shape(k, 1)],
            [code] + terms + (dens if i else []),
            [acc],
            resident=list(range(1, 1 + len(terms) + 2 * i)),
            keep=[0, 1],
            thread=True,
            us=5,
        )
        terms = proto_terms(sums)
    code, mine, other, scales = run(
        functools.partial(token_part, parts=len(terms), scale=pred_scale, total=total, own=own),
        [shape(own // 2, d), shape(own // 2, d), shape(2, tokens)],
        [code, centres, tok, factor] + terms,
        [pltpu.VMEM((d, own), F32)],
        resident=list(range(1, 4 + len(terms))),
        keep=[0, 1, 2],
        thread=True,
        us=4,
    )
    mine = chip_sum(mine + swapped(other, "proto", 1))
    (proto_grad,) = run(
        functools.partial(proto_part, scale=pred_scale),
        [shape(k, d)],
        [code, centres, tok, factor, scales],
        [],
        resident=range(5),
        us=10,
    )
    mine, proto_grad = lax.optimization_barrier((mine, proto_grad))
    other = swapped(mine, "proto", 1)
    first = lax.rem(lax.axis_index("proto"), 2) == 0
    token_grad = jnp.where(
        first, jnp.concatenate([mine, other]), jnp.concatenate([other, mine])
    )
    return proto_grad, token_grad


def solution(mesh):
    return jax.shard_map(
        local,
        mesh=mesh,
        in_specs=(P("dp", None), P("dp", None), P("proto", None)),
        out_specs=(P("proto", None), P("dp", None)),
        check_vma=False,
    )
```

time: 103 us -> 87.5 us (0.85)
  waiting for transfers between devices: 17.1 us -> 12.5 us
  Pallas kernels: 49.7 us -> 45.9 us
  local copies, waits for them, and re-layouts: 3.29 us -> 0.01 us
  other arithmetic: 3.81 us -> 0.8 us
    pallas_call x6 -> x9, Pallas kernels: 49.7 us -> 45.9 us  [run(): pl.pallas_call(body, out_shape=tuple((pltpu.VMEM(s.shape, s.dtype) if i i...]
    unnamed x36 -> x2, local copies, waits for them, and re-layouts: 3.29 us -> 0.01 us
    ppermute x6, waiting for transfers between devices: 2.76 us -> 0.02 us  [shifted(): lax.ppermute(x, axis, [(i, (i + s) % n) for i in range(n)])]
    add x3, other arithmetic: 2.14 us -> 0.03 us  [proto_terms(): x = x + swapped(x, 'proto', 1)]
    ppermute x17, waiting for transfers between devices: 14.3 us -> 12.4 us  [swapped(): lax.ppermute(x, axis, [(i, i ^ mask) for i in range(lax.axis_size(axis))])]
  transfers between devices with their start and end apart: 23 -> 23, of which waited for: 12 -> 8; matrix products, arithmetic and copies ran while one was open for 1% -> 0% of each run, Pallas kernels for 31% -> 37%
where the time goes in v3:
time: 87.5 us; the launch traced here: 87.3 us
  Pallas kernels  45.9 us (52%)
  starting transfers between devices  27.3 us (31%)
  waiting for transfers between devices  12.5 us (14%)
    pallas_call x9, Pallas kernels, run(): pl.pallas_call(body, out_shape=tuple((pltpu.VMEM(s.shape, s.dtype) if i i...  45.9 us
    ppermute x17, starting transfers between devices, swapped(): lax.ppermute(x, axis, [(i, i ^ mask) for i in range(lax.axis_size(axis))])  18.3 us
    ppermute x17, waiting for transfers between devices, swapped(): lax.ppermute(x, axis, [(i, i ^ mask) for i in range(lax.axis_size(axis))])  12.4 us
    ppermute x6, starting transfers between devices, shifted(): lax.ppermute(x, axis, [(i, (i + s) % n) for i in range(n)])  9.03 us
  transfers between devices with their start and end apart: 23, of which 8 were waited for; matrix products, arithmetic and copies ran while one was open for 0% of the time, Pallas kernels for 37%

profile of v3, /device:TPU:0, one launch (start us, length us, event | category | flops | bytes accessed | tf_op | source)
XLA Modules:
  0.0 87.3 jit_solution(7880340505385045911)
XLA Ops:
  0.6 3.0 %collective-permute-start = (bf16[512,128]{1,0:T(8,128)(2,1)}, bf16[512,128]{1,0:T(8,128)(2,1)S(1)}, u32[]{:S(2)}, u32[]{:S(2)}) collective-permute-start(bf16[512,128]{1,0:T(8,128)(2,1)} %token_ref.1), channel_id=1, source_target_pairs={{0,8},{8,16},{16,24},{24,0},{1,9},{9,17},{17,25},{25,1},{2,10},{10... | collective-permute-start | bytes 393224 | tf_op jit(solution)/shard_map/ppermute | solution.py:197
  3.6 1.5 %collective-permute-start.1 = (bf16[512,128]{1,0:T(8,128)(2,1)}, bf16[512,128]{1,0:T(8,128)(2,1)S(1)}, u32[]{:S(2)}, u32[]{:S(2)}) collective-permute-start(bf16[512,128]{1,0:T(8,128)(2,1)} %token_ref.1), channel_id=1, source_target_pairs={{0,16},{8,24},{16,0},{24,8},{1,17},{9,25},{17,1},{25,9},{2,18},{10... | collective-permute-start | bytes 393224 | tf_op jit(solution)/shard_map/ppermute | solution.py:197
  5.2 1.4 %collective-permute-start.2 = (bf16[512,128]{1,0:T(8,128)(2,1)}, bf16[512,128]{1,0:T(8,128)(2,1)S(1)}, u32[]{:S(2)}, u32[]{:S(2)}) collective-permute-start(bf16[512,128]{1,0:T(8,128)(2,1)} %token_ref.1), channel_id=1, source_target_pairs={{0,24},{8,0},{16,8},{24,16},{1,25},{9,1},{17,9},{25,17},{2,26},{10... | collective-permute-start | bytes 393224 | tf_op jit(solution)/shard_map/ppermute | solution.py:197
  6.6 3.9 %shard_map.50 = (f32[4096,2048]{1,0:T(8,128)S(1)}, bf16[4096,128]{1,0:T(8,128)(2,1)S(1)}, f32[4096,1]{1,0:T(8,128)S(1)}) custom-call(bf16[4096,128]{1,0:T(8,128)(2,1)} %proto_ref.1, bf16[512,128]{1,0:T(8,128)(2,1)} %token_ref.1), custom_call_target="tpu_custom_call" | custom-call | flops 3000000000 | bytes 1048576 | tf_op jit(solution)/shard_map/pallas_call | solution.py:32
  11.7 1.9 %collective-permute-start.5 = (bf16[512,128]{1,0:T(8,128)(2,1)}, bf16[512,128]{1,0:T(8,128)(2,1)S(1)}, u32[]{:S(2)}, u32[]{:S(2)}) collective-permute-start(bf16[512,128]{1,0:T(8,128)(2,1)} %refs_0_), channel_id=1, source_target_pairs={{0,24},{8,0},{16,8},{24,16},{1,25},{9,1},{17,9},{25,17},{2,26},{10... | collective-permute-start | bytes 393224 | tf_op jit(solution)/shard_map/ppermute | solution.py:197
  13.6 9.5 %shard_map.51 = (f32[4096,2048]{1,0:T(8,128)S(1)}, f32[1,2048]{1,0:T(1,128)S(1)}) custom-call(f32[4096,2048]{1,0:T(8,128)S(1)} %get-tuple-element.26.refs_0_, bf16[4096,128]{1,0:T(8,128)(2,1)S(1)} %get-tuple-element.27.refs_1_.centre_ref, f32[4096,1]{1,0:T(8,128)S(1)} %get-tuple-element.29.refs_2_, ...), custom_call_target="tpu_custom_call", output_to_operand_aliasing={{0}: (0, {})} | custom-call | flops 7000000000 | bytes 1048576 | tf_op jit(solution)/shard_map/pallas_call | solution.py:32
  24.4 2.0 %collective-permute-start.7 = (f32[1,2048]{1,0:T(1,128)S(1)}, f32[1,2048]{1,0:T(1,128)S(1)}, u32[]{:S(2)}, u32[]{:S(2)}) collective-permute-start(f32[1,2048]{1,0:T(1,128)S(1)} %add.21.refs_1_), channel_id=1, source_target_pairs={{0,2},{1,3},{2,0},{3,1},{4,6},{5,7},{6,4},{7,5},{8,10},{9,11},{10,... | collective-permute-start | bytes 24584 | tf_op jit(solution)/shard_map/ppermute | solution.py:201
  26.4 2.6 %collective-permute-start.8 = (f32[1,2048]{1,0:T(1,128)S(1)}, f32[1,2048]{1,0:T(1,128)S(1)}, u32[]{:S(2)}, u32[]{:S(2)}) collective-permute-start(f32[1,2048]{1,0:T(1,128)S(1)} %add.21.refs_1_), channel_id=1, source_target_pairs={{0,4},{1,5},{2,6},{3,7},{4,0},{5,1},{6,2},{7,3},{8,12},{9,13},{10,... | collective-permute-start | bytes 24584 | tf_op jit(solution)/shard_map/ppermute | solution.py:201
  29.0 2.9 %shard_map.53 = (f32[4096,2048]{1,0:T(8,128)S(1)}, f32[1,2048]{1,0:T(1,128)S(1)}) custom-call(f32[4096,2048]{1,0:T(8,128)S(1)} %get-tuple-element.32.code_in, bf16[4096,128]{1,0:T(8,128)(2,1)S(1)} %get-tuple-element.27.refs_1_.centre_ref, bf16[2048,128]{1,0:T(8,128)(2,1)S(1)} %get-tuple-element.33.tok_ref.refs_2_), custom_call_target="tpu_custom_call", output_to_operand_aliasing={{0}: (0, {})} | custom-call | flops 3000000000 | bytes 1048576 | tf_op jit(solution)/shard_map/pallas_call | solution.py:32
  32.0 2.5 %collective-permute-done.9.refs_4_ = f32[1,2048]{1,0:T(1,128)S(1)} collective-permute-done((f32[1,2048]{1,0:T(1,128)S(1)}, f32[1,2048]{1,0:T(1,128)S(1)}, u32[]{:S(2)}, u32[]{:S(2)}) %collective-permute-start.9) | collective-permute-done | bytes 8224 | tf_op jit(solution)/shard_map/ppermute | solution.py:201
  34.5 5.8 %shard_map.54 = (f32[4096,2048]{1,0:T(8,128)S(1)}, f32[1,2048]{1,0:T(1,128)S(1)}, f32[4096,1]{1,0:T(8,128)}) custom-call(f32[4096,2048]{1,0:T(8,128)S(1)} %get-tuple-element.34.refs_0_, f32[1,2048]{1,0:T(1,128)S(1)} %add.21.refs_1_, f32[1,2048]{1,0:T(1,128)S(1)} %collective-permute-done.7.refs_2_, ...), custom_call_target="tpu_custom_call", output_to_operand_aliasing={{0}: (0, {})} | custom-call | flops 5000000000 | bytes 1048576 | tf_op jit(solution)/shard_map/pallas_call | solution.py:32
  41.5 1.9 %collective-permute-start.12 = (f32[1,2048]{1,0:T(1,128)S(1)}, f32[1,2048]{1,0:T(1,128)S(1)}, u32[]{:S(2)}, u32[]{:S(2)}) collective-permute-start(f32[1,2048]{1,0:T(1,128)S(1)} %add.22.refs_1_), channel_id=1, source_target_pairs={{0,4},{1,5},{2,6},{3,7},{4,0},{5,1},{6,2},{7,3},{8,12},{9,13},{10,... | collective-permute-start | bytes 24584 | tf_op jit(solution)/shard_map/ppermute | solution.py:201
  43.4 2.5 %collective-permute-start.13 = (f32[1,2048]{1,0:T(1,128)S(1)}, f32[1,2048]{1,0:T(1,128)S(1)}, u32[]{:S(2)}, u32[]{:S(2)}) collective-permute-start(f32[1,2048]{1,0:T(1,128)S(1)} %add.22.refs_1_), channel_id=1, source_target_pairs={{0,6},{1,7},{2,4},{3,5},{4,2},{5,3},{6,0},{7,1},{8,14},{9,15},{10,... | collective-permute-start | bytes 24584 | tf_op jit(solution)/shard_map/ppermute | solution.py:201
  45.9 2.9 %shard_map.55 = (f32[4096,2048]{1,0:T(8,128)S(1)}, f32[1,2048]{1,0:T(1,128)S(1)}) custom-call(f32[4096,2048]{1,0:T(8,128)S(1)} %get-tuple-element.36.code_in, bf16[4096,128]{1,0:T(8,128)(2,1)S(1)} %get-tuple-element.27.refs_1_.centre_ref, bf16[2048,128]{1,0:T(8,128)(2,1)S(1)} %get-tuple-element.33.tok_ref.refs_2_), custom_call_target="tpu_custom_call", output_to_operand_aliasing={{0}: (0, {})} | custom-call | flops 3000000000 | bytes 1048576 | tf_op jit(solution)/shard_map/pallas_call | solution.py:32
  48.9 4.5 %shard_map.56 = (f32[4096,2048]{1,0:T(8,128)S(1)}, f32[2,2048]{1,0:T(2,128)S(1)}, f32[4096,1]{1,0:T(8,128)S(1)}) custom-call(f32[4096,2048]{1,0:T(8,128)S(1)} %get-tuple-element.37.refs_0_, f32[1,2048]{1,0:T(1,128)S(1)} %add.22.refs_1_, f32[1,2048]{1,0:T(1,128)S(1)} %collective-permute-done.11.refs_2_, ...), custom_call_target="tpu_custom_call", output_to_operand_aliasing={{0}: (0, {})} | custom-call | flops 5000000000 | bytes 1048576 | tf_op jit(solution)/shard_map/pallas_call | solution.py:32
  54.8 3.0 %collective-permute-start.16 = (f32[2,2048]{1,0:T(2,128)S(1)}, f32[2,2048]{1,0:T(2,128)S(1)}, u32[]{:S(2)}, u32[]{:S(2)}) collective-permute-start(f32[2,2048]{1,0:T(2,128)S(1)} %add.23.refs_4_), channel_id=1, source_target_pairs={{0,4},{1,5},{2,6},{3,7},{4,0},{5,1},{6,2},{7,3},{8,12},{9,13},{10,... | collective-permute-start | bytes 49160 | tf_op jit(solution)/shard_map/ppermute | solution.py:201
  57.8 1.4 %collective-permute-start.17 = (f32[2,2048]{1,0:T(2,128)S(1)}, f32[2,2048]{1,0:T(2,128)S(1)}, u32[]{:S(2)}, u32[]{:S(2)}) collective-permute-start(f32[2,2048]{1,0:T(2,128)S(1)} %add.23.refs_4_), channel_id=1, source_target_pairs={{0,6},{1,7},{2,4},{3,5},{4,2},{5,3},{6,0},{7,1},{8,14},{9,15},{10,... | collective-permute-start | bytes 49160 | tf_op jit(solution)/shard_map/ppermute | solution.py:201
  59.5 3.8 %collective-permute-done.17.refs_7_ = f32[2,2048]{1,0:T(2,128)S(1)} collective-permute-done((f32[2,2048]{1,0:T(2,128)S(1)}, f32[2,2048]{1,0:T(2,128)S(1)}, u32[]{:S(2)}, u32[]{:S(2)}) %collective-permute-start.17) | collective-permute-done | bytes 16416 | tf_op jit(solution)/shard_map/ppermute | solution.py:201
  63.3 3.7 %shard_map.57 = (f32[4096,2048]{1,0:T(8,128)S(1)}, f32[256,128]{1,0:T(8,128)S(1)}, f32[256,128]{1,0:T(8,128)S(1)}, f32[2,2048]{1,0:T(2,128)S(1)}) custom-call(f32[4096,2048]{1,0:T(8,128)S(1)} %get-tuple-element.41.refs_0_, bf16[4096,128]{1,0:T(8,128)(2,1)S(1)} %get-tuple-element.27.refs_1_.centre_ref, ...), custom_call_target="tpu_custom_call", output_to_operand_aliasing={{0}: (0, {})} | custom-call | flops 4000000000 | bytes 1048576 | tf_op jit(solution)/shard_map/pallas_call | solution.py:32
  67.1 1.3 %collective-permute-done.18 = f32[256,128]{1,0:T(8,128)S(1)} collective-permute-done((f32[256,128]{1,0:T(8,128)S(1)}, f32[256,128]{1,0:T(8,128)S(1)}, u32[]{:S(2)}, u32[]{:S(2)}) %collective-permute-start.18) | collective-permute-done | bytes 131104 | tf_op jit(solution)/shard_map/ppermute | solution.py:201
  68.5 1.9 %collective-permute-start.20 = (f32[256,128]{1,0:T(8,128)S(1)}, f32[256,128]{1,0:T(8,128)S(1)}, u32[]{:S(2)}, u32[]{:S(2)}) collective-permute-start(f32[256,128]{1,0:T(8,128)S(1)} %add.24), channel_id=1, source_target_pairs={{0,4},{1,5},{2,6},{3,7},{4,0},{5,1},{6,2},{7,3},{8,12},{9,13},{10,... | collective-permute-start | bytes 393224 | tf_op jit(solution)/shard_map/ppermute | solution.py:201
  70.4 2.5 %collective-permute-start.21 = (f32[256,128]{1,0:T(8,128)S(1)}, f32[256,128]{1,0:T(8,128)S(1)}, u32[]{:S(2)}, u32[]{:S(2)}) collective-permute-start(f32[256,128]{1,0:T(8,128)S(1)} %add.24), channel_id=1, source_target_pairs={{0,6},{1,7},{2,4},{3,5},{4,2},{5,3},{6,0},{7,1},{8,14},{9,15},{10,... | collective-permute-start | bytes 393224 | tf_op jit(solution)/shard_map/ppermute | solution.py:201
  72.9 12.3 %shard_map.58 = f32[4096,128]{1,0:T(8,128)} custom-call(f32[4096,2048]{1,0:T(8,128)S(1)} %get-tuple-element.46.code_ref, bf16[4096,128]{1,0:T(8,128)(2,1)S(1)} %get-tuple-element.27.refs_1_.centre_ref, bf16[2048,128]{1,0:T(8,128)(2,1)S(1)} %get-tuple-element.33.tok_ref.refs_2_, f32[4096,1]{1,0:T(8,128)S(1)} %get-tuple-element.42.refs_3_.factor_ref, ...), custom_call_target="tpu_custom_call" | custom-call | flops 10000000000 | bytes 1048576 | tf_op jit(solution)/shard_map/pallas_call | solution.py:32
  85.3 1.3 %collective-permute-done.22 = f32[256,128]{1,0:T(8,128)S(1)} collective-permute-done((f32[256,128]{1,0:T(8,128)S(1)}, f32[256,128]{1,0:T(8,128)S(1)}, u32[]{:S(2)}, u32[]{:S(2)}) %collective-permute-start.22) | collective-permute-done | bytes 131104 | tf_op jit(solution)/shard_map/ppermute | solution.py:201
  (39 shorter events, 6.3 us)
Async XLA Ops:
  0.6 22.6 %copy-start = (bf16[512,128]{1,0:T(8,128)(2,1)S(1)}, bf16[512,128]{1,0:T(8,128)(2,1)}, u32[]{:S(2)}) copy-start(bf16[512,128]{1,0:T(8,128)(2,1)} %refs_0_) | copy-start | bytes 393220
  0.6 11.0 %collective-permute-start = (bf16[512,128]{1,0:T(8,128)(2,1)}, bf16[512,128]{1,0:T(8,128)(2,1)S(1)}, u32[]{:S(2)}, u32[]{:S(2)}) collective-permute-start(bf16[512,128]{1,0:T(8,128)(2,1)} %token_ref.1), channel_id=1, source_target_pairs={{0,8},{8,16},{16,24},{24,0},{1,9},{9,17},{17,25},{25,1},{2,10},{10... | collective-permute-start | bytes 393224 | tf_op jit(solution)/shard_map/ppermute | solution.py:197
  3.6 10.0 %collective-permute-start.1 = (bf16[512,128]{1,0:T(8,128)(2,1)}, bf16[512,128]{1,0:T(8,128)(2,1)S(1)}, u32[]{:S(2)}, u32[]{:S(2)}) collective-permute-start(bf16[512,128]{1,0:T(8,128)(2,1)} %token_ref.1), channel_id=1, source_target_pairs={{0,16},{8,24},{16,0},{24,8},{1,17},{9,25},{17,1},{25,9},{2,18},{10... | collective-permute-start | bytes 393224 | tf_op jit(solution)/shard_map/ppermute | solution.py:197
  5.2 8.5 %collective-permute-start.2 = (bf16[512,128]{1,0:T(8,128)(2,1)}, bf16[512,128]{1,0:T(8,128)(2,1)S(1)}, u32[]{:S(2)}, u32[]{:S(2)}) collective-permute-start(bf16[512,128]{1,0:T(8,128)(2,1)} %token_ref.1), channel_id=1, source_target_pairs={{0,24},{8,0},{16,8},{24,16},{1,25},{9,1},{17,9},{25,17},{2,26},{10... | collective-permute-start | bytes 393224 | tf_op jit(solution)/shard_map/ppermute | solution.py:197
  10.5 12.7 %collective-permute-start.3 = (bf16[512,128]{1,0:T(8,128)(2,1)}, bf16[512,128]{1,0:T(8,128)(2,1)S(1)}, u32[]{:S(2)}, u32[]{:S(2)}) collective-permute-start(bf16[512,128]{1,0:T(8,128)(2,1)} %refs_0_), channel_id=1, source_target_pairs={{0,8},{8,16},{16,24},{24,0},{1,9},{9,17},{17,25},{25,1},{2,10},{10... | collective-permute-start | bytes 393224 | tf_op jit(solution)/shard_map/ppermute | solution.py:197
  11.2 12.1 %collective-permute-start.4 = (bf16[512,128]{1,0:T(8,128)(2,1)}, bf16[512,128]{1,0:T(8,128)(2,1)S(1)}, u32[]{:S(2)}, u32[]{:S(2)}) collective-permute-start(bf16[512,128]{1,0:T(8,128)(2,1)} %refs_0_), channel_id=1, source_target_pairs={{0,16},{8,24},{16,0},{24,8},{1,17},{9,25},{17,1},{25,9},{2,18},{10... | collective-permute-start | bytes 393224 | tf_op jit(solution)/shard_map/ppermute | solution.py:197
  11.7 11.6 %collective-permute-start.5 = (bf16[512,128]{1,0:T(8,128)(2,1)}, bf16[512,128]{1,0:T(8,128)(2,1)S(1)}, u32[]{:S(2)}, u32[]{:S(2)}) collective-permute-start(bf16[512,128]{1,0:T(8,128)(2,1)} %refs_0_), channel_id=1, source_target_pairs={{0,24},{8,0},{16,8},{24,16},{1,25},{9,1},{17,9},{25,17},{2,26},{10... | collective-permute-start | bytes 393224 | tf_op jit(solution)/shard_map/ppermute | solution.py:197
  23.1 1.2 %collective-permute-start.6 = (f32[1,2048]{1,0:T(1,128)S(1)}, f32[1,2048]{1,0:T(1,128)S(1)}, u32[]{:S(2)}, u32[]{:S(2)}) collective-permute-start(f32[1,2048]{1,0:T(1,128)S(1)} %get-tuple-element.35), channel_id=1, source_target_pairs={{0,1},{1,0},{2,3},{3,2},{4,5},{5,4},{6,7},{7,6},{8,9},{9,8},{10,11... | collective-permute-start | bytes 24584 | tf_op jit(solution)/shard_map/ppermute | solution.py:201
  24.4 7.6 %collective-permute-start.7 = (f32[1,2048]{1,0:T(1,128)S(1)}, f32[1,2048]{1,0:T(1,128)S(1)}, u32[]{:S(2)}, u32[]{:S(2)}) collective-permute-start(f32[1,2048]{1,0:T(1,128)S(1)} %add.21.refs_1_), channel_id=1, source_target_pairs={{0,2},{1,3},{2,0},{3,1},{4,6},{5,7},{6,4},{7,5},{8,10},{9,11},{10,... | collective-permute-start | bytes 24584 | tf_op jit(solution)/shard_map/ppermute | solution.py:201
  26.4 5.6 %collective-permute-start.8 = (f32[1,2048]{1,0:T(1,128)S(1)}, f32[1,2048]{1,0:T(1,128)S(1)}, u32[]{:S(2)}, u32[]{:S(2)}) collective-permute-start(f32[1,2048]{1,0:T(1,128)S(1)} %add.21.refs_1_), channel_id=1, source_target_pairs={{0,4},{1,5},{2,6},{3,7},{4,0},{5,1},{6,2},{7,3},{8,12},{9,13},{10,... | collective-permute-start | bytes 24584 | tf_op jit(solution)/shard_map/ppermute | solution.py:201
  29.0 5.4 %collective-permute-start.9 = (f32[1,2048]{1,0:T(1,128)S(1)}, f32[1,2048]{1,0:T(1,128)S(1)}, u32[]{:S(2)}, u32[]{:S(2)}) collective-permute-start(f32[1,2048]{1,0:T(1,128)S(1)} %add.21.refs_1_), channel_id=1, source_target_pairs={{0,6},{1,7},{2,4},{3,5},{4,2},{5,3},{6,0},{7,1},{8,14},{9,15},{10,... | collective-permute-start | bytes 24584 | tf_op jit(solution)/shard_map/ppermute | solution.py:201
  40.3 1.2 %collective-permute-start.10 = (f32[1,2048]{1,0:T(1,128)S(1)}, f32[1,2048]{1,0:T(1,128)S(1)}, u32[]{:S(2)}, u32[]{:S(2)}) collective-permute-start(f32[1,2048]{1,0:T(1,128)S(1)} %get-tuple-element.38), channel_id=1, source_target_pairs={{0,1},{1,0},{2,3},{3,2},{4,5},{5,4},{6,7},{7,6},{8,9},{9,8},{10,11... | collective-permute-start | bytes 24584 | tf_op jit(solution)/shard_map/ppermute | solution.py:201
  41.4 7.4 %collective-permute-start.11 = (f32[1,2048]{1,0:T(1,128)S(1)}, f32[1,2048]{1,0:T(1,128)S(1)}, u32[]{:S(2)}, u32[]{:S(2)}) collective-permute-start(f32[1,2048]{1,0:T(1,128)S(1)} %add.22.refs_1_), channel_id=1, source_target_pairs={{0,2},{1,3},{2,0},{3,1},{4,6},{5,7},{6,4},{7,5},{8,10},{9,11},{10,... | collective-permute-start | bytes 24584 | tf_op jit(solution)/shard_map/ppermute | solution.py:201
  41.5 7.3 %collective-permute-start.12 = (f32[1,2048]{1,0:T(1,128)S(1)}, f32[1,2048]{1,0:T(1,128)S(1)}, u32[]{:S(2)}, u32[]{:S(2)}) collective-permute-start(f32[1,2048]{1,0:T(1,128)S(1)} %add.22.refs_1_), channel_id=1, source_target_pairs={{0,4},{1,5},{2,6},{3,7},{4,0},{5,1},{6,2},{7,3},{8,12},{9,13},{10,... | collective-permute-start | bytes 24584 | tf_op jit(solution)/shard_map/ppermute | solution.py:201
  43.4 5.4 %collective-permute-start.13 = (f32[1,2048]{1,0:T(1,128)S(1)}, f32[1,2048]{1,0:T(1,128)S(1)}, u32[]{:S(2)}, u32[]{:S(2)}) collective-permute-start(f32[1,2048]{1,0:T(1,128)S(1)} %add.22.refs_1_), channel_id=1, source_target_pairs={{0,6},{1,7},{2,4},{3,5},{4,2},{5,3},{6,0},{7,1},{8,14},{9,15},{10,... | collective-permute-start | bytes 24584 | tf_op jit(solution)/shard_map/ppermute | solution.py:201
  53.4 1.2 %collective-permute-start.14 = (f32[2,2048]{1,0:T(2,128)S(1)}, f32[2,2048]{1,0:T(2,128)S(1)}, u32[]{:S(2)}, u32[]{:S(2)}) collective-permute-start(f32[2,2048]{1,0:T(2,128)S(1)} %get-tuple-element.43), channel_id=1, source_target_pairs={{0,1},{1,0},{2,3},{3,2},{4,5},{5,4},{6,7},{7,6},{8,9},{9,8},{10,11... | collective-permute-start | bytes 49160 | tf_op jit(solution)/shard_map/ppermute | solution.py:201
  54.7 4.5 %collective-permute-start.15 = (f32[2,2048]{1,0:T(2,128)S(1)}, f32[2,2048]{1,0:T(2,128)S(1)}, u32[]{:S(2)}, u32[]{:S(2)}) collective-permute-start(f32[2,2048]{1,0:T(2,128)S(1)} %add.23.refs_4_), channel_id=1, source_target_pairs={{0,2},{1,3},{2,0},{3,1},{4,6},{5,7},{6,4},{7,5},{8,10},{9,11},{10,... | collective-permute-start | bytes 49160 | tf_op jit(solution)/shard_map/ppermute | solution.py:201
  54.8 4.7 %collective-permute-start.16 = (f32[2,2048]{1,0:T(2,128)S(1)}, f32[2,2048]{1,0:T(2,128)S(1)}, u32[]{:S(2)}, u32[]{:S(2)}) collective-permute-start(f32[2,2048]{1,0:T(2,128)S(1)} %add.23.refs_4_), channel_id=1, source_target_pairs={{0,4},{1,5},{2,6},{3,7},{4,0},{5,1},{6,2},{7,3},{8,12},{9,13},{10,... | collective-permute-start | bytes 49160 | tf_op jit(solution)/shard_map/ppermute | solution.py:201
  57.8 5.5 %collective-permute-start.17 = (f32[2,2048]{1,0:T(2,128)S(1)}, f32[2,2048]{1,0:T(2,128)S(1)}, u32[]{:S(2)}, u32[]{:S(2)}) collective-permute-start(f32[2,2048]{1,0:T(2,128)S(1)} %add.23.refs_4_), channel_id=1, source_target_pairs={{0,6},{1,7},{2,4},{3,5},{4,2},{5,3},{6,0},{7,1},{8,14},{9,15},{10,... | collective-permute-start | bytes 49160 | tf_op jit(solution)/shard_map/ppermute | solution.py:201
  67.0 1.4 %collective-permute-start.18 = (f32[256,128]{1,0:T(8,128)S(1)}, f32[256,128]{1,0:T(8,128)S(1)}, u32[]{:S(2)}, u32[]{:S(2)}) collective-permute-start(f32[256,128]{1,0:T(8,128)S(1)} %get-tuple-element.45), channel_id=1, source_target_pairs={{0,1},{1,0},{2,3},{3,2},{4,5},{5,4},{6,7},{7,6},{8,9},{9,8},{10,11... | collective-permute-start | bytes 393224 | tf_op jit(solution)/shard_map/ppermute | solution.py:201
  68.4 16.7 %collective-permute-start.19 = (f32[256,128]{1,0:T(8,128)S(1)}, f32[256,128]{1,0:T(8,128)S(1)}, u32[]{:S(2)}, u32[]{:S(2)}) collective-permute-start(f32[256,128]{1,0:T(8,128)S(1)} %add.24), channel_id=1, source_target_pairs={{0,2},{1,3},{2,0},{3,1},{4,6},{5,7},{6,4},{7,5},{8,10},{9,11},{10,... | collective-permute-start | bytes 393224 | tf_op jit(solution)/shard_map/ppermute | solution.py:201
  68.5 16.6 %collective-permute-start.20 = (f32[256,128]{1,0:T(8,128)S(1)}, f32[256,128]{1,0:T(8,128)S(1)}, u32[]{:S(2)}, u32[]{:S(2)}) collective-permute-start(f32[256,128]{1,0:T(8,128)S(1)} %add.24), channel_id=1, source_target_pairs={{0,4},{1,5},{2,6},{3,7},{4,0},{5,1},{6,2},{7,3},{8,12},{9,13},{10,... | collective-permute-start | bytes 393224 | tf_op jit(solution)/shard_map/ppermute | solution.py:201
  70.4 14.7 %collective-permute-start.21 = (f32[256,128]{1,0:T(8,128)S(1)}, f32[256,128]{1,0:T(8,128)S(1)}, u32[]{:S(2)}, u32[]{:S(2)}) collective-permute-start(f32[256,128]{1,0:T(8,128)S(1)} %add.24), channel_id=1, source_target_pairs={{0,6},{1,7},{2,4},{3,5},{4,2},{5,3},{6,0},{7,1},{8,14},{9,15},{10,... | collective-permute-start | bytes 393224 | tf_op jit(solution)/shard_map/ppermute | solution.py:201
  85.2 1.4 %collective-permute-start.22 = (f32[256,128]{1,0:T(8,128)S(1)}, f32[256,128]{1,0:T(8,128)S(1)}, u32[]{:S(2)}, u32[]{:S(2)}) collective-permute-start(f32[256,128]{1,0:T(8,128)S(1)} %add_add_fusion), channel_id=1, source_target_pairs={{0,1},{1,0},{2,3},{3,2},{4,5},{5,4},{6,7},{7,6},{8,9},{9,8},{10,11... | collective-permute-start | bytes 393224 | tf_op jit(solution)/shard_map/ppermute | solution.py:201

commit v4 on v3

v4 whole, which is shorter than its diff:
```python
import functools
import math

import jax
import jax.numpy as jnp
from jax import lax
from jax.experimental import pallas as pl
from jax.experimental.pallas import tpu as pltpu
from jax.sharding import PartitionSpec as P

CODE_TEMP = 0.05
PRED_TEMP = 0.1
F32 = jnp.float32
BF16 = jnp.bfloat16
VMEM_LIMIT = 20 << 20
CHUNK = 256
BLOCKS = {"own": 1024, "first": 1024, "den": 512, "middle": 512, "token": 2048, "proto": 1024}


def vmem_spec():
    return pl.BlockSpec(memory_space=pltpu.VMEM)


def shape(*dims, dtype=F32):
    return jax.ShapeDtypeStruct(dims, dtype)


def run(body, outs, args, scratch, resident=(), keep=(), us=1.0, thread=False):
    if thread:
        outs = [shape(*args[0].shape, dtype=args[0].dtype)] + outs
        keep = [0] + [i + 1 for i in keep]
        resident = [0] + list(resident)
    return pl.pallas_call(
        body,
        out_shape=tuple(pltpu.VMEM(s.shape, s.dtype) if i in keep else s for i, s in enumerate(outs)),
        in_specs=[vmem_spec()] * len(args),
        out_specs=tuple(vmem_spec() for _ in outs),
        scratch_shapes=scratch,
        input_output_aliases={0: 0} if thread else {},
        compiler_params=pltpu.CompilerParams(vmem_limit_bytes=VMEM_LIMIT),
        cost_estimate=pl.CostEstimate(flops=int(us * 1e9), bytes_accessed=1 << 20, transcendentals=0),
    )(
        *[
            pltpu.with_memory_space_constraint(a, pltpu.VMEM) if i in resident else a
            for i, a in enumerate(args)
        ]
    )


def normalize(values):
    floats = values.astype(F32)
    mean_square = jnp.mean(floats * floats, axis=-1, keepdims=True)
    return (floats * lax.rsqrt(mean_square + 1e-06)).astype(BF16)


def steps(name, size, step):
    block = min(BLOCKS[name], size)

    def body(i, carry):
        step(pl.ds(pl.multiple_of(i * block, block), block))
        return carry

    lax.fori_loop(0, size // block, body, 0)


def block_of(name, size):
    return min(BLOCKS[name], size // 2)


def pipelined(name, size, fill, work):
    block = block_of(name, size)
    n = size // block

    def at(i):
        return pl.ds(i * block if isinstance(i, int) else pl.multiple_of(i * block, block), block)

    def pair(i):
        fill(at(i), 1)
        work(at(i - 1), 0)
        fill(at(i + 1), 0)
        work(at(i), 1)

    def body(i, carry):
        pair(2 * i + 1)
        return carry

    fill(at(0), 0)
    lax.fori_loop(0, n // 2 - 1, body, 0)
    fill(at(n - 1), 1)
    work(at(n - 2), 0)
    work(at(n - 1), 1)


def chunks(first, last):
    width = min(CHUNK, last - first)
    return [slice(i, i + width) for i in range(first, last, width)]


def similarity(a, b):
    return lax.dot_general(a, b, (((1,), (1,)), ((), ())), preferred_element_type=F32)


def sublane_sums(block):
    return jnp.sum(block.reshape(block.shape[0] // 8, 8, block.shape[1]), axis=0)


def own_codes(proto_ref, token_ref, code_ref, centre_ref, column_ref, *, scale):
    own = token_ref.shape[0]
    tok = normalize(token_ref[...])

    def fill(at, slot):
        centre = normalize(proto_ref[at, :])
        centre_ref[at, :] = centre
        code_ref[at, :own] = jnp.exp2(similarity(centre, tok) * scale)

    def work(at, slot):
        column_ref[at, :] = jnp.sum(code_ref[at, :own], axis=1, keepdims=True)

    pipelined("own", proto_ref.shape[0], fill, work)


def first_pass(*refs, parts, scale, total):
    (_, centre_ref, column_ref), token_refs = refs[:3], refs[3 : 3 + parts]
    code_ref, out_ref, tok, acc = refs[3 + parts :]
    n = token_refs[0].shape[0]
    for i, t in enumerate(token_refs):
        tok[i * n : (i + 1) * n, :] = normalize(t[...])
    acc[...] = jnp.zeros_like(acc)

    def fill(at, slot):
        code_ref[at, n:] = jnp.exp2(similarity(centre_ref[at, :], tok[...]) * scale)

    def work(at, slot):
        columns = column_ref[at, :] + jnp.sum(code_ref[at, n:], axis=1, keepdims=True)
        factor = 1.0 / (total * columns)
        acc[...] += sublane_sums(code_ref[at, :] * factor)

    pipelined("first", centre_ref.shape[0], fill, work)
    out_ref[...] = jnp.sum(acc[...], axis=0, keepdims=True)


def denominators(_, centre_ref, tok_ref, code_ref, out_ref, acc, *slots, scale, first, size):
    acc[...] = jnp.zeros_like(acc)

    def fill(at, slot):
        centre = centre_ref[pl.ds(first + at.start, at.size), :]
        slots[slot][...] = similarity(centre, tok_ref[...])

    def work(at, slot):
        acc[...] += sublane_sums(jnp.exp2(slots[slot][...] * scale))

    pipelined("den", size, fill, work)
    out_ref[...] = jnp.sum(acc[...], axis=0, keepdims=True)


def target_rows(code_in, *refs):
    *token_refs, code_ref, tok = refs
    n = token_refs[0].shape[0]
    for i, t in enumerate(token_refs):
        tok[i * n : (i + 1) * n, :] = normalize(t[...])


def middle_pass(*refs, parts, extras, total):
    sum_refs, extra_refs = refs[1 : 1 + parts], refs[1 + parts : 1 + parts + extras]
    code_ref, out_ref, acc = refs[1 + parts + extras :]
    sums = sum_refs[0][0:1, :]
    for s in sum_refs[1:]:
        sums = sums + s[0:1, :]
    token_scale = 1.0 / sums
    acc[...] = jnp.zeros_like(acc)

    def step(at):
        code = code_ref[at, :]
        factor = 1.0 / (total * jnp.sum(code * token_scale, axis=1, keepdims=True))
        scaled = code * factor
        if extras:
            code_ref[at, :] = scaled
        acc[...] += sublane_sums(scaled)

    steps("middle", code_ref.shape[0], step)
    out_ref[0:1, :] = jnp.sum(acc[...], axis=0, keepdims=True)
    if extras:
        extra = extra_refs[0][...]
        for e in extra_refs[1:]:
            extra = extra + e[...]
        out_ref[1:2, :] = extra


def logit_block(centre, tok_ref, code_ref, scales_ref, logits, at, columns, scale):
    for c in columns:
        pred = jnp.exp2(similarity(centre, tok_ref[c, :]) * scale) * scales_ref[1:2, c]
        logits[:, c] = (pred - code_ref[at, c] * scales_ref[0:1, c]).astype(BF16)


def token_part(*refs, parts, scale, total, own):
    centre_ref, tok_ref = refs[1:3]
    sum_refs = refs[3 : 3 + parts]
    code_ref, mine_ref, other_ref, scales_ref, acc, *logits = refs[3 + parts :]
    core = lax.rem(lax.axis_index("proto"), 2)
    sums = sum_refs[0][...]
    for s in sum_refs[1:]:
        sums = sums + s[...]
    scales_ref[...] = total / sums
    acc[...] = jnp.zeros_like(acc)

    def fill(at, slot):
        logit_block(
            centre_ref[at, :], tok_ref, code_ref, scales_ref, logits[slot], at, chunks(0, own), scale
        )

    def work(at, slot):
        acc[...] += lax.dot_general(
            centre_ref[at, :], logits[slot][...], (((0,), (0,)), ((), ())), preferred_element_type=F32
        )

    pipelined("token", code_ref.shape[0], fill, work)
    acc[...] = acc[...] * total ** (-0.5)
    half = own // 2
    for c in range(2):

        @pl.when(core == c)
        def _():
            mine_ref[...] = acc[:, c * half : (c + 1) * half].T
            other_ref[...] = acc[:, (1 - c) * half : (2 - c) * half].T


def proto_part(code_ref, centre_ref, tok_ref, scales_ref, out_ref, *logits, scale):
    tokens = code_ref.shape[1]

    def fill(at, slot):
        logit_block(
            centre_ref[at, :], tok_ref, code_ref, scales_ref, logits[slot], at, chunks(0, tokens), scale
        )

    def work(at, slot):
        grad = jnp.dot(logits[slot][...], tok_ref[...], preferred_element_type=F32)
        out_ref[at, :] = grad * tokens ** (-0.5)

    pipelined("proto", code_ref.shape[0], fill, work)


def swapped(x, axis, mask):
    return lax.ppermute(x, axis, [(i, i ^ mask) for i in range(lax.axis_size(axis))])


def others_of(x, axis):
    return [swapped(x, axis, m) for m in range(lax.axis_size(axis) - 1, 0, -1)]


def proto_terms(x):
    n = lax.axis_size("proto")
    x = x + swapped(x, "proto", 1)
    terms, unit = [x], 2
    while unit < n:
        group = min(4, n // unit)
        if unit > 2:
            terms = [sum(terms)]
        terms = [terms[0]] + [swapped(terms[0], "proto", unit * m) for m in range(group - 1, 0, -1)]
        unit *= group
    return terms


def chip_sum(x):
    n, unit = lax.axis_size("proto"), 2
    while unit < n:
        group = min(4, n // unit)
        x = sum([swapped(x, "proto", unit * m) for m in range(group - 1, 0, -1)], x)
        unit *= group
    return x


def local(first_view, alternate_augmentation, prototypes):
    own, d = first_view.shape
    k = prototypes.shape[0]
    tokens = own * lax.axis_size("dp")
    total = float(k * lax.axis_size("proto"))
    log2e = math.log2(math.e)
    code_scale = log2e / d / CODE_TEMP
    pred_scale = log2e / d / PRED_TEMP
    acc = pltpu.VMEM((8, tokens), F32)

    def slots(name, size, columns, dtype=F32):
        return [pltpu.VMEM((block_of(name, size), columns), dtype)] * 2


    views = others_of(first_view, "dp")
    code, centres, columns = run(
        functools.partial(own_codes, scale=code_scale),
        [shape(k, tokens), shape(k, d, dtype=BF16), shape(k, 1)],
        [prototypes, first_view],
        [],
        keep=(0, 1, 2),
        us=3,
    )
    alternate_augmentation, columns = lax.optimization_barrier((alternate_augmentation, columns))
    others = others_of(alternate_augmentation, "dp")
    code, sums = run(
        functools.partial(first_pass, parts=len(views), scale=code_scale, total=total),
        [shape(1, tokens)],
        [code, centres, columns] + views,
        [pltpu.VMEM((tokens - own, d), BF16), acc],
        resident=list(range(1, 3 + len(views))),
        keep=[0],
        thread=True,
        us=7,
    )
    terms = proto_terms(sums)
    code, tok = run(
        target_rows,
        [shape(tokens, d, dtype=BF16)],
        [code, alternate_augmentation] + others,
        [],
        keep=[0],
        thread=True,
        us=1,
    )
    dens = []
    for i in range(2):
        code, den = run(
            functools.partial(denominators, scale=pred_scale, first=i * k // 2, size=k // 2),
            [shape(1, tokens)],
            [code, centres, tok],
            [acc] + slots("den", k // 2, tokens),
            resident=[1, 2],
            keep=[0],
            thread=True,
            us=3,
        )
        dens.append(den)
        code, sums = run(
            functools.partial(
                middle_pass, parts=len(terms), extras=2 * i, total=total
            ),
            [shape(1 + i, tokens)],
            [code] + terms + (dens if i else []),
            [acc],
            resident=list(range(1, 1 + len(terms) + 2 * i)),
            keep=[0],
            thread=True,
            us=5,
        )
        terms = proto_terms(sums)
    code, mine, other, scales = run(
        functools.partial(token_part, parts=len(terms), scale=pred_scale, total=total, own=own),
        [shape(own // 2, d), shape(own // 2, d), shape(2, tokens)],
        [code, centres, tok] + terms,
        [pltpu.VMEM((d, own), F32)] + slots("token", k, own, BF16),
        resident=list(range(1, 3 + len(terms))),
        keep=[0, 1, 2],
        thread=True,
        us=4,
    )
    mine = chip_sum(mine + swapped(other, "proto", 1))
    (proto_grad,) = run(
        functools.partial(proto_part, scale=pred_scale),
        [shape(k, d)],
        [code, centres, tok, scales],
        slots("proto", k, tokens, BF16),
        resident=range(4),
        us=10,
    )
    mine, proto_grad = lax.optimization_barrier((mine, proto_grad))
    other = swapped(mine, "proto", 1)
    first = lax.rem(lax.axis_index("proto"), 2) == 0
    token_grad = jnp.where(
        first, jnp.concatenate([mine, other]), jnp.concatenate([other, mine])
    )
    return proto_grad, token_grad


def solution(mesh):
    return jax.shard_map(
        local,
        mesh=mesh,
        in_specs=(P("dp", None), P("dp", None), P("proto", None)),
        out_specs=(P("proto", None), P("dp", None)),
        check_vma=False,
    )
```

time: 87.5 us -> 76.9 us (0.88)
  Pallas kernels: 45.9 us -> 38.7 us
  waiting for transfers between devices: 12.5 us -> 9.82 us
    ppermute x6 -> x0, starting transfers between devices: 9.03 us -> none  [shifted(): lax.ppermute(x, axis, [(i, (i + s) % n) for i in range(n)])]
    ppermute x17 -> x23, starting transfers between devices: 18.3 us -> 26.6 us  [swapped(): lax.ppermute(x, axis, [(i, i ^ mask) for i in range(lax.axis_size(axis))])]
    pallas_call x9, Pallas kernels: 45.9 us -> 38.7 us  [run(): pl.pallas_call(body, out_shape=tuple((pltpu.VMEM(s.shape, s.dtype) if i i...]
    ppermute x17 -> x23, waiting for transfers between devices: 12.4 us -> 9.82 us  [swapped(): lax.ppermute(x, axis, [(i, i ^ mask) for i in range(lax.axis_size(axis))])]
  transfers between devices with their start and end apart: 23 -> 23, of which waited for: 8 -> 9; matrix products, arithmetic and copies ran while one was open for 0% -> 0% of each run, Pallas kernels for 37% -> 35%
where the time goes in v4:
time: 76.9 us; the launch traced here: 76.7 us
  Pallas kernels  38.7 us (50%)
  starting transfers between devices  26.6 us (35%)
  waiting for transfers between devices  9.82 us (13%)
  between operations  0.81 us (1%)
  other arithmetic  0.8 us (1%)
    pallas_call x9, Pallas kernels, run(): pl.pallas_call(body, out_shape=tuple((pltpu.VMEM(s.shape, s.dtype) if i i...  38.7 us
    ppermute x23, starting transfers between devices, swapped(): lax.ppermute(x, axis, [(i, i ^ mask) for i in range(lax.axis_size(axis))])  26.6 us
    ppermute x23, waiting for transfers between devices, swapped(): lax.ppermute(x, axis, [(i, i ^ mask) for i in range(lax.axis_size(axis))])  9.82 us
  transfers between devices with their start and end apart: 23, of which 9 were waited for; matrix products, arithmetic and copies ran while one was open for 0% of the time, Pallas kernels for 35%

profile of v4, /device:TPU:0, one launch (start us, length us, event | category | flops | bytes accessed | tf_op | source)
XLA Modules:
  0.0 76.7 jit_solution(6423165765229995848)
XLA Ops:
  0.6 4.0 %collective-permute-start = (bf16[512,128]{1,0:T(8,128)(2,1)}, bf16[512,128]{1,0:T(8,128)(2,1)S(1)}, u32[]{:S(2)}, u32[]{:S(2)}) collective-permute-start(bf16[512,128]{1,0:T(8,128)(2,1)} %token_ref.1), channel_id=1, source_target_pairs={{0,24},{8,16},{16,8},{24,0},{1,25},{9,17},{17,9},{25,1},{2,26},{10... | collective-permute-start | bytes 393224 | tf_op jit(solution)/shard_map/ppermute | solution.py:243
  5.2 3.3 %shard_map.50 = (f32[4096,2048]{1,0:T(8,128)S(1)}, bf16[4096,128]{1,0:T(8,128)(2,1)S(1)}, f32[4096,1]{1,0:T(8,128)S(1)}) custom-call(bf16[4096,128]{1,0:T(8,128)(2,1)} %proto_ref.1, bf16[512,128]{1,0:T(8,128)(2,1)} %token_ref.1), custom_call_target="tpu_custom_call" | custom-call | flops 3000000000 | bytes 1048576 | tf_op jit(solution)/shard_map/pallas_call | solution.py:33
  8.5 2.9 %collective-permute-start.3 = (bf16[512,128]{1,0:T(8,128)(2,1)}, bf16[512,128]{1,0:T(8,128)(2,1)S(1)}, u32[]{:S(2)}, u32[]{:S(2)}) collective-permute-start(bf16[512,128]{1,0:T(8,128)(2,1)} %refs_0_), channel_id=1, source_target_pairs={{0,24},{8,16},{16,8},{24,0},{1,25},{9,17},{17,9},{25,1},{2,26},{10... | collective-permute-start | bytes 393224 | tf_op jit(solution)/shard_map/ppermute | solution.py:243
  12.1 7.9 %shard_map.51 = (f32[4096,2048]{1,0:T(8,128)S(1)}, f32[1,2048]{1,0:T(1,128)S(1)}) custom-call(f32[4096,2048]{1,0:T(8,128)S(1)} %get-tuple-element.25.refs_0_, bf16[4096,128]{1,0:T(8,128)(2,1)S(1)} %get-tuple-element.26.refs_1_.centre_ref, f32[4096,1]{1,0:T(8,128)S(1)} %get-tuple-element.28.refs_2_, ...), custom_call_target="tpu_custom_call", output_to_operand_aliasing={{0}: (0, {})} | custom-call | flops 7000000000 | bytes 1048576 | tf_op jit(solution)/shard_map/pallas_call | solution.py:33
  21.2 4.1 %collective-permute-start.7 = (f32[1,2048]{1,0:T(1,128)S(1)}, f32[1,2048]{1,0:T(1,128)S(1)}, u32[]{:S(2)}, u32[]{:S(2)}) collective-permute-start(f32[1,2048]{1,0:T(1,128)S(1)} %add.21.refs_1_), channel_id=1, source_target_pairs={{0,6},{1,7},{2,4},{3,5},{4,2},{5,3},{6,0},{7,1},{8,14},{9,15},{10,... | collective-permute-start | bytes 24584 | tf_op jit(solution)/shard_map/ppermute | solution.py:243
  25.9 2.6 %shard_map.53 = (f32[4096,2048]{1,0:T(8,128)S(1)}, f32[1,2048]{1,0:T(1,128)S(1)}) custom-call(f32[4096,2048]{1,0:T(8,128)S(1)} %get-tuple-element.31._, bf16[4096,128]{1,0:T(8,128)(2,1)S(1)} %get-tuple-element.26.refs_1_.centre_ref, bf16[2048,128]{1,0:T(8,128)(2,1)S(1)} %get-tuple-element.32.tok_ref.refs_2_), custom_call_target="tpu_custom_call", output_to_operand_aliasing={{0}: (0, {})} | custom-call | flops 3000000000 | bytes 1048576 | tf_op jit(solution)/shard_map/pallas_call | solution.py:33
  28.5 1.3 %collective-permute-done.8.refs_3_ = f32[1,2048]{1,0:T(1,128)S(1)} collective-permute-done((f32[1,2048]{1,0:T(1,128)S(1)}, f32[1,2048]{1,0:T(1,128)S(1)}, u32[]{:S(2)}, u32[]{:S(2)}) %collective-permute-start.8) | collective-permute-done | bytes 8224 | tf_op jit(solution)/shard_map/ppermute | solution.py:243
  29.8 4.5 %shard_map.54 = (f32[4096,2048]{1,0:T(8,128)S(1)}, f32[1,2048]{1,0:T(1,128)S(1)}) custom-call(f32[4096,2048]{1,0:T(8,128)S(1)} %get-tuple-element.33.refs_0_, f32[1,2048]{1,0:T(1,128)S(1)} %add.21.refs_1_, f32[1,2048]{1,0:T(1,128)S(1)} %collective-permute-done.7.refs_2_, ...), custom_call_target="tpu_custom_call", output_to_operand_aliasing={{0}: (0, {})} | custom-call | flops 5000000000 | bytes 1048576 | tf_op jit(solution)/shard_map/pallas_call | solution.py:33
  34.4 1.2 %collective-permute-done.10 = f32[1,2048]{1,0:T(1,128)S(1)} collective-permute-done((f32[1,2048]{1,0:T(1,128)S(1)}, f32[1,2048]{1,0:T(1,128)S(1)}, u32[]{:S(2)}, u32[]{:S(2)}) %collective-permute-start.10) | collective-permute-done | bytes 8224 | tf_op jit(solution)/shard_map/ppermute | solution.py:243
  35.6 2.5 %collective-permute-start.11 = (f32[1,2048]{1,0:T(1,128)S(1)}, f32[1,2048]{1,0:T(1,128)S(1)}, u32[]{:S(2)}, u32[]{:S(2)}) collective-permute-start(f32[1,2048]{1,0:T(1,128)S(1)} %add.22.refs_1_), channel_id=1, source_target_pairs={{0,6},{1,7},{2,4},{3,5},{4,2},{5,3},{6,0},{7,1},{8,14},{9,15},{10,... | collective-permute-start | bytes 24584 | tf_op jit(solution)/shard_map/ppermute | solution.py:243
  38.1 2.0 %collective-permute-start.13 = (f32[1,2048]{1,0:T(1,128)S(1)}, f32[1,2048]{1,0:T(1,128)S(1)}, u32[]{:S(2)}, u32[]{:S(2)}) collective-permute-start(f32[1,2048]{1,0:T(1,128)S(1)} %add.22.refs_1_), channel_id=1, source_target_pairs={{0,2},{1,3},{2,0},{3,1},{4,6},{5,7},{6,4},{7,5},{8,10},{9,11},{10,... | collective-permute-start | bytes 24584 | tf_op jit(solution)/shard_map/ppermute | solution.py:243
  40.1 2.4 %shard_map.55 = (f32[4096,2048]{1,0:T(8,128)S(1)}, f32[1,2048]{1,0:T(1,128)S(1)}) custom-call(f32[4096,2048]{1,0:T(8,128)S(1)} %get-tuple-element.35._, bf16[4096,128]{1,0:T(8,128)(2,1)S(1)} %get-tuple-element.26.refs_1_.centre_ref, bf16[2048,128]{1,0:T(8,128)(2,1)S(1)} %get-tuple-element.32.tok_ref.refs_2_), custom_call_target="tpu_custom_call", output_to_operand_aliasing={{0}: (0, {})} | custom-call | flops 3000000000 | bytes 1048576 | tf_op jit(solution)/shard_map/pallas_call | solution.py:33
  42.7 4.9 %shard_map.56 = (f32[4096,2048]{1,0:T(8,128)S(1)}, f32[2,2048]{1,0:T(2,128)S(1)}) custom-call(f32[4096,2048]{1,0:T(8,128)S(1)} %get-tuple-element.36.refs_0_, f32[1,2048]{1,0:T(1,128)S(1)} %add.22.refs_1_, f32[1,2048]{1,0:T(1,128)S(1)} %collective-permute-done.11.refs_2_, ...), custom_call_target="tpu_custom_call", output_to_operand_aliasing={{0}: (0, {})} | custom-call | flops 5000000000 | bytes 1048576 | tf_op jit(solution)/shard_map/pallas_call | solution.py:33
  47.7 1.2 %collective-permute-done.14 = f32[2,2048]{1,0:T(2,128)S(1)} collective-permute-done((f32[2,2048]{1,0:T(2,128)S(1)}, f32[2,2048]{1,0:T(2,128)S(1)}, u32[]{:S(2)}, u32[]{:S(2)}) %collective-permute-start.14) | collective-permute-done | bytes 16416 | tf_op jit(solution)/shard_map/ppermute | solution.py:243
  48.9 2.3 %collective-permute-start.15 = (f32[2,2048]{1,0:T(2,128)S(1)}, f32[2,2048]{1,0:T(2,128)S(1)}, u32[]{:S(2)}, u32[]{:S(2)}) collective-permute-start(f32[2,2048]{1,0:T(2,128)S(1)} %add.23.refs_3_), channel_id=1, source_target_pairs={{0,6},{1,7},{2,4},{3,5},{4,2},{5,3},{6,0},{7,1},{8,14},{9,15},{10,... | collective-permute-start | bytes 49160 | tf_op jit(solution)/shard_map/ppermute | solution.py:243
  51.4 1.9 %collective-permute-start.17 = (f32[2,2048]{1,0:T(2,128)S(1)}, f32[2,2048]{1,0:T(2,128)S(1)}, u32[]{:S(2)}, u32[]{:S(2)}) collective-permute-start(f32[2,2048]{1,0:T(2,128)S(1)} %add.23.refs_3_), channel_id=1, source_target_pairs={{0,2},{1,3},{2,0},{3,1},{4,6},{5,7},{6,4},{7,5},{8,10},{9,11},{10,... | collective-permute-start | bytes 49160 | tf_op jit(solution)/shard_map/ppermute | solution.py:243
  53.3 1.3 %collective-permute-done.15.refs_4_ = f32[2,2048]{1,0:T(2,128)S(1)} collective-permute-done((f32[2,2048]{1,0:T(2,128)S(1)}, f32[2,2048]{1,0:T(2,128)S(1)}, u32[]{:S(2)}, u32[]{:S(2)}) %collective-permute-start.15) | collective-permute-done | bytes 16416 | tf_op jit(solution)/shard_map/ppermute | solution.py:243
  54.6 1.2 %collective-permute-done.16.refs_5_ = f32[2,2048]{1,0:T(2,128)S(1)} collective-permute-done((f32[2,2048]{1,0:T(2,128)S(1)}, f32[2,2048]{1,0:T(2,128)S(1)}, u32[]{:S(2)}, u32[]{:S(2)}) %collective-permute-start.16) | collective-permute-done | bytes 16416 | tf_op jit(solution)/shard_map/ppermute | solution.py:243
  55.8 2.5 %shard_map.57 = (f32[4096,2048]{1,0:T(8,128)S(1)}, f32[256,128]{1,0:T(8,128)S(1)}, f32[256,128]{1,0:T(8,128)S(1)}, f32[2,2048]{1,0:T(2,128)S(1)}) custom-call(f32[4096,2048]{1,0:T(8,128)S(1)} %get-tuple-element.40.refs_0_, bf16[4096,128]{1,0:T(8,128)(2,1)S(1)} %get-tuple-element.26.refs_1_.centre_ref, ...), custom_call_target="tpu_custom_call", output_to_operand_aliasing={{0}: (0, {})} | custom-call | flops 4000000000 | bytes 1048576 | tf_op jit(solution)/shard_map/pallas_call | solution.py:33
  58.3 1.3 %collective-permute-done.18 = f32[256,128]{1,0:T(8,128)S(1)} collective-permute-done((f32[256,128]{1,0:T(8,128)S(1)}, f32[256,128]{1,0:T(8,128)S(1)}, u32[]{:S(2)}, u32[]{:S(2)}) %collective-permute-start.18) | collective-permute-done | bytes 131104 | tf_op jit(solution)/shard_map/ppermute | solution.py:243
  59.7 1.9 %collective-permute-start.19 = (f32[256,128]{1,0:T(8,128)S(1)}, f32[256,128]{1,0:T(8,128)S(1)}, u32[]{:S(2)}, u32[]{:S(2)}) collective-permute-start(f32[256,128]{1,0:T(8,128)S(1)} %add.24), channel_id=1, source_target_pairs={{0,6},{1,7},{2,4},{3,5},{4,2},{5,3},{6,0},{7,1},{8,14},{9,15},{10,... | collective-permute-start | bytes 393224 | tf_op jit(solution)/shard_map/ppermute | solution.py:243
  62.5 1.7 %collective-permute-start.21 = (f32[256,128]{1,0:T(8,128)S(1)}, f32[256,128]{1,0:T(8,128)S(1)}, u32[]{:S(2)}, u32[]{:S(2)}) collective-permute-start(f32[256,128]{1,0:T(8,128)S(1)} %add.24), channel_id=1, source_target_pairs={{0,2},{1,3},{2,0},{3,1},{4,6},{5,7},{6,4},{7,5},{8,10},{9,11},{10,... | collective-permute-start | bytes 393224 | tf_op jit(solution)/shard_map/ppermute | solution.py:243
  64.1 10.4 %shard_map.58 = f32[4096,128]{1,0:T(8,128)} custom-call(f32[4096,2048]{1,0:T(8,128)S(1)} %get-tuple-element.44.code_ref, bf16[4096,128]{1,0:T(8,128)(2,1)S(1)} %get-tuple-element.26.refs_1_.centre_ref, bf16[2048,128]{1,0:T(8,128)(2,1)S(1)} %get-tuple-element.32.tok_ref.refs_2_, f32[2,2048]{1,0:T(2,128)S(1)} %get-tuple-element.45.scales_ref), custom_call_target="tpu_custom_call" | custom-call | flops 10000000000 | bytes 1048576 | tf_op jit(solution)/shard_map/pallas_call | solution.py:33
  74.7 1.3 %collective-permute-done.22 = f32[256,128]{1,0:T(8,128)S(1)} collective-permute-done((f32[256,128]{1,0:T(8,128)S(1)}, f32[256,128]{1,0:T(8,128)S(1)}, u32[]{:S(2)}, u32[]{:S(2)}) %collective-permute-start.22) | collective-permute-done | bytes 131104 | tf_op jit(solution)/shard_map/ppermute | solution.py:243
  (39 shorter events, 5.7 us)
Async XLA Ops:
  0.6 19.5 %copy-start = (bf16[512,128]{1,0:T(8,128)(2,1)S(1)}, bf16[512,128]{1,0:T(8,128)(2,1)}, u32[]{:S(2)}) copy-start(bf16[512,128]{1,0:T(8,128)(2,1)} %refs_0_) | copy-start | bytes 393220
  0.6 11.3 %collective-permute-start = (bf16[512,128]{1,0:T(8,128)(2,1)}, bf16[512,128]{1,0:T(8,128)(2,1)S(1)}, u32[]{:S(2)}, u32[]{:S(2)}) collective-permute-start(bf16[512,128]{1,0:T(8,128)(2,1)} %token_ref.1), channel_id=1, source_target_pairs={{0,24},{8,16},{16,8},{24,0},{1,25},{9,17},{17,9},{25,1},{2,26},{10... | collective-permute-start | bytes 393224 | tf_op jit(solution)/shard_map/ppermute | solution.py:243
  4.6 7.5 %collective-permute-start.1 = (bf16[512,128]{1,0:T(8,128)(2,1)}, bf16[512,128]{1,0:T(8,128)(2,1)S(1)}, u32[]{:S(2)}, u32[]{:S(2)}) collective-permute-start(bf16[512,128]{1,0:T(8,128)(2,1)} %token_ref.1), channel_id=1, source_target_pairs={{0,16},{8,24},{16,0},{24,8},{1,17},{9,25},{17,1},{25,9},{2,18},{10... | collective-permute-start | bytes 393224 | tf_op jit(solution)/shard_map/ppermute | solution.py:243
  5.1 7.0 %collective-permute-start.2 = (bf16[512,128]{1,0:T(8,128)(2,1)}, bf16[512,128]{1,0:T(8,128)(2,1)S(1)}, u32[]{:S(2)}, u32[]{:S(2)}) collective-permute-start(bf16[512,128]{1,0:T(8,128)(2,1)} %token_ref.1), channel_id=1, source_target_pairs={{0,8},{8,0},{16,24},{24,16},{1,9},{9,1},{17,25},{25,17},{2,10},{10... | collective-permute-start | bytes 393224 | tf_op jit(solution)/shard_map/ppermute | solution.py:243
  8.5 11.6 %collective-permute-start.3 = (bf16[512,128]{1,0:T(8,128)(2,1)}, bf16[512,128]{1,0:T(8,128)(2,1)S(1)}, u32[]{:S(2)}, u32[]{:S(2)}) collective-permute-start(bf16[512,128]{1,0:T(8,128)(2,1)} %refs_0_), channel_id=1, source_target_pairs={{0,24},{8,16},{16,8},{24,0},{1,25},{9,17},{17,9},{25,1},{2,26},{10... | collective-permute-start | bytes 393224 | tf_op jit(solution)/shard_map/ppermute | solution.py:243
  11.4 8.7 %collective-permute-start.4 = (bf16[512,128]{1,0:T(8,128)(2,1)}, bf16[512,128]{1,0:T(8,128)(2,1)S(1)}, u32[]{:S(2)}, u32[]{:S(2)}) collective-permute-start(bf16[512,128]{1,0:T(8,128)(2,1)} %refs_0_), channel_id=1, source_target_pairs={{0,16},{8,24},{16,0},{24,8},{1,17},{9,25},{17,1},{25,9},{2,18},{10... | collective-permute-start | bytes 393224 | tf_op jit(solution)/shard_map/ppermute | solution.py:243
  11.9 8.1 %collective-permute-start.5 = (bf16[512,128]{1,0:T(8,128)(2,1)}, bf16[512,128]{1,0:T(8,128)(2,1)S(1)}, u32[]{:S(2)}, u32[]{:S(2)}) collective-permute-start(bf16[512,128]{1,0:T(8,128)(2,1)} %refs_0_), channel_id=1, source_target_pairs={{0,8},{8,0},{16,24},{24,16},{1,9},{9,1},{17,25},{25,17},{2,10},{10... | collective-permute-start | bytes 393224 | tf_op jit(solution)/shard_map/ppermute | solution.py:243
  20.0 1.2 %collective-permute-start.6 = (f32[1,2048]{1,0:T(1,128)S(1)}, f32[1,2048]{1,0:T(1,128)S(1)}, u32[]{:S(2)}, u32[]{:S(2)}) collective-permute-start(f32[1,2048]{1,0:T(1,128)S(1)} %get-tuple-element.34), channel_id=1, source_target_pairs={{0,1},{1,0},{2,3},{3,2},{4,5},{5,4},{6,7},{7,6},{8,9},{9,8},{10,11... | collective-permute-start | bytes 24584 | tf_op jit(solution)/shard_map/ppermute | solution.py:243
  21.2 7.3 %collective-permute-start.7 = (f32[1,2048]{1,0:T(1,128)S(1)}, f32[1,2048]{1,0:T(1,128)S(1)}, u32[]{:S(2)}, u32[]{:S(2)}) collective-permute-start(f32[1,2048]{1,0:T(1,128)S(1)} %add.21.refs_1_), channel_id=1, source_target_pairs={{0,6},{1,7},{2,4},{3,5},{4,2},{5,3},{6,0},{7,1},{8,14},{9,15},{10,... | collective-permute-start | bytes 24584 | tf_op jit(solution)/shard_map/ppermute | solution.py:243
  25.3 4.5 %collective-permute-start.8 = (f32[1,2048]{1,0:T(1,128)S(1)}, f32[1,2048]{1,0:T(1,128)S(1)}, u32[]{:S(2)}, u32[]{:S(2)}) collective-permute-start(f32[1,2048]{1,0:T(1,128)S(1)} %add.21.refs_1_), channel_id=1, source_target_pairs={{0,4},{1,5},{2,6},{3,7},{4,0},{5,1},{6,2},{7,3},{8,12},{9,13},{10,... | collective-permute-start | bytes 24584 | tf_op jit(solution)/shard_map/ppermute | solution.py:243
  25.3 4.5 %collective-permute-start.9 = (f32[1,2048]{1,0:T(1,128)S(1)}, f32[1,2048]{1,0:T(1,128)S(1)}, u32[]{:S(2)}, u32[]{:S(2)}) collective-permute-start(f32[1,2048]{1,0:T(1,128)S(1)} %add.21.refs_1_), channel_id=1, source_target_pairs={{0,2},{1,3},{2,0},{3,1},{4,6},{5,7},{6,4},{7,5},{8,10},{9,11},{10,... | collective-permute-start | bytes 24584 | tf_op jit(solution)/shard_map/ppermute | solution.py:243
  34.4 1.2 %collective-permute-start.10 = (f32[1,2048]{1,0:T(1,128)S(1)}, f32[1,2048]{1,0:T(1,128)S(1)}, u32[]{:S(2)}, u32[]{:S(2)}) collective-permute-start(f32[1,2048]{1,0:T(1,128)S(1)} %get-tuple-element.37), channel_id=1, source_target_pairs={{0,1},{1,0},{2,3},{3,2},{4,5},{5,4},{6,7},{7,6},{8,9},{9,8},{10,11... | collective-permute-start | bytes 24584 | tf_op jit(solution)/shard_map/ppermute | solution.py:243
  35.6 6.8 %collective-permute-start.11 = (f32[1,2048]{1,0:T(1,128)S(1)}, f32[1,2048]{1,0:T(1,128)S(1)}, u32[]{:S(2)}, u32[]{:S(2)}) collective-permute-start(f32[1,2048]{1,0:T(1,128)S(1)} %add.22.refs_1_), channel_id=1, source_target_pairs={{0,6},{1,7},{2,4},{3,5},{4,2},{5,3},{6,0},{7,1},{8,14},{9,15},{10,... | collective-permute-start | bytes 24584 | tf_op jit(solution)/shard_map/ppermute | solution.py:243
  38.1 4.5 %collective-permute-start.12 = (f32[1,2048]{1,0:T(1,128)S(1)}, f32[1,2048]{1,0:T(1,128)S(1)}, u32[]{:S(2)}, u32[]{:S(2)}) collective-permute-start(f32[1,2048]{1,0:T(1,128)S(1)} %add.22.refs_1_), channel_id=1, source_target_pairs={{0,4},{1,5},{2,6},{3,7},{4,0},{5,1},{6,2},{7,3},{8,12},{9,13},{10,... | collective-permute-start | bytes 24584 | tf_op jit(solution)/shard_map/ppermute | solution.py:243
  38.1 4.5 %collective-permute-start.13 = (f32[1,2048]{1,0:T(1,128)S(1)}, f32[1,2048]{1,0:T(1,128)S(1)}, u32[]{:S(2)}, u32[]{:S(2)}) collective-permute-start(f32[1,2048]{1,0:T(1,128)S(1)} %add.22.refs_1_), channel_id=1, source_target_pairs={{0,2},{1,3},{2,0},{3,1},{4,6},{5,7},{6,4},{7,5},{8,10},{9,11},{10,... | collective-permute-start | bytes 24584 | tf_op jit(solution)/shard_map/ppermute | solution.py:243
  47.6 1.2 %collective-permute-start.14 = (f32[2,2048]{1,0:T(2,128)S(1)}, f32[2,2048]{1,0:T(2,128)S(1)}, u32[]{:S(2)}, u32[]{:S(2)}) collective-permute-start(f32[2,2048]{1,0:T(2,128)S(1)} %get-tuple-element.41), channel_id=1, source_target_pairs={{0,1},{1,0},{2,3},{3,2},{4,5},{5,4},{6,7},{7,6},{8,9},{9,8},{10,11... | collective-permute-start | bytes 49160 | tf_op jit(solution)/shard_map/ppermute | solution.py:243
  48.9 5.7 %collective-permute-start.15 = (f32[2,2048]{1,0:T(2,128)S(1)}, f32[2,2048]{1,0:T(2,128)S(1)}, u32[]{:S(2)}, u32[]{:S(2)}) collective-permute-start(f32[2,2048]{1,0:T(2,128)S(1)} %add.23.refs_3_), channel_id=1, source_target_pairs={{0,6},{1,7},{2,4},{3,5},{4,2},{5,3},{6,0},{7,1},{8,14},{9,15},{10,... | collective-permute-start | bytes 49160 | tf_op jit(solution)/shard_map/ppermute | solution.py:243
  51.1 4.6 %collective-permute-start.16 = (f32[2,2048]{1,0:T(2,128)S(1)}, f32[2,2048]{1,0:T(2,128)S(1)}, u32[]{:S(2)}, u32[]{:S(2)}) collective-permute-start(f32[2,2048]{1,0:T(2,128)S(1)} %add.23.refs_3_), channel_id=1, source_target_pairs={{0,4},{1,5},{2,6},{3,7},{4,0},{5,1},{6,2},{7,3},{8,12},{9,13},{10,... | collective-permute-start | bytes 49160 | tf_op jit(solution)/shard_map/ppermute | solution.py:243
  51.4 4.3 %collective-permute-start.17 = (f32[2,2048]{1,0:T(2,128)S(1)}, f32[2,2048]{1,0:T(2,128)S(1)}, u32[]{:S(2)}, u32[]{:S(2)}) collective-permute-start(f32[2,2048]{1,0:T(2,128)S(1)} %add.23.refs_3_), channel_id=1, source_target_pairs={{0,2},{1,3},{2,0},{3,1},{4,6},{5,7},{6,4},{7,5},{8,10},{9,11},{10,... | collective-permute-start | bytes 49160 | tf_op jit(solution)/shard_map/ppermute | solution.py:243
  58.3 1.4 %collective-permute-start.18 = (f32[256,128]{1,0:T(8,128)S(1)}, f32[256,128]{1,0:T(8,128)S(1)}, u32[]{:S(2)}, u32[]{:S(2)}) collective-permute-start(f32[256,128]{1,0:T(8,128)S(1)} %get-tuple-element.43), channel_id=1, source_target_pairs={{0,1},{1,0},{2,3},{3,2},{4,5},{5,4},{6,7},{7,6},{8,9},{9,8},{10,11... | collective-permute-start | bytes 393224 | tf_op jit(solution)/shard_map/ppermute | solution.py:243
  59.7 14.9 %collective-permute-start.19 = (f32[256,128]{1,0:T(8,128)S(1)}, f32[256,128]{1,0:T(8,128)S(1)}, u32[]{:S(2)}, u32[]{:S(2)}) collective-permute-start(f32[256,128]{1,0:T(8,128)S(1)} %add.24), channel_id=1, source_target_pairs={{0,6},{1,7},{2,4},{3,5},{4,2},{5,3},{6,0},{7,1},{8,14},{9,15},{10,... | collective-permute-start | bytes 393224 | tf_op jit(solution)/shard_map/ppermute | solution.py:243
  61.6 13.0 %collective-permute-start.20 = (f32[256,128]{1,0:T(8,128)S(1)}, f32[256,128]{1,0:T(8,128)S(1)}, u32[]{:S(2)}, u32[]{:S(2)}) collective-permute-start(f32[256,128]{1,0:T(8,128)S(1)} %add.24), channel_id=1, source_target_pairs={{0,4},{1,5},{2,6},{3,7},{4,0},{5,1},{6,2},{7,3},{8,12},{9,13},{10,... | collective-permute-start | bytes 393224 | tf_op jit(solution)/shard_map/ppermute | solution.py:243
  62.5 12.1 %collective-permute-start.21 = (f32[256,128]{1,0:T(8,128)S(1)}, f32[256,128]{1,0:T(8,128)S(1)}, u32[]{:S(2)}, u32[]{:S(2)}) collective-permute-start(f32[256,128]{1,0:T(8,128)S(1)} %add.24), channel_id=1, source_target_pairs={{0,2},{1,3},{2,0},{3,1},{4,6},{5,7},{6,4},{7,5},{8,10},{9,11},{10,... | collective-permute-start | bytes 393224 | tf_op jit(solution)/shard_map/ppermute | solution.py:243
  74.6 1.4 %collective-permute-start.22 = (f32[256,128]{1,0:T(8,128)S(1)}, f32[256,128]{1,0:T(8,128)S(1)}, u32[]{:S(2)}, u32[]{:S(2)}) collective-permute-start(f32[256,128]{1,0:T(8,128)S(1)} %add_add_fusion), channel_id=1, source_target_pairs={{0,1},{1,0},{2,3},{3,2},{4,5},{5,4},{6,7},{7,6},{8,9},{9,8},{10,11... | collective-permute-start | bytes 393224 | tf_op jit(solution)/shard_map/ppermute | solution.py:243

commit v5 on v3

v5 whole, which is shorter than its diff:
```python
import functools
import math

import jax
import jax.numpy as jnp
from jax import lax
from jax.experimental import pallas as pl
from jax.experimental.pallas import tpu as pltpu
from jax.sharding import PartitionSpec as P

CODE_TEMP = 0.05
PRED_TEMP = 0.1
F32 = jnp.float32
BF16 = jnp.bfloat16
VMEM_LIMIT = 20 << 20
CHUNK = 256
BLOCKS = {"own": 2048, "first": 1024, "den": 2048, "middle": 512, "token": 2048}
SPLIT = 3
TILE = 16


def vmem_spec():
    return pl.BlockSpec(memory_space=pltpu.VMEM)


def shape(*dims, dtype=F32):
    return jax.ShapeDtypeStruct(dims, dtype)


def run(body, outs, args, scratch, resident=(), keep=(), us=1.0, thread=False):
    if thread:
        outs = [shape(*args[0].shape, dtype=args[0].dtype)] + outs
        keep = [0] + [i + 1 for i in keep]
        resident = [0] + list(resident)
    return pl.pallas_call(
        body,
        out_shape=tuple(pltpu.VMEM(s.shape, s.dtype) if i in keep else s for i, s in enumerate(outs)),
        in_specs=[vmem_spec()] * len(args),
        out_specs=tuple(vmem_spec() for _ in outs),
        scratch_shapes=scratch,
        input_output_aliases={0: 0} if thread else {},
        compiler_params=pltpu.CompilerParams(vmem_limit_bytes=VMEM_LIMIT),
        cost_estimate=pl.CostEstimate(flops=int(us * 1e9), bytes_accessed=1 << 20, transcendentals=0),
    )(
        *[
            pltpu.with_memory_space_constraint(a, pltpu.VMEM) if i in resident else a
            for i, a in enumerate(args)
        ]
    )


def normalize(values):
    floats = values.astype(F32)
    mean_square = jnp.mean(floats * floats, axis=-1, keepdims=True)
    return (floats * lax.rsqrt(mean_square + 1e-06)).astype(BF16)


def steps(name, size, step):
    block = min(BLOCKS[name], size)

    def body(i, carry):
        step(pl.ds(pl.multiple_of(i * block, block), block))
        return carry

    lax.fori_loop(0, size // block, body, 0)


def block_of(name, size):
    return min(BLOCKS[name], size // 2)


def pipelined(n, fill, work):
    def body(i, carry):
        fill(2 * i + 1, 1)
        work(2 * i, 0)
        fill(2 * i + 2, 0)
        work(2 * i + 1, 1)
        return carry

    fill(0, 0)
    lax.fori_loop(0, n // 2 - 1, body, 0)
    fill(n - 1, 1)
    work(n - 2, 0)
    work(n - 1, 1)


def part(i, size):
    return pl.ds(i * size if isinstance(i, int) else pl.multiple_of(i * size, size), size)


def similarity(a, b):
    return lax.dot_general(a, b, (((1,), (1,)), ((), ())), preferred_element_type=F32)


def sublane_sums(block):
    return jnp.sum(block.reshape(block.shape[0] // 8, 8, block.shape[1]), axis=0)


def lane_sums(block):
    return sum(block[:, i : i + 128] for i in range(0, block.shape[1], 128))


def own_codes(proto_ref, token_ref, code_ref, centre_ref, column_ref, *, scale):
    own = token_ref.shape[0]
    tok = normalize(token_ref[...])

    def step(at):
        centre = normalize(proto_ref[at, :])
        centre_ref[at, :] = centre
        code = jnp.exp2(similarity(centre, tok) * scale)
        code_ref[at, :own] = code
        column_ref[at, :] = lane_sums(code)

    steps("own", proto_ref.shape[0], step)


def first_pass(*refs, parts, scale, total):
    (_, centre_ref, column_ref), token_refs = refs[:3], refs[3 : 3 + parts]
    code_ref, out_ref, tok, acc, columns = refs[3 + parts :]
    n = token_refs[0].shape[0]
    for i, t in enumerate(token_refs):
        tok[i * n : (i + 1) * n, :] = normalize(t[...])
    acc[...] = jnp.zeros_like(acc)
    block = block_of("first", centre_ref.shape[0])

    def fill(i, slot):
        at = part(i, block)
        code = jnp.exp2(similarity(centre_ref[at, :], tok[...]) * scale)
        code_ref[at, n:] = code
        columns[at, :] = column_ref[at, :] + lane_sums(code)

    def work(i, slot):
        at = part(i, block)
        factor = 1.0 / (total * jnp.sum(columns[at, :], axis=1, keepdims=True))
        acc[...] += sublane_sums(code_ref[at, :] * factor)

    pipelined(centre_ref.shape[0] // block, fill, work)
    out_ref[...] = jnp.sum(acc[...], axis=0, keepdims=True)


def denominators(_, centre_ref, token_ref, code_ref, tok_ref, out_ref, acc, *, scale):
    tok_ref[...] = normalize(token_ref[...])
    acc[...] = jnp.zeros_like(acc)

    def step(at):
        acc[...] += sublane_sums(jnp.exp2(similarity(centre_ref[at, :], tok_ref[...]) * scale))

    steps("den", centre_ref.shape[0], step)
    out_ref[...] = jnp.sum(acc[...], axis=0, keepdims=True)


def term_sum(refs):
    return functools.reduce(lambda a, b: a + b, [r[...] for r in refs])


def middle_pass(*refs, parts, total):
    den_ref, (code_ref, out_ref, acc) = refs[1 + parts], refs[2 + parts :]
    token_scale = 1.0 / term_sum(refs[1 : 1 + parts])
    acc[...] = jnp.zeros_like(acc)

    def step(at):
        code = code_ref[at, :]
        factor = 1.0 / (total * jnp.sum(code * token_scale, axis=1, keepdims=True))
        acc[...] += sublane_sums(code * factor)

    steps("middle", code_ref.shape[0], step)
    tokens = acc.shape[1]
    out_ref[:, :tokens] = jnp.sum(acc[...], axis=0, keepdims=True)
    out_ref[:, tokens:] = den_ref[...]


def last_pass(*refs, parts, total):
    tok_ref, (code_ref, out_ref, weight_ref, pack_ref, acc) = refs[1 + parts], refs[2 + parts :]
    tokens, own = acc.shape[1], tok_ref.shape[0]
    sums = term_sum(refs[1 : 1 + parts])
    token_scale = 1.0 / sums[:, :tokens]
    weight = total / sums[:, tokens:]
    weight_ref[...] = weight
    pack_ref[:own, :] = tok_ref[...]
    lines = [weight[:, i : i + 128] for i in range(0, own, 128)]
    pieces, rest = [], jnp.concatenate(lines, axis=0)
    for _ in range(SPLIT):
        piece = rest.astype(BF16).astype(F32)
        pieces.append(piece)
        rest = rest - piece
    rows = SPLIT * len(lines)
    pad = -rows % TILE
    pack_ref[own:, :] = jnp.concatenate(pieces + [jnp.zeros((pad, 128), F32)], axis=0).astype(BF16)
    acc[...] = jnp.zeros_like(acc)

    def step(at):
        code = code_ref[at, :]
        factor = 1.0 / (total * jnp.sum(code * token_scale, axis=1, keepdims=True))
        scaled = code * factor
        code_ref[at, :] = scaled
        acc[...] += sublane_sums(scaled)

    steps("middle", code_ref.shape[0], step)
    out_ref[...] = jnp.sum(acc[...], axis=0, keepdims=True)


def logit(centre, tok, code, token_scale, weight, scale):
    pred = jnp.exp2(similarity(centre, tok) * scale) * weight
    return (pred - code * token_scale).astype(BF16)


def token_part(*refs, parts, scale, total):
    centre_ref, tok_ref, weight_ref = refs[1:4]
    code_ref, mine_ref, other_ref, scale_ref, logit_ref, acc = refs[4 + parts :]
    own = tok_ref.shape[0]
    core = lax.rem(lax.axis_index("proto"), 2)
    scale_ref[...] = total / term_sum(refs[4 : 4 + parts])
    acc[...] = jnp.zeros_like(acc)
    block = block_of("token", code_ref.shape[0])

    def fill(i, slot):
        at = part(i, block)
        for c in range(0, own, CHUNK):
            c = slice(c, min(c + CHUNK, own))
            logit_ref[at, c] = logit(
                centre_ref[at, :], tok_ref[c, :], code_ref[at, c], scale_ref[:, c], weight_ref[:, c], scale
            )

    def work(i, slot):
        at = part(i, block)
        acc[...] += lax.dot_general(
            centre_ref[at, :], logit_ref[at, :], (((0,), (0,)), ((), ())), preferred_element_type=F32
        )

    pipelined(code_ref.shape[0] // block, fill, work)
    acc[...] = acc[...] * total ** (-0.5)
    half = own // 2
    for c in range(2):

        @pl.when(core == c)
        def _():
            mine_ref[...] = acc[:, c * half : (c + 1) * half].T
            other_ref[...] = acc[:, (1 - c) * half : (2 - c) * half].T


def proto_part(*refs, parts, scale):
    (code_ref, centre_ref, tok_ref, scale_ref, logit_ref), packs = refs[:5], refs[5 : 5 + parts]
    out_ref, tok, weight, *slots = refs[5 + parts :]
    tokens, own = code_ref.shape[1], tok_ref.shape[0]
    for i, pack in enumerate(packs):
        tok[i * own : (i + 1) * own, :] = pack[:own, :]
        pieces = pack[own:, :].astype(F32)
        count = own // 128
        lines = sum(pieces[j * count : (j + 1) * count, :] for j in range(SPLIT))
        for j in range(count):
            at = i * own + j * 128
            weight[:, at : at + 128] = lines[j : j + 1, :]

    def fill(i, slot):
        at = part(i, CHUNK)
        c = pl.ds(pl.multiple_of(own + i * CHUNK, 128), CHUNK)
        slots[slot][...] = logit(
            centre_ref[...], tok[at, :], code_ref[:, c], scale_ref[:, c], weight[:, at], scale
        )

    def work(i, slot):
        out_ref[...] += jnp.dot(slots[slot][...], tok[part(i, CHUNK), :], preferred_element_type=F32)

    out_ref[...] = jnp.dot(logit_ref[...], tok_ref[...], preferred_element_type=F32)
    pipelined(parts * own // CHUNK, fill, work)
    out_ref[...] = out_ref[...] * tokens ** (-0.5)


def swapped(x, axis, mask):
    return lax.ppermute(x, axis, [(i, i ^ mask) for i in range(lax.axis_size(axis))])


def others_of(x, axis):
    return [swapped(x, axis, m) for m in range(lax.axis_size(axis) - 1, 0, -1)]


def proto_terms(x):
    n = lax.axis_size("proto")
    x = x + swapped(x, "proto", 1)
    terms, unit = [x], 2
    while unit < n:
        group = min(4, n // unit)
        if unit > 2:
            terms = [sum(terms)]
        terms = [terms[0]] + [swapped(terms[0], "proto", unit * m) for m in range(group - 1, 0, -1)]
        unit *= group
    return terms


def chip_sum(x):
    n, unit = lax.axis_size("proto"), 2
    while unit < n:
        group = min(4, n // unit)
        x = sum([swapped(x, "proto", unit * m) for m in range(group - 1, 0, -1)], x)
        unit *= group
    return x


def local(first_view, alternate_augmentation, prototypes):
    own, d = first_view.shape
    k = prototypes.shape[0]
    tokens = own * lax.axis_size("dp")
    total = float(k * lax.axis_size("proto"))
    log2e = math.log2(math.e)
    code_scale = log2e / d / CODE_TEMP
    pred_scale = log2e / d / PRED_TEMP
    acc = pltpu.VMEM((8, tokens), F32)

    views = others_of(first_view, "dp")
    code, centres, columns = run(
        functools.partial(own_codes, scale=code_scale),
        [shape(k, tokens), shape(k, d, dtype=BF16), shape(k, 128)],
        [prototypes, first_view],
        [],
        keep=(0, 1, 2),
        us=3,
    )
    parts = len(views)
    code, sums = run(
        functools.partial(first_pass, parts=parts, scale=code_scale, total=total),
        [shape(1, tokens)],
        [code, centres, columns] + views,
        [pltpu.VMEM((tokens - own, d), BF16), acc, pltpu.VMEM((k, 128), F32)],
        resident=list(range(1, 3 + parts)),
        keep=[0],
        thread=True,
        us=7,
    )
    terms = proto_terms(sums)
    code, tok, den = run(
        functools.partial(denominators, scale=pred_scale),
        [shape(own, d, dtype=BF16), shape(1, own)],
        [code, centres, alternate_augmentation],
        [pltpu.VMEM((8, own), F32)],
        resident=[1],
        keep=[0, 1],
        thread=True,
        us=2,
    )
    code, sums = run(
        functools.partial(middle_pass, parts=len(terms), total=total),
        [shape(1, tokens + own)],
        [code] + terms + [den],
        [acc],
        resident=list(range(1, 2 + len(terms))),
        keep=[0],
        thread=True,
        us=5,
    )
    terms = proto_terms(sums)
    pack_rows = own + -(-SPLIT * own // 128 // TILE) * TILE
    code, sums, weight, pack = run(
        functools.partial(last_pass, parts=len(terms), total=total),
        [shape(1, tokens), shape(1, own), shape(pack_rows, d, dtype=BF16)],
        [code] + terms + [tok],
        [acc],
        resident=list(range(1, 2 + len(terms))),
        keep=[0, 1, 2],
        thread=True,
        us=5,
    )
    terms = proto_terms(sums)
    packs = others_of(pack, "dp")
    code, mine, other, token_scale, logits = run(
        functools.partial(token_part, parts=len(terms), scale=pred_scale, total=total),
        [shape(own // 2, d), shape(own // 2, d), shape(1, tokens), shape(k, own, dtype=BF16)],
        [code, centres, tok, weight] + terms,
        [pltpu.VMEM((d, own), F32)],
        resident=list(range(1, 4 + len(terms))),
        keep=[0, 1, 2, 3],
        thread=True,
        us=4,
    )
    mine = chip_sum(mine + swapped(other, "proto", 1))
    (proto_grad,) = run(
        functools.partial(proto_part, parts=parts, scale=pred_scale),
        [shape(k, d)],
        [code, centres, tok, token_scale, logits] + packs,
        [pltpu.VMEM((tokens - own, d), BF16), pltpu.VMEM((1, tokens - own), F32)]
        + [pltpu.VMEM((k, CHUNK), BF16)] * 2,
        resident=range(5 + parts),
        us=10,
    )
    mine, proto_grad = lax.optimization_barrier((mine, proto_grad))
    other = swapped(mine, "proto", 1)
    first = lax.rem(lax.axis_index("proto"), 2) == 0
    token_grad = jnp.where(
        first, jnp.concatenate([mine, other]), jnp.concatenate([other, mine])
    )
    return proto_grad, token_grad


def solution(mesh):
    return jax.shard_map(
        local,
        mesh=mesh,
        in_specs=(P("dp", None), P("dp", None), P("proto", None)),
        out_specs=(P("proto", None), P("dp", None)),
        check_vma=False,
    )
```

time: 87.5 us -> 76.4 us (0.87)
  Pallas kernels: 45.9 us -> 33.5 us
  waiting for transfers between devices: 12.5 us -> 15.8 us
  starting transfers between devices: 27.3 us -> 25.3 us
    pallas_call x9 -> x7, Pallas kernels: 45.9 us -> 33.5 us  [run(): pl.pallas_call(body, out_shape=tuple((pltpu.VMEM(s.shape, s.dtype) if i i...]
    ppermute x6 -> x0, starting transfers between devices: 9.03 us -> none  [shifted(): lax.ppermute(x, axis, [(i, (i + s) % n) for i in range(n)])]
    ppermute x17 -> x23, starting transfers between devices: 18.3 us -> 25.3 us  [swapped(): lax.ppermute(x, axis, [(i, i ^ mask) for i in range(lax.axis_size(axis))])]
    ppermute x17 -> x23, waiting for transfers between devices: 12.4 us -> 15.8 us  [swapped(): lax.ppermute(x, axis, [(i, i ^ mask) for i in range(lax.axis_size(axis))])]
  transfers between devices with their start and end apart: 23 -> 23, of which waited for: 8 -> 12; matrix products, arithmetic and copies ran while one was open for 0% -> 0% of each run, Pallas kernels for 37% -> 23%
where the time goes in v5:
time: 76.4 us; the launch traced here: 76.2 us
  Pallas kernels  33.5 us (44%)
  starting transfers between devices  25.3 us (33%)
  waiting for transfers between devices  15.8 us (21%)
  other arithmetic  0.82 us (1%)
  between operations  0.77 us (1%)
    pallas_call x7, Pallas kernels, run(): pl.pallas_call(body, out_shape=tuple((pltpu.VMEM(s.shape, s.dtype) if i i...  33.5 us
    ppermute x23, starting transfers between devices, swapped(): lax.ppermute(x, axis, [(i, i ^ mask) for i in range(lax.axis_size(axis))])  25.3 us
    ppermute x23, waiting for transfers between devices, swapped(): lax.ppermute(x, axis, [(i, i ^ mask) for i in range(lax.axis_size(axis))])  15.8 us
  transfers between devices with their start and end apart: 23, of which 12 were waited for; matrix products, arithmetic and copies ran while one was open for 0% of the time, Pallas kernels for 23%

profile of v5, /device:TPU:0, one launch (start us, length us, event | category | flops | bytes accessed | tf_op | source)
XLA Modules:
  0.0 76.2 jit_solution(3849594333059972155)
XLA Ops:
  0.6 4.0 %collective-permute-start = (bf16[512,128]{1,0:T(8,128)(2,1)}, bf16[512,128]{1,0:T(8,128)(2,1)S(1)}, u32[]{:S(2)}, u32[]{:S(2)}) collective-permute-start(bf16[512,128]{1,0:T(8,128)(2,1)} %token_ref.2), channel_id=1, source_target_pairs={{0,24},{8,16},{16,8},{24,0},{1,25},{9,17},{17,9},{25,1},{2,26},{10... | collective-permute-start | bytes 393224 | tf_op jit(solution)/shard_map/ppermute | solution.py:270
  5.2 3.2 %shard_map.50 = (f32[4096,2048]{1,0:T(8,128)S(1)}, bf16[4096,128]{1,0:T(8,128)(2,1)S(1)}, f32[4096,128]{1,0:T(8,128)S(1)}) custom-call(bf16[4096,128]{1,0:T(8,128)(2,1)} %proto_ref.1, bf16[512,128]{1,0:T(8,128)(2,1)} %token_ref.2), custom_call_target="tpu_custom_call" | custom-call | flops 3000000000 | bytes 1048576 | tf_op jit(solution)/shard_map/pallas_call | solution.py:35
  8.8 2.3 %collective-permute-done.1.refs_4_ = bf16[512,128]{1,0:T(8,128)(2,1)S(1)} collective-permute-done((bf16[512,128]{1,0:T(8,128)(2,1)}, bf16[512,128]{1,0:T(8,128)(2,1)S(1)}, u32[]{:S(2)}, u32[]{:S(2)}) %collective-permute-start.1) | collective-permute-done | bytes 131104 | tf_op jit(solution)/shard_map/ppermute | solution.py:270
  11.4 6.6 %shard_map.51 = (f32[4096,2048]{1,0:T(8,128)S(1)}, f32[1,2048]{1,0:T(1,128)S(1)}) custom-call(f32[4096,2048]{1,0:T(8,128)S(1)} %get-tuple-element.23.refs_0_, bf16[4096,128]{1,0:T(8,128)(2,1)S(1)} %get-tuple-element.24.refs_1_.centre_ref, f32[4096,128]{1,0:T(8,128)S(1)} %get-tuple-element.25.refs_2_, ...), custom_call_target="tpu_custom_call", output_to_operand_aliasing={{0}: (0, {})} | custom-call | flops 7000000000 | bytes 1048576 | tf_op jit(solution)/shard_map/pallas_call | solution.py:35
  18.1 1.2 %collective-permute-done.3 = f32[1,2048]{1,0:T(1,128)S(1)} collective-permute-done((f32[1,2048]{1,0:T(1,128)S(1)}, f32[1,2048]{1,0:T(1,128)S(1)}, u32[]{:S(2)}, u32[]{:S(2)}) %collective-permute-start.3) | collective-permute-done | bytes 8224 | tf_op jit(solution)/shard_map/ppermute | solution.py:270
  19.2 3.7 %collective-permute-start.4 = (f32[1,2048]{1,0:T(1,128)S(1)}, f32[1,2048]{1,0:T(1,128)S(1)}, u32[]{:S(2)}, u32[]{:S(2)}) collective-permute-start(f32[1,2048]{1,0:T(1,128)S(1)} %add.21.refs_1_), channel_id=1, source_target_pairs={{0,6},{1,7},{2,4},{3,5},{4,2},{5,3},{6,0},{7,1},{8,14},{9,15},{10,... | collective-permute-start | bytes 24584 | tf_op jit(solution)/shard_map/ppermute | solution.py:270
  23.7 1.6 %shard_map.52 = (f32[4096,2048]{1,0:T(8,128)S(1)}, bf16[512,128]{1,0:T(8,128)(2,1)S(1)}, f32[1,512]{1,0:T(1,128)S(1)}) custom-call(f32[4096,2048]{1,0:T(8,128)S(1)} %get-tuple-element.26._, bf16[4096,128]{1,0:T(8,128)(2,1)S(1)} %get-tuple-element.24.refs_1_.centre_ref, bf16[512,128]{1,0:T(8,128)(2,1)S(1)} %copy-done), custom_call_target="tpu_custom_call", output_to_operand_aliasing={{0}: (0, {})} | custom-call | flops 2000000000 | bytes 1048576 | tf_op jit(solution)/shard_map/pallas_call | solution.py:35
  25.3 2.1 %collective-permute-done.5.refs_3_ = f32[1,2048]{1,0:T(1,128)S(1)} collective-permute-done((f32[1,2048]{1,0:T(1,128)S(1)}, f32[1,2048]{1,0:T(1,128)S(1)}, u32[]{:S(2)}, u32[]{:S(2)}) %collective-permute-start.5) | collective-permute-done | bytes 8224 | tf_op jit(solution)/shard_map/ppermute | solution.py:270
  27.4 4.5 %shard_map.53 = (f32[4096,2048]{1,0:T(8,128)S(1)}, f32[1,2560]{1,0:T(1,128)S(1)}) custom-call(f32[4096,2048]{1,0:T(8,128)S(1)} %get-tuple-element.27.refs_0_, f32[1,2048]{1,0:T(1,128)S(1)} %add.21.refs_1_, f32[1,2048]{1,0:T(1,128)S(1)} %collective-permute-done.4.refs_2_, ...), custom_call_target="tpu_custom_call", output_to_operand_aliasing={{0}: (0, {})} | custom-call | flops 5000000000 | bytes 1048576 | tf_op jit(solution)/shard_map/pallas_call | solution.py:35
  32.0 1.2 %collective-permute-done.7 = f32[1,2560]{1,0:T(1,128)S(1)} collective-permute-done((f32[1,2560]{1,0:T(1,128)S(1)}, f32[1,2560]{1,0:T(1,128)S(1)}, u32[]{:S(2)}, u32[]{:S(2)}) %collective-permute-start.7) | collective-permute-done | bytes 10272 | tf_op jit(solution)/shard_map/ppermute | solution.py:270
  33.3 3.5 %collective-permute-start.8 = (f32[1,2560]{1,0:T(1,128)S(1)}, f32[1,2560]{1,0:T(1,128)S(1)}, u32[]{:S(2)}, u32[]{:S(2)}) collective-permute-start(f32[1,2560]{1,0:T(1,128)S(1)} %add.22.refs_1_), channel_id=1, source_target_pairs={{0,6},{1,7},{2,4},{3,5},{4,2},{5,3},{6,0},{7,1},{8,14},{9,15},{10,... | collective-permute-start | bytes 30728 | tf_op jit(solution)/shard_map/ppermute | solution.py:270
  36.9 1.9 %collective-permute-done.8.refs_2_ = f32[1,2560]{1,0:T(1,128)S(1)} collective-permute-done((f32[1,2560]{1,0:T(1,128)S(1)}, f32[1,2560]{1,0:T(1,128)S(1)}, u32[]{:S(2)}, u32[]{:S(2)}) %collective-permute-start.8) | collective-permute-done | bytes 10272 | tf_op jit(solution)/shard_map/ppermute | solution.py:270
  38.9 2.4 %collective-permute-done.9.refs_3_ = f32[1,2560]{1,0:T(1,128)S(1)} collective-permute-done((f32[1,2560]{1,0:T(1,128)S(1)}, f32[1,2560]{1,0:T(1,128)S(1)}, u32[]{:S(2)}, u32[]{:S(2)}) %collective-permute-start.9) | collective-permute-done | bytes 10272 | tf_op jit(solution)/shard_map/ppermute | solution.py:270
  41.3 5.1 %shard_map.54 = (f32[4096,2048]{1,0:T(8,128)S(1)}, f32[1,2048]{1,0:T(1,128)S(1)}, f32[1,512]{1,0:T(1,128)S(1)}, bf16[528,128]{1,0:T(8,128)(2,1)S(1)}) custom-call(f32[4096,2048]{1,0:T(8,128)S(1)} %get-tuple-element.30.refs_0_, f32[1,2560]{1,0:T(1,128)S(1)} %add.22.refs_1_, ...), custom_call_target="tpu_custom_call", output_to_operand_aliasing={{0}: (0, {})} | custom-call | flops 5000000000 | bytes 1048576 | tf_op jit(solution)/shard_map/pallas_call | solution.py:35
  46.5 1.2 %collective-permute-done.11 = f32[1,2048]{1,0:T(1,128)S(1)} collective-permute-done((f32[1,2048]{1,0:T(1,128)S(1)}, f32[1,2048]{1,0:T(1,128)S(1)}, u32[]{:S(2)}, u32[]{:S(2)}) %collective-permute-start.11) | collective-permute-done | bytes 8224 | tf_op jit(solution)/shard_map/ppermute | solution.py:270
  47.7 1.0 %collective-permute-start.12 = (f32[1,2048]{1,0:T(1,128)S(1)}, f32[1,2048]{1,0:T(1,128)S(1)}, u32[]{:S(2)}, u32[]{:S(2)}) collective-permute-start(f32[1,2048]{1,0:T(1,128)S(1)} %add.23.refs_4_), channel_id=1, source_target_pairs={{0,6},{1,7},{2,4},{3,5},{4,2},{5,3},{6,0},{7,1},{8,14},{9,15},{10,... | collective-permute-start | bytes 24584 | tf_op jit(solution)/shard_map/ppermute | solution.py:270
  48.7 3.5 %collective-permute-start.14 = (f32[1,2048]{1,0:T(1,128)S(1)}, f32[1,2048]{1,0:T(1,128)S(1)}, u32[]{:S(2)}, u32[]{:S(2)}) collective-permute-start(f32[1,2048]{1,0:T(1,128)S(1)} %add.23.refs_4_), channel_id=1, source_target_pairs={{0,2},{1,3},{2,0},{3,1},{4,6},{5,7},{6,4},{7,5},{8,10},{9,11},{10,... | collective-permute-start | bytes 24584 | tf_op jit(solution)/shard_map/ppermute | solution.py:270
  52.2 1.7 %collective-permute-start.19 = (bf16[528,128]{1,0:T(8,128)(2,1)S(1)}, bf16[528,128]{1,0:T(8,128)(2,1)S(1)}, u32[]{:S(2)}, u32[]{:S(2)}) collective-permute-start(bf16[528,128]{1,0:T(8,128)(2,1)S(1)} %get-tuple-element.41), channel_id=1, source_target_pairs={{0,24},{8,16},{16,8},{24,0},{1,25},{9,17},{17,9},{25,1},{2,26},{10... | collective-permute-start | bytes 405512 | tf_op jit(solution)/shard_map/ppermute | solution.py:270
  53.9 1.3 %collective-permute-start.20 = (bf16[528,128]{1,0:T(8,128)(2,1)S(1)}, bf16[528,128]{1,0:T(8,128)(2,1)S(1)}, u32[]{:S(2)}, u32[]{:S(2)}) collective-permute-start(bf16[528,128]{1,0:T(8,128)(2,1)S(1)} %get-tuple-element.41), channel_id=1, source_target_pairs={{0,16},{8,24},{16,0},{24,8},{1,17},{9,25},{17,1},{25,9},{2,18},{10... | collective-permute-start | bytes 405512 | tf_op jit(solution)/shard_map/ppermute | solution.py:270
  55.7 2.5 %shard_map.55 = (f32[4096,2048]{1,0:T(8,128)S(1)}, f32[256,128]{1,0:T(8,128)S(1)}, f32[256,128]{1,0:T(8,128)S(1)}, f32[1,2048]{1,0:T(1,128)S(1)}, bf16[4096,512]{1,0:T(8,128)(2,1)S(1)}) custom-call(f32[4096,2048]{1,0:T(8,128)S(1)} %get-tuple-element.33.refs_0_, ...), custom_call_target="tpu_custom_call", output_to_operand_aliasing={{0}: (0, {})} | custom-call | flops 4000000000 | bytes 1048576 | tf_op jit(solution)/shard_map/pallas_call | solution.py:35
  58.2 1.3 %collective-permute-done.15 = f32[256,128]{1,0:T(8,128)S(1)} collective-permute-done((f32[256,128]{1,0:T(8,128)S(1)}, f32[256,128]{1,0:T(8,128)S(1)}, u32[]{:S(2)}, u32[]{:S(2)}) %collective-permute-start.15) | collective-permute-done | bytes 131104 | tf_op jit(solution)/shard_map/ppermute | solution.py:270
  61.3 2.8 %collective-permute-start.18 = (f32[256,128]{1,0:T(8,128)S(1)}, f32[256,128]{1,0:T(8,128)S(1)}, u32[]{:S(2)}, u32[]{:S(2)}) collective-permute-start(f32[256,128]{1,0:T(8,128)S(1)} %add.24), channel_id=1, source_target_pairs={{0,2},{1,3},{2,0},{3,1},{4,6},{5,7},{6,4},{7,5},{8,10},{9,11},{10,... | collective-permute-start | bytes 393224 | tf_op jit(solution)/shard_map/ppermute | solution.py:270
  64.0 10.0 %shard_map.56 = f32[4096,128]{1,0:T(8,128)} custom-call(f32[4096,2048]{1,0:T(8,128)S(1)} %get-tuple-element.38.refs_0_, bf16[4096,128]{1,0:T(8,128)(2,1)S(1)} %get-tuple-element.24.refs_1_.centre_ref, bf16[512,128]{1,0:T(8,128)(2,1)S(1)} %get-tuple-element.32.refs_5_.refs_2_, f32[1,2048]{1,0:T(1,128)S(1)} %get-tuple-element.39.refs_3_, ...), custom_call_target="tpu_custom_call" | custom-call | flops 10000000000 | bytes 1048576 | tf_op jit(solution)/shard_map/pallas_call | solution.py:35
  74.2 1.3 %collective-permute-done.22 = f32[256,128]{1,0:T(8,128)S(1)} collective-permute-done((f32[256,128]{1,0:T(8,128)S(1)}, f32[256,128]{1,0:T(8,128)S(1)}, u32[]{:S(2)}, u32[]{:S(2)}) %collective-permute-start.22) | collective-permute-done | bytes 131104 | tf_op jit(solution)/shard_map/ppermute | solution.py:270
  (37 shorter events, 5.7 us)
Async XLA Ops:
  0.6 23.1 %copy-start = (bf16[512,128]{1,0:T(8,128)(2,1)S(1)}, bf16[512,128]{1,0:T(8,128)(2,1)}, u32[]{:S(2)}) copy-start(bf16[512,128]{1,0:T(8,128)(2,1)} %token_ref.3) | copy-start | bytes 393220
  0.6 8.2 %collective-permute-start = (bf16[512,128]{1,0:T(8,128)(2,1)}, bf16[512,128]{1,0:T(8,128)(2,1)S(1)}, u32[]{:S(2)}, u32[]{:S(2)}) collective-permute-start(bf16[512,128]{1,0:T(8,128)(2,1)} %token_ref.2), channel_id=1, source_target_pairs={{0,24},{8,16},{16,8},{24,0},{1,25},{9,17},{17,9},{25,1},{2,26},{10... | collective-permute-start | bytes 393224 | tf_op jit(solution)/shard_map/ppermute | solution.py:270
  4.6 6.5 %collective-permute-start.1 = (bf16[512,128]{1,0:T(8,128)(2,1)}, bf16[512,128]{1,0:T(8,128)(2,1)S(1)}, u32[]{:S(2)}, u32[]{:S(2)}) collective-permute-start(bf16[512,128]{1,0:T(8,128)(2,1)} %token_ref.2), channel_id=1, source_target_pairs={{0,16},{8,24},{16,0},{24,8},{1,17},{9,25},{17,1},{25,9},{2,18},{10... | collective-permute-start | bytes 393224 | tf_op jit(solution)/shard_map/ppermute | solution.py:270
  5.1 6.3 %collective-permute-start.2 = (bf16[512,128]{1,0:T(8,128)(2,1)}, bf16[512,128]{1,0:T(8,128)(2,1)S(1)}, u32[]{:S(2)}, u32[]{:S(2)}) collective-permute-start(bf16[512,128]{1,0:T(8,128)(2,1)} %token_ref.2), channel_id=1, source_target_pairs={{0,8},{8,0},{16,24},{24,16},{1,9},{9,1},{17,25},{25,17},{2,10},{10... | collective-permute-start | bytes 393224 | tf_op jit(solution)/shard_map/ppermute | solution.py:270
  18.0 1.2 %collective-permute-start.3 = (f32[1,2048]{1,0:T(1,128)S(1)}, f32[1,2048]{1,0:T(1,128)S(1)}, u32[]{:S(2)}, u32[]{:S(2)}) collective-permute-start(f32[1,2048]{1,0:T(1,128)S(1)} %get-tuple-element.28), channel_id=1, source_target_pairs={{0,1},{1,0},{2,3},{3,2},{4,5},{5,4},{6,7},{7,6},{8,9},{9,8},{10,11... | collective-permute-start | bytes 24584 | tf_op jit(solution)/shard_map/ppermute | solution.py:270
  19.2 6.0 %collective-permute-start.4 = (f32[1,2048]{1,0:T(1,128)S(1)}, f32[1,2048]{1,0:T(1,128)S(1)}, u32[]{:S(2)}, u32[]{:S(2)}) collective-permute-start(f32[1,2048]{1,0:T(1,128)S(1)} %add.21.refs_1_), channel_id=1, source_target_pairs={{0,6},{1,7},{2,4},{3,5},{4,2},{5,3},{6,0},{7,1},{8,14},{9,15},{10,... | collective-permute-start | bytes 24584 | tf_op jit(solution)/shard_map/ppermute | solution.py:270
  22.9 4.5 %collective-permute-start.5 = (f32[1,2048]{1,0:T(1,128)S(1)}, f32[1,2048]{1,0:T(1,128)S(1)}, u32[]{:S(2)}, u32[]{:S(2)}) collective-permute-start(f32[1,2048]{1,0:T(1,128)S(1)} %add.21.refs_1_), channel_id=1, source_target_pairs={{0,4},{1,5},{2,6},{3,7},{4,0},{5,1},{6,2},{7,3},{8,12},{9,13},{10,... | collective-permute-start | bytes 24584 | tf_op jit(solution)/shard_map/ppermute | solution.py:270
  22.9 4.5 %collective-permute-start.6 = (f32[1,2048]{1,0:T(1,128)S(1)}, f32[1,2048]{1,0:T(1,128)S(1)}, u32[]{:S(2)}, u32[]{:S(2)}) collective-permute-start(f32[1,2048]{1,0:T(1,128)S(1)} %add.21.refs_1_), channel_id=1, source_target_pairs={{0,2},{1,3},{2,0},{3,1},{4,6},{5,7},{6,4},{7,5},{8,10},{9,11},{10,... | collective-permute-start | bytes 24584 | tf_op jit(solution)/shard_map/ppermute | solution.py:270
  32.0 1.2 %collective-permute-start.7 = (f32[1,2560]{1,0:T(1,128)S(1)}, f32[1,2560]{1,0:T(1,128)S(1)}, u32[]{:S(2)}, u32[]{:S(2)}) collective-permute-start(f32[1,2560]{1,0:T(1,128)S(1)} %get-tuple-element.31), channel_id=1, source_target_pairs={{0,1},{1,0},{2,3},{3,2},{4,5},{5,4},{6,7},{7,6},{8,9},{9,8},{10,11... | collective-permute-start | bytes 30728 | tf_op jit(solution)/shard_map/ppermute | solution.py:270
  33.2 3.7 %collective-permute-start.10 = (f32[1,2560]{1,0:T(1,128)S(1)}, f32[1,2560]{1,0:T(1,128)S(1)}, u32[]{:S(2)}, u32[]{:S(2)}) collective-permute-start(f32[1,2560]{1,0:T(1,128)S(1)} %add.22.refs_1_), channel_id=1, source_target_pairs={{0,2},{1,3},{2,0},{3,1},{4,6},{5,7},{6,4},{7,5},{8,10},{9,11},{10,... | collective-permute-start | bytes 30728 | tf_op jit(solution)/shard_map/ppermute | solution.py:270
  33.3 5.6 %collective-permute-start.8 = (f32[1,2560]{1,0:T(1,128)S(1)}, f32[1,2560]{1,0:T(1,128)S(1)}, u32[]{:S(2)}, u32[]{:S(2)}) collective-permute-start(f32[1,2560]{1,0:T(1,128)S(1)} %add.22.refs_1_), channel_id=1, source_target_pairs={{0,6},{1,7},{2,4},{3,5},{4,2},{5,3},{6,0},{7,1},{8,14},{9,15},{10,... | collective-permute-start | bytes 30728 | tf_op jit(solution)/shard_map/ppermute | solution.py:270
  36.8 4.6 %collective-permute-start.9 = (f32[1,2560]{1,0:T(1,128)S(1)}, f32[1,2560]{1,0:T(1,128)S(1)}, u32[]{:S(2)}, u32[]{:S(2)}) collective-permute-start(f32[1,2560]{1,0:T(1,128)S(1)} %add.22.refs_1_), channel_id=1, source_target_pairs={{0,4},{1,5},{2,6},{3,7},{4,0},{5,1},{6,2},{7,3},{8,12},{9,13},{10,... | collective-permute-start | bytes 30728 | tf_op jit(solution)/shard_map/ppermute | solution.py:270
  46.5 1.2 %collective-permute-start.11 = (f32[1,2048]{1,0:T(1,128)S(1)}, f32[1,2048]{1,0:T(1,128)S(1)}, u32[]{:S(2)}, u32[]{:S(2)}) collective-permute-start(f32[1,2048]{1,0:T(1,128)S(1)} %get-tuple-element.35), channel_id=1, source_target_pairs={{0,1},{1,0},{2,3},{3,2},{4,5},{5,4},{6,7},{7,6},{8,9},{9,8},{10,11... | collective-permute-start | bytes 24584 | tf_op jit(solution)/shard_map/ppermute | solution.py:270
  47.7 7.5 %collective-permute-start.12 = (f32[1,2048]{1,0:T(1,128)S(1)}, f32[1,2048]{1,0:T(1,128)S(1)}, u32[]{:S(2)}, u32[]{:S(2)}) collective-permute-start(f32[1,2048]{1,0:T(1,128)S(1)} %add.23.refs_4_), channel_id=1, source_target_pairs={{0,6},{1,7},{2,4},{3,5},{4,2},{5,3},{6,0},{7,1},{8,14},{9,15},{10,... | collective-permute-start | bytes 24584 | tf_op jit(solution)/shard_map/ppermute | solution.py:270
  48.7 7.0 %collective-permute-start.13 = (f32[1,2048]{1,0:T(1,128)S(1)}, f32[1,2048]{1,0:T(1,128)S(1)}, u32[]{:S(2)}, u32[]{:S(2)}) collective-permute-start(f32[1,2048]{1,0:T(1,128)S(1)} %add.23.refs_4_), channel_id=1, source_target_pairs={{0,4},{1,5},{2,6},{3,7},{4,0},{5,1},{6,2},{7,3},{8,12},{9,13},{10,... | collective-permute-start | bytes 24584 | tf_op jit(solution)/shard_map/ppermute | solution.py:270
  48.7 7.0 %collective-permute-start.14 = (f32[1,2048]{1,0:T(1,128)S(1)}, f32[1,2048]{1,0:T(1,128)S(1)}, u32[]{:S(2)}, u32[]{:S(2)}) collective-permute-start(f32[1,2048]{1,0:T(1,128)S(1)} %add.23.refs_4_), channel_id=1, source_target_pairs={{0,2},{1,3},{2,0},{3,1},{4,6},{5,7},{6,4},{7,5},{8,10},{9,11},{10,... | collective-permute-start | bytes 24584 | tf_op jit(solution)/shard_map/ppermute | solution.py:270
  52.2 9.1 %collective-permute-start.19 = (bf16[528,128]{1,0:T(8,128)(2,1)S(1)}, bf16[528,128]{1,0:T(8,128)(2,1)S(1)}, u32[]{:S(2)}, u32[]{:S(2)}) collective-permute-start(bf16[528,128]{1,0:T(8,128)(2,1)S(1)} %get-tuple-element.41), channel_id=1, source_target_pairs={{0,24},{8,16},{16,8},{24,0},{1,25},{9,17},{17,9},{25,1},{2,26},{10... | collective-permute-start | bytes 405512 | tf_op jit(solution)/shard_map/ppermute | solution.py:270
  53.9 10.2 %collective-permute-start.20 = (bf16[528,128]{1,0:T(8,128)(2,1)S(1)}, bf16[528,128]{1,0:T(8,128)(2,1)S(1)}, u32[]{:S(2)}, u32[]{:S(2)}) collective-permute-start(bf16[528,128]{1,0:T(8,128)(2,1)S(1)} %get-tuple-element.41), channel_id=1, source_target_pairs={{0,16},{8,24},{16,0},{24,8},{1,17},{9,25},{17,1},{25,9},{2,18},{10... | collective-permute-start | bytes 405512 | tf_op jit(solution)/shard_map/ppermute | solution.py:270
  55.2 8.9 %collective-permute-start.21 = (bf16[528,128]{1,0:T(8,128)(2,1)S(1)}, bf16[528,128]{1,0:T(8,128)(2,1)S(1)}, u32[]{:S(2)}, u32[]{:S(2)}) collective-permute-start(bf16[528,128]{1,0:T(8,128)(2,1)S(1)} %get-tuple-element.41), channel_id=1, source_target_pairs={{0,8},{8,0},{16,24},{24,16},{1,9},{9,1},{17,25},{25,17},{2,10},{10... | collective-permute-start | bytes 405512 | tf_op jit(solution)/shard_map/ppermute | solution.py:270
  58.1 1.4 %collective-permute-start.15 = (f32[256,128]{1,0:T(8,128)S(1)}, f32[256,128]{1,0:T(8,128)S(1)}, u32[]{:S(2)}, u32[]{:S(2)}) collective-permute-start(f32[256,128]{1,0:T(8,128)S(1)} %get-tuple-element.37), channel_id=1, source_target_pairs={{0,1},{1,0},{2,3},{3,2},{4,5},{5,4},{6,7},{7,6},{8,9},{9,8},{10,11... | collective-permute-start | bytes 393224 | tf_op jit(solution)/shard_map/ppermute | solution.py:270
  59.6 14.5 %collective-permute-start.16 = (f32[256,128]{1,0:T(8,128)S(1)}, f32[256,128]{1,0:T(8,128)S(1)}, u32[]{:S(2)}, u32[]{:S(2)}) collective-permute-start(f32[256,128]{1,0:T(8,128)S(1)} %add.24), channel_id=1, source_target_pairs={{0,6},{1,7},{2,4},{3,5},{4,2},{5,3},{6,0},{7,1},{8,14},{9,15},{10,... | collective-permute-start | bytes 393224 | tf_op jit(solution)/shard_map/ppermute | solution.py:270
  60.6 13.5 %collective-permute-start.17 = (f32[256,128]{1,0:T(8,128)S(1)}, f32[256,128]{1,0:T(8,128)S(1)}, u32[]{:S(2)}, u32[]{:S(2)}) collective-permute-start(f32[256,128]{1,0:T(8,128)S(1)} %add.24), channel_id=1, source_target_pairs={{0,4},{1,5},{2,6},{3,7},{4,0},{5,1},{6,2},{7,3},{8,12},{9,13},{10,... | collective-permute-start | bytes 393224 | tf_op jit(solution)/shard_map/ppermute | solution.py:270
  61.3 12.8 %collective-permute-start.18 = (f32[256,128]{1,0:T(8,128)S(1)}, f32[256,128]{1,0:T(8,128)S(1)}, u32[]{:S(2)}, u32[]{:S(2)}) collective-permute-start(f32[256,128]{1,0:T(8,128)S(1)} %add.24), channel_id=1, source_target_pairs={{0,2},{1,3},{2,0},{3,1},{4,6},{5,7},{6,4},{7,5},{8,10},{9,11},{10,... | collective-permute-start | bytes 393224 | tf_op jit(solution)/shard_map/ppermute | solution.py:270
  74.1 1.4 %collective-permute-start.22 = (f32[256,128]{1,0:T(8,128)S(1)}, f32[256,128]{1,0:T(8,128)S(1)}, u32[]{:S(2)}, u32[]{:S(2)}) collective-permute-start(f32[256,128]{1,0:T(8,128)S(1)} %add_add_fusion), channel_id=1, source_target_pairs={{0,1},{1,0},{2,3},{3,2},{4,5},{5,4},{6,7},{7,6},{8,9},{9,8},{10,11... | collective-permute-start | bytes 393224 | tf_op jit(solution)/shard_map/ppermute | solution.py:270

commit v6 on v5

--- a/solution.py
+++ b/solution.py
@@ -15,6 +15,7 @@
 VMEM_LIMIT = 20 << 20
 CHUNK = 256
 BLOCKS = {"own": 2048, "first": 1024, "den": 2048, "middle": 512, "token": 2048}
+SUBS = {"first": 1, "proto": 1}
 SPLIT = 3
 TILE = 16
 
@@ -69,19 +70,27 @@
     return min(BLOCKS[name], size // 2)
 
 
-def pipelined(n, fill, work):
+def pipelined(n, fill, work, subs=1):
+    def both(i, slot):
+        for m in range(subs):
+            fill(i, slot, m)
+            work(i - 1, 1 - slot, m)
+
     def body(i, carry):
-        fill(2 * i + 1, 1)
-        work(2 * i, 0)
-        fill(2 * i + 2, 0)
-        work(2 * i + 1, 1)
+        both(2 * i + 1, 1)
+        both(2 * i + 2, 0)
         return carry
 
-    fill(0, 0)
-    lax.fori_loop(0, n // 2 - 1, body, 0)
-    fill(n - 1, 1)
-    work(n - 2, 0)
-    work(n - 1, 1)
+    for m in range(subs):
+        fill(0, 0, m)
+    if n <= 4:
+        for i in range(1, n - 1):
+            both(i, i % 2)
+    else:
+        lax.fori_loop(0, n // 2 - 1, body, 0)
+    both(n - 1, 1)
+    for m in range(subs):
+        work(n - 1, 1, m)
 
 
 def part(i, size):
@@ -123,18 +132,24 @@
     acc[...] = jnp.zeros_like(acc)
     block = block_of("first", centre_ref.shape[0])
 
-    def fill(i, slot):
-        at = part(i, block)
+    size = block // SUBS["first"]
+
+    def rows(i, m):
+        start = i * block + m * size
+        return pl.ds(start if isinstance(i, int) else pl.multiple_of(start, size), size)
+
+    def fill(i, slot, m):
+        at = rows(i, m)
         code = jnp.exp2(similarity(centre_ref[at, :], tok[...]) * scale)
         code_ref[at, n:] = code
         columns[at, :] = column_ref[at, :] + lane_sums(code)
 
-    def work(i, slot):
-        at = part(i, block)
+    def work(i, slot, m):
+        at = rows(i, m)
         factor = 1.0 / (total * jnp.sum(columns[at, :], axis=1, keepdims=True))
         acc[...] += sublane_sums(code_ref[at, :] * factor)
 
-    pipelined(centre_ref.shape[0] // block, fill, work)
+    pipelined(centre_ref.shape[0] // block, fill, work, SUBS["first"])
     out_ref[...] = jnp.sum(acc[...], axis=0, keepdims=True)
 
 
@@ -213,7 +228,7 @@
     acc[...] = jnp.zeros_like(acc)
     block = block_of("token", code_ref.shape[0])
 
-    def fill(i, slot):
+    def fill(i, slot, m):
         at = part(i, block)
         for c in range(0, own, CHUNK):
             c = slice(c, min(c + CHUNK, own))
@@ -221,7 +236,7 @@
                 centre_ref[at, :], tok_ref[c, :], code_ref[at, c], scale_ref[:, c], weight_ref[:, c], scale
             )
 
-    def work(i, slot):
+    def work(i, slot, m):
         at = part(i, block)
         acc[...] += lax.dot_general(
             centre_ref[at, :], logit_ref[at, :], (((0,), (0,)), ((), ())), preferred_element_type=F32
@@ -251,18 +266,23 @@
             at = i * own + j * 128
             weight[:, at : at + 128] = lines[j : j + 1, :]
 
-    def fill(i, slot):
+    subs = SUBS["proto"]
+    size = code_ref.shape[0] // subs
+
+    def fill(i, slot, m):
         at = part(i, CHUNK)
         c = pl.ds(pl.multiple_of(own + i * CHUNK, 128), CHUNK)
-        slots[slot][...] = logit(
-            centre_ref[...], tok[at, :], code_ref[:, c], scale_ref[:, c], weight[:, at], scale
+        r = slice(m * size, (m + 1) * size)
+        slots[slot][r, :] = logit(
+            centre_ref[r, :], tok[at, :], code_ref[r, c], scale_ref[:, c], weight[:, at], scale
         )
 
-    def work(i, slot):
-        out_ref[...] += jnp.dot(slots[slot][...], tok[part(i, CHUNK), :], preferred_element_type=F32)
+    def work(i, slot, m):
+        r = slice(m * size, (m + 1) * size)
+        out_ref[r, :] += jnp.dot(slots[slot][r, :], tok[part(i, CHUNK), :], preferred_element_type=F32)
 
     out_ref[...] = jnp.dot(logit_ref[...], tok_ref[...], preferred_element_type=F32)
-    pipelined(parts * own // CHUNK, fill, work)
+    pipelined(parts * own // CHUNK, fill, work, subs)
     out_ref[...] = out_ref[...] * tokens ** (-0.5)
 
 
@@ -348,6 +368,7 @@
         us=5,
     )
     terms = proto_terms(sums)
+    terms = terms[:1] + terms[2:] + terms[1:2]
     pack_rows = own + -(-SPLIT * own // 128 // TILE) * TILE
     code, sums, weight, pack = run(
         functools.partial(last_pass, parts=len(terms), total=total),

time: 76.4 us -> 74.5 us (0.975)
  waiting for transfers between devices: 15.8 us -> 13 us
  starting transfers between devices: 25.3 us -> 26.3 us
    ppermute x23, waiting for transfers between devices: 15.8 us -> 13 us  [swapped(): lax.ppermute(x, axis, [(i, i ^ mask) for i in range(lax.axis_size(axis))])]
    ppermute x23, starting transfers between devices: 25.3 us -> 26.3 us  [swapped(): lax.ppermute(x, axis, [(i, i ^ mask) for i in range(lax.axis_size(axis))])]
where the time goes in v6:
time: 74.5 us; the launch traced here: 74.4 us
  Pallas kernels  33.5 us (45%)
  starting transfers between devices  26.3 us (35%)
  waiting for transfers between devices  13 us (17%)
  other arithmetic  0.82 us (1%)
  between operations  0.76 us (1%)
    pallas_call x7, Pallas kernels, run(): pl.pallas_call(body, out_shape=tuple((pltpu.VMEM(s.shape, s.dtype) if i i...  33.5 us
    ppermute x23, starting transfers between devices, swapped(): lax.ppermute(x, axis, [(i, i ^ mask) for i in range(lax.axis_size(axis))])  26.3 us
    ppermute x23, waiting for transfers between devices, swapped(): lax.ppermute(x, axis, [(i, i ^ mask) for i in range(lax.axis_size(axis))])  13 us
  transfers between devices with their start and end apart: 23, of which 12 were waited for; matrix products, arithmetic and copies ran while one was open for 0% of the time, Pallas kernels for 23%

profile of v6, /device:TPU:0, one launch (start us, length us, event | category | flops | bytes accessed | tf_op | source)
XLA Modules:
  0.0 74.4 jit_solution(16154386421271487520)
XLA Ops:
  0.6 4.0 %collective-permute-start = (bf16[512,128]{1,0:T(8,128)(2,1)}, bf16[512,128]{1,0:T(8,128)(2,1)S(1)}, u32[]{:S(2)}, u32[]{:S(2)}) collective-permute-start(bf16[512,128]{1,0:T(8,128)(2,1)} %token_ref.2), channel_id=1, source_target_pairs={{0,24},{8,16},{16,8},{24,0},{1,25},{9,17},{17,9},{25,1},{2,26},{10... | collective-permute-start | bytes 393224 | tf_op jit(solution)/shard_map/ppermute | solution.py:290
  5.2 3.2 %shard_map.50 = (f32[4096,2048]{1,0:T(8,128)S(1)}, bf16[4096,128]{1,0:T(8,128)(2,1)S(1)}, f32[4096,128]{1,0:T(8,128)S(1)}) custom-call(bf16[4096,128]{1,0:T(8,128)(2,1)} %proto_ref.1, bf16[512,128]{1,0:T(8,128)(2,1)} %token_ref.2), custom_call_target="tpu_custom_call" | custom-call | flops 3000000000 | bytes 1048576 | tf_op jit(solution)/shard_map/pallas_call | solution.py:36
  8.8 2.3 %collective-permute-done.1.refs_4_ = bf16[512,128]{1,0:T(8,128)(2,1)S(1)} collective-permute-done((bf16[512,128]{1,0:T(8,128)(2,1)}, bf16[512,128]{1,0:T(8,128)(2,1)S(1)}, u32[]{:S(2)}, u32[]{:S(2)}) %collective-permute-start.1) | collective-permute-done | bytes 131104 | tf_op jit(solution)/shard_map/ppermute | solution.py:290
  11.4 6.6 %shard_map.51 = (f32[4096,2048]{1,0:T(8,128)S(1)}, f32[1,2048]{1,0:T(1,128)S(1)}) custom-call(f32[4096,2048]{1,0:T(8,128)S(1)} %get-tuple-element.23.refs_0_, bf16[4096,128]{1,0:T(8,128)(2,1)S(1)} %get-tuple-element.24.refs_1_.centre_ref, f32[4096,128]{1,0:T(8,128)S(1)} %get-tuple-element.25.refs_2_, ...), custom_call_target="tpu_custom_call", output_to_operand_aliasing={{0}: (0, {})} | custom-call | flops 7000000000 | bytes 1048576 | tf_op jit(solution)/shard_map/pallas_call | solution.py:36
  18.1 1.2 %collective-permute-done.3 = f32[1,2048]{1,0:T(1,128)S(1)} collective-permute-done((f32[1,2048]{1,0:T(1,128)S(1)}, f32[1,2048]{1,0:T(1,128)S(1)}, u32[]{:S(2)}, u32[]{:S(2)}) %collective-permute-start.3) | collective-permute-done | bytes 8224 | tf_op jit(solution)/shard_map/ppermute | solution.py:290
  19.2 3.7 %collective-permute-start.4 = (f32[1,2048]{1,0:T(1,128)S(1)}, f32[1,2048]{1,0:T(1,128)S(1)}, u32[]{:S(2)}, u32[]{:S(2)}) collective-permute-start(f32[1,2048]{1,0:T(1,128)S(1)} %add.21.refs_1_), channel_id=1, source_target_pairs={{0,6},{1,7},{2,4},{3,5},{4,2},{5,3},{6,0},{7,1},{8,14},{9,15},{10,... | collective-permute-start | bytes 24584 | tf_op jit(solution)/shard_map/ppermute | solution.py:290
  23.7 1.6 %shard_map.52 = (f32[4096,2048]{1,0:T(8,128)S(1)}, bf16[512,128]{1,0:T(8,128)(2,1)S(1)}, f32[1,512]{1,0:T(1,128)S(1)}) custom-call(f32[4096,2048]{1,0:T(8,128)S(1)} %get-tuple-element.26._, bf16[4096,128]{1,0:T(8,128)(2,1)S(1)} %get-tuple-element.24.refs_1_.centre_ref, bf16[512,128]{1,0:T(8,128)(2,1)S(1)} %copy-done), custom_call_target="tpu_custom_call", output_to_operand_aliasing={{0}: (0, {})} | custom-call | flops 2000000000 | bytes 1048576 | tf_op jit(solution)/shard_map/pallas_call | solution.py:36
  25.3 2.1 %collective-permute-done.5.refs_3_ = f32[1,2048]{1,0:T(1,128)S(1)} collective-permute-done((f32[1,2048]{1,0:T(1,128)S(1)}, f32[1,2048]{1,0:T(1,128)S(1)}, u32[]{:S(2)}, u32[]{:S(2)}) %collective-permute-start.5) | collective-permute-done | bytes 8224 | tf_op jit(solution)/shard_map/ppermute | solution.py:290
  27.4 4.5 %shard_map.53 = (f32[4096,2048]{1,0:T(8,128)S(1)}, f32[1,2560]{1,0:T(1,128)S(1)}) custom-call(f32[4096,2048]{1,0:T(8,128)S(1)} %get-tuple-element.27.refs_0_, f32[1,2048]{1,0:T(1,128)S(1)} %add.21.refs_1_, f32[1,2048]{1,0:T(1,128)S(1)} %collective-permute-done.4.refs_2_, ...), custom_call_target="tpu_custom_call", output_to_operand_aliasing={{0}: (0, {})} | custom-call | flops 5000000000 | bytes 1048576 | tf_op jit(solution)/shard_map/pallas_call | solution.py:36
  32.0 1.2 %collective-permute-done.7 = f32[1,2560]{1,0:T(1,128)S(1)} collective-permute-done((f32[1,2560]{1,0:T(1,128)S(1)}, f32[1,2560]{1,0:T(1,128)S(1)}, u32[]{:S(2)}, u32[]{:S(2)}) %collective-permute-start.7) | collective-permute-done | bytes 10272 | tf_op jit(solution)/shard_map/ppermute | solution.py:290
  33.2 1.5 %collective-permute-start.10 = (f32[1,2560]{1,0:T(1,128)S(1)}, f32[1,2560]{1,0:T(1,128)S(1)}, u32[]{:S(2)}, u32[]{:S(2)}) collective-permute-start(f32[1,2560]{1,0:T(1,128)S(1)} %add.22.refs_1_), channel_id=1, source_target_pairs={{0,6},{1,7},{2,4},{3,5},{4,2},{5,3},{6,0},{7,1},{8,14},{9,15},{10,... | collective-permute-start | bytes 30728 | tf_op jit(solution)/shard_map/ppermute | solution.py:290
  35.4 2.3 %collective-permute-start.9 = (f32[1,2560]{1,0:T(1,128)S(1)}, f32[1,2560]{1,0:T(1,128)S(1)}, u32[]{:S(2)}, u32[]{:S(2)}) collective-permute-start(f32[1,2560]{1,0:T(1,128)S(1)} %add.22.refs_1_), channel_id=1, source_target_pairs={{0,2},{1,3},{2,0},{3,1},{4,6},{5,7},{6,4},{7,5},{8,10},{9,11},{10,... | collective-permute-start | bytes 30728 | tf_op jit(solution)/shard_map/ppermute | solution.py:290
  37.7 1.1 %collective-permute-done.10.refs_4_ = f32[1,2560]{1,0:T(1,128)S(1)} collective-permute-done((f32[1,2560]{1,0:T(1,128)S(1)}, f32[1,2560]{1,0:T(1,128)S(1)}, u32[]{:S(2)}, u32[]{:S(2)}) %collective-permute-start.10) | collective-permute-done | bytes 10272 | tf_op jit(solution)/shard_map/ppermute | solution.py:290
  39.4 5.1 %shard_map.54 = (f32[4096,2048]{1,0:T(8,128)S(1)}, f32[1,2048]{1,0:T(1,128)S(1)}, f32[1,512]{1,0:T(1,128)S(1)}, bf16[528,128]{1,0:T(8,128)(2,1)S(1)}) custom-call(f32[4096,2048]{1,0:T(8,128)S(1)} %get-tuple-element.30.refs_0_, f32[1,2560]{1,0:T(1,128)S(1)} %add.22.refs_1_, ...), custom_call_target="tpu_custom_call", output_to_operand_aliasing={{0}: (0, {})} | custom-call | flops 5000000000 | bytes 1048576 | tf_op jit(solution)/shard_map/pallas_call | solution.py:36
  44.6 1.2 %collective-permute-done.11 = f32[1,2048]{1,0:T(1,128)S(1)} collective-permute-done((f32[1,2048]{1,0:T(1,128)S(1)}, f32[1,2048]{1,0:T(1,128)S(1)}, u32[]{:S(2)}, u32[]{:S(2)}) %collective-permute-start.11) | collective-permute-done | bytes 8224 | tf_op jit(solution)/shard_map/ppermute | solution.py:290
  45.8 2.5 %collective-permute-start.12 = (f32[1,2048]{1,0:T(1,128)S(1)}, f32[1,2048]{1,0:T(1,128)S(1)}, u32[]{:S(2)}, u32[]{:S(2)}) collective-permute-start(f32[1,2048]{1,0:T(1,128)S(1)} %add.23.refs_4_), channel_id=1, source_target_pairs={{0,6},{1,7},{2,4},{3,5},{4,2},{5,3},{6,0},{7,1},{8,14},{9,15},{10,... | collective-permute-start | bytes 24584 | tf_op jit(solution)/shard_map/ppermute | solution.py:290
  50.3 1.7 %collective-permute-start.19 = (bf16[528,128]{1,0:T(8,128)(2,1)S(1)}, bf16[528,128]{1,0:T(8,128)(2,1)S(1)}, u32[]{:S(2)}, u32[]{:S(2)}) collective-permute-start(bf16[528,128]{1,0:T(8,128)(2,1)S(1)} %get-tuple-element.41), channel_id=1, source_target_pairs={{0,24},{8,16},{16,8},{24,0},{1,25},{9,17},{17,9},{25,1},{2,26},{10... | collective-permute-start | bytes 405512 | tf_op jit(solution)/shard_map/ppermute | solution.py:290
  51.9 1.3 %collective-permute-start.20 = (bf16[528,128]{1,0:T(8,128)(2,1)S(1)}, bf16[528,128]{1,0:T(8,128)(2,1)S(1)}, u32[]{:S(2)}, u32[]{:S(2)}) collective-permute-start(bf16[528,128]{1,0:T(8,128)(2,1)S(1)} %get-tuple-element.41), channel_id=1, source_target_pairs={{0,16},{8,24},{16,0},{24,8},{1,17},{9,25},{17,1},{25,9},{2,18},{10... | collective-permute-start | bytes 405512 | tf_op jit(solution)/shard_map/ppermute | solution.py:290
  53.8 2.5 %shard_map.55 = (f32[4096,2048]{1,0:T(8,128)S(1)}, f32[256,128]{1,0:T(8,128)S(1)}, f32[256,128]{1,0:T(8,128)S(1)}, f32[1,2048]{1,0:T(1,128)S(1)}, bf16[4096,512]{1,0:T(8,128)(2,1)S(1)}) custom-call(f32[4096,2048]{1,0:T(8,128)S(1)} %get-tuple-element.33.refs_0_, ...), custom_call_target="tpu_custom_call", output_to_operand_aliasing={{0}: (0, {})} | custom-call | flops 4000000000 | bytes 1048576 | tf_op jit(solution)/shard_map/pallas_call | solution.py:36
  56.3 1.3 %collective-permute-done.15 = f32[256,128]{1,0:T(8,128)S(1)} collective-permute-done((f32[256,128]{1,0:T(8,128)S(1)}, f32[256,128]{1,0:T(8,128)S(1)}, u32[]{:S(2)}, u32[]{:S(2)}) %collective-permute-start.15) | collective-permute-done | bytes 131104 | tf_op jit(solution)/shard_map/ppermute | solution.py:290
  57.7 2.5 %collective-permute-start.16 = (f32[256,128]{1,0:T(8,128)S(1)}, f32[256,128]{1,0:T(8,128)S(1)}, u32[]{:S(2)}, u32[]{:S(2)}) collective-permute-start(f32[256,128]{1,0:T(8,128)S(1)} %add.24), channel_id=1, source_target_pairs={{0,6},{1,7},{2,4},{3,5},{4,2},{5,3},{6,0},{7,1},{8,14},{9,15},{10,... | collective-permute-start | bytes 393224 | tf_op jit(solution)/shard_map/ppermute | solution.py:290
  60.2 1.9 %collective-permute-start.18 = (f32[256,128]{1,0:T(8,128)S(1)}, f32[256,128]{1,0:T(8,128)S(1)}, u32[]{:S(2)}, u32[]{:S(2)}) collective-permute-start(f32[256,128]{1,0:T(8,128)S(1)} %add.24), channel_id=1, source_target_pairs={{0,2},{1,3},{2,0},{3,1},{4,6},{5,7},{6,4},{7,5},{8,10},{9,11},{10,... | collective-permute-start | bytes 393224 | tf_op jit(solution)/shard_map/ppermute | solution.py:290
  62.1 10.0 %shard_map.56 = f32[4096,128]{1,0:T(8,128)} custom-call(f32[4096,2048]{1,0:T(8,128)S(1)} %get-tuple-element.38.refs_0_, bf16[4096,128]{1,0:T(8,128)(2,1)S(1)} %get-tuple-element.24.refs_1_.centre_ref, bf16[512,128]{1,0:T(8,128)(2,1)S(1)} %get-tuple-element.32.refs_5_.refs_2_, f32[1,2048]{1,0:T(1,128)S(1)} %get-tuple-element.39.refs_3_, ...), custom_call_target="tpu_custom_call" | custom-call | flops 10000000000 | bytes 1048576 | tf_op jit(solution)/shard_map/pallas_call | solution.py:36
  72.3 1.3 %collective-permute-done.22 = f32[256,128]{1,0:T(8,128)S(1)} collective-permute-done((f32[256,128]{1,0:T(8,128)S(1)}, f32[256,128]{1,0:T(8,128)S(1)}, u32[]{:S(2)}, u32[]{:S(2)}) %collective-permute-start.22) | collective-permute-done | bytes 131104 | tf_op jit(solution)/shard_map/ppermute | solution.py:290
  (37 shorter events, 7.0 us)
Async XLA Ops:
  0.6 23.1 %copy-start = (bf16[512,128]{1,0:T(8,128)(2,1)S(1)}, bf16[512,128]{1,0:T(8,128)(2,1)}, u32[]{:S(2)}) copy-start(bf16[512,128]{1,0:T(8,128)(2,1)} %token_ref.3) | copy-start | bytes 393220
  0.6 8.2 %collective-permute-start = (bf16[512,128]{1,0:T(8,128)(2,1)}, bf16[512,128]{1,0:T(8,128)(2,1)S(1)}, u32[]{:S(2)}, u32[]{:S(2)}) collective-permute-start(bf16[512,128]{1,0:T(8,128)(2,1)} %token_ref.2), channel_id=1, source_target_pairs={{0,24},{8,16},{16,8},{24,0},{1,25},{9,17},{17,9},{25,1},{2,26},{10... | collective-permute-start | bytes 393224 | tf_op jit(solution)/shard_map/ppermute | solution.py:290
  4.6 6.5 %collective-permute-start.1 = (bf16[512,128]{1,0:T(8,128)(2,1)}, bf16[512,128]{1,0:T(8,128)(2,1)S(1)}, u32[]{:S(2)}, u32[]{:S(2)}) collective-permute-start(bf16[512,128]{1,0:T(8,128)(2,1)} %token_ref.2), channel_id=1, source_target_pairs={{0,16},{8,24},{16,0},{24,8},{1,17},{9,25},{17,1},{25,9},{2,18},{10... | collective-permute-start | bytes 393224 | tf_op jit(solution)/shard_map/ppermute | solution.py:290
  5.1 6.3 %collective-permute-start.2 = (bf16[512,128]{1,0:T(8,128)(2,1)}, bf16[512,128]{1,0:T(8,128)(2,1)S(1)}, u32[]{:S(2)}, u32[]{:S(2)}) collective-permute-start(bf16[512,128]{1,0:T(8,128)(2,1)} %token_ref.2), channel_id=1, source_target_pairs={{0,8},{8,0},{16,24},{24,16},{1,9},{9,1},{17,25},{25,17},{2,10},{10... | collective-permute-start | bytes 393224 | tf_op jit(solution)/shard_map/ppermute | solution.py:290
  18.0 1.2 %collective-permute-start.3 = (f32[1,2048]{1,0:T(1,128)S(1)}, f32[1,2048]{1,0:T(1,128)S(1)}, u32[]{:S(2)}, u32[]{:S(2)}) collective-permute-start(f32[1,2048]{1,0:T(1,128)S(1)} %get-tuple-element.28), channel_id=1, source_target_pairs={{0,1},{1,0},{2,3},{3,2},{4,5},{5,4},{6,7},{7,6},{8,9},{9,8},{10,11... | collective-permute-start | bytes 24584 | tf_op jit(solution)/shard_map/ppermute | solution.py:290
  19.2 6.0 %collective-permute-start.4 = (f32[1,2048]{1,0:T(1,128)S(1)}, f32[1,2048]{1,0:T(1,128)S(1)}, u32[]{:S(2)}, u32[]{:S(2)}) collective-permute-start(f32[1,2048]{1,0:T(1,128)S(1)} %add.21.refs_1_), channel_id=1, source_target_pairs={{0,6},{1,7},{2,4},{3,5},{4,2},{5,3},{6,0},{7,1},{8,14},{9,15},{10,... | collective-permute-start | bytes 24584 | tf_op jit(solution)/shard_map/ppermute | solution.py:290
  22.9 4.5 %collective-permute-start.5 = (f32[1,2048]{1,0:T(1,128)S(1)}, f32[1,2048]{1,0:T(1,128)S(1)}, u32[]{:S(2)}, u32[]{:S(2)}) collective-permute-start(f32[1,2048]{1,0:T(1,128)S(1)} %add.21.refs_1_), channel_id=1, source_target_pairs={{0,4},{1,5},{2,6},{3,7},{4,0},{5,1},{6,2},{7,3},{8,12},{9,13},{10,... | collective-permute-start | bytes 24584 | tf_op jit(solution)/shard_map/ppermute | solution.py:290
  22.9 4.5 %collective-permute-start.6 = (f32[1,2048]{1,0:T(1,128)S(1)}, f32[1,2048]{1,0:T(1,128)S(1)}, u32[]{:S(2)}, u32[]{:S(2)}) collective-permute-start(f32[1,2048]{1,0:T(1,128)S(1)} %add.21.refs_1_), channel_id=1, source_target_pairs={{0,2},{1,3},{2,0},{3,1},{4,6},{5,7},{6,4},{7,5},{8,10},{9,11},{10,... | collective-permute-start | bytes 24584 | tf_op jit(solution)/shard_map/ppermute | solution.py:290
  32.0 1.2 %collective-permute-start.7 = (f32[1,2560]{1,0:T(1,128)S(1)}, f32[1,2560]{1,0:T(1,128)S(1)}, u32[]{:S(2)}, u32[]{:S(2)}) collective-permute-start(f32[1,2560]{1,0:T(1,128)S(1)} %get-tuple-element.31), channel_id=1, source_target_pairs={{0,1},{1,0},{2,3},{3,2},{4,5},{5,4},{6,7},{7,6},{8,9},{9,8},{10,11... | collective-permute-start | bytes 30728 | tf_op jit(solution)/shard_map/ppermute | solution.py:290
  33.2 5.6 %collective-permute-start.10 = (f32[1,2560]{1,0:T(1,128)S(1)}, f32[1,2560]{1,0:T(1,128)S(1)}, u32[]{:S(2)}, u32[]{:S(2)}) collective-permute-start(f32[1,2560]{1,0:T(1,128)S(1)} %add.22.refs_1_), channel_id=1, source_target_pairs={{0,6},{1,7},{2,4},{3,5},{4,2},{5,3},{6,0},{7,1},{8,14},{9,15},{10,... | collective-permute-start | bytes 30728 | tf_op jit(solution)/shard_map/ppermute | solution.py:290
  34.7 4.6 %collective-permute-start.8 = (f32[1,2560]{1,0:T(1,128)S(1)}, f32[1,2560]{1,0:T(1,128)S(1)}, u32[]{:S(2)}, u32[]{:S(2)}) collective-permute-start(f32[1,2560]{1,0:T(1,128)S(1)} %add.22.refs_1_), channel_id=1, source_target_pairs={{0,4},{1,5},{2,6},{3,7},{4,0},{5,1},{6,2},{7,3},{8,12},{9,13},{10,... | collective-permute-start | bytes 30728 | tf_op jit(solution)/shard_map/ppermute | solution.py:290
  35.4 4.0 %collective-permute-start.9 = (f32[1,2560]{1,0:T(1,128)S(1)}, f32[1,2560]{1,0:T(1,128)S(1)}, u32[]{:S(2)}, u32[]{:S(2)}) collective-permute-start(f32[1,2560]{1,0:T(1,128)S(1)} %add.22.refs_1_), channel_id=1, source_target_pairs={{0,2},{1,3},{2,0},{3,1},{4,6},{5,7},{6,4},{7,5},{8,10},{9,11},{10,... | collective-permute-start | bytes 30728 | tf_op jit(solution)/shard_map/ppermute | solution.py:290
  44.5 1.2 %collective-permute-start.11 = (f32[1,2048]{1,0:T(1,128)S(1)}, f32[1,2048]{1,0:T(1,128)S(1)}, u32[]{:S(2)}, u32[]{:S(2)}) collective-permute-start(f32[1,2048]{1,0:T(1,128)S(1)} %get-tuple-element.35), channel_id=1, source_target_pairs={{0,1},{1,0},{2,3},{3,2},{4,5},{5,4},{6,7},{7,6},{8,9},{9,8},{10,11... | collective-permute-start | bytes 24584 | tf_op jit(solution)/shard_map/ppermute | solution.py:290
  45.8 7.5 %collective-permute-start.12 = (f32[1,2048]{1,0:T(1,128)S(1)}, f32[1,2048]{1,0:T(1,128)S(1)}, u32[]{:S(2)}, u32[]{:S(2)}) collective-permute-start(f32[1,2048]{1,0:T(1,128)S(1)} %add.23.refs_4_), channel_id=1, source_target_pairs={{0,6},{1,7},{2,4},{3,5},{4,2},{5,3},{6,0},{7,1},{8,14},{9,15},{10,... | collective-permute-start | bytes 24584 | tf_op jit(solution)/shard_map/ppermute | solution.py:290
  48.3 5.4 %collective-permute-start.13 = (f32[1,2048]{1,0:T(1,128)S(1)}, f32[1,2048]{1,0:T(1,128)S(1)}, u32[]{:S(2)}, u32[]{:S(2)}) collective-permute-start(f32[1,2048]{1,0:T(1,128)S(1)} %add.23.refs_4_), channel_id=1, source_target_pairs={{0,4},{1,5},{2,6},{3,7},{4,0},{5,1},{6,2},{7,3},{8,12},{9,13},{10,... | collective-permute-start | bytes 24584 | tf_op jit(solution)/shard_map/ppermute | solution.py:290
  49.2 4.5 %collective-permute-start.14 = (f32[1,2048]{1,0:T(1,128)S(1)}, f32[1,2048]{1,0:T(1,128)S(1)}, u32[]{:S(2)}, u32[]{:S(2)}) collective-permute-start(f32[1,2048]{1,0:T(1,128)S(1)} %add.23.refs_4_), channel_id=1, source_target_pairs={{0,2},{1,3},{2,0},{3,1},{4,6},{5,7},{6,4},{7,5},{8,10},{9,11},{10,... | collective-permute-start | bytes 24584 | tf_op jit(solution)/shard_map/ppermute | solution.py:290
  50.3 10.0 %collective-permute-start.19 = (bf16[528,128]{1,0:T(8,128)(2,1)S(1)}, bf16[528,128]{1,0:T(8,128)(2,1)S(1)}, u32[]{:S(2)}, u32[]{:S(2)}) collective-permute-start(bf16[528,128]{1,0:T(8,128)(2,1)S(1)} %get-tuple-element.41), channel_id=1, source_target_pairs={{0,24},{8,16},{16,8},{24,0},{1,25},{9,17},{17,9},{25,1},{2,26},{10... | collective-permute-start | bytes 405512 | tf_op jit(solution)/shard_map/ppermute | solution.py:290
  51.9 10.2 %collective-permute-start.20 = (bf16[528,128]{1,0:T(8,128)(2,1)S(1)}, bf16[528,128]{1,0:T(8,128)(2,1)S(1)}, u32[]{:S(2)}, u32[]{:S(2)}) collective-permute-start(bf16[528,128]{1,0:T(8,128)(2,1)S(1)} %get-tuple-element.41), channel_id=1, source_target_pairs={{0,16},{8,24},{16,0},{24,8},{1,17},{9,25},{17,1},{25,9},{2,18},{10... | collective-permute-start | bytes 405512 | tf_op jit(solution)/shard_map/ppermute | solution.py:290
  53.2 8.9 %collective-permute-start.21 = (bf16[528,128]{1,0:T(8,128)(2,1)S(1)}, bf16[528,128]{1,0:T(8,128)(2,1)S(1)}, u32[]{:S(2)}, u32[]{:S(2)}) collective-permute-start(bf16[528,128]{1,0:T(8,128)(2,1)S(1)} %get-tuple-element.41), channel_id=1, source_target_pairs={{0,8},{8,0},{16,24},{24,16},{1,9},{9,1},{17,25},{25,17},{2,10},{10... | collective-permute-start | bytes 405512 | tf_op jit(solution)/shard_map/ppermute | solution.py:290
  56.2 1.4 %collective-permute-start.15 = (f32[256,128]{1,0:T(8,128)S(1)}, f32[256,128]{1,0:T(8,128)S(1)}, u32[]{:S(2)}, u32[]{:S(2)}) collective-permute-start(f32[256,128]{1,0:T(8,128)S(1)} %get-tuple-element.37), channel_id=1, source_target_pairs={{0,1},{1,0},{2,3},{3,2},{4,5},{5,4},{6,7},{7,6},{8,9},{9,8},{10,11... | collective-permute-start | bytes 393224 | tf_op jit(solution)/shard_map/ppermute | solution.py:290
  57.7 14.5 %collective-permute-start.16 = (f32[256,128]{1,0:T(8,128)S(1)}, f32[256,128]{1,0:T(8,128)S(1)}, u32[]{:S(2)}, u32[]{:S(2)}) collective-permute-start(f32[256,128]{1,0:T(8,128)S(1)} %add.24), channel_id=1, source_target_pairs={{0,6},{1,7},{2,4},{3,5},{4,2},{5,3},{6,0},{7,1},{8,14},{9,15},{10,... | collective-permute-start | bytes 393224 | tf_op jit(solution)/shard_map/ppermute | solution.py:290
  60.2 12.0 %collective-permute-start.17 = (f32[256,128]{1,0:T(8,128)S(1)}, f32[256,128]{1,0:T(8,128)S(1)}, u32[]{:S(2)}, u32[]{:S(2)}) collective-permute-start(f32[256,128]{1,0:T(8,128)S(1)} %add.24), channel_id=1, source_target_pairs={{0,4},{1,5},{2,6},{3,7},{4,0},{5,1},{6,2},{7,3},{8,12},{9,13},{10,... | collective-permute-start | bytes 393224 | tf_op jit(solution)/shard_map/ppermute | solution.py:290
  60.2 11.9 %collective-permute-start.18 = (f32[256,128]{1,0:T(8,128)S(1)}, f32[256,128]{1,0:T(8,128)S(1)}, u32[]{:S(2)}, u32[]{:S(2)}) collective-permute-start(f32[256,128]{1,0:T(8,128)S(1)} %add.24), channel_id=1, source_target_pairs={{0,2},{1,3},{2,0},{3,1},{4,6},{5,7},{6,4},{7,5},{8,10},{9,11},{10,... | collective-permute-start | bytes 393224 | tf_op jit(solution)/shard_map/ppermute | solution.py:290
  72.2 1.4 %collective-permute-start.22 = (f32[256,128]{1,0:T(8,128)S(1)}, f32[256,128]{1,0:T(8,128)S(1)}, u32[]{:S(2)}, u32[]{:S(2)}) collective-permute-start(f32[256,128]{1,0:T(8,128)S(1)} %add_add_fusion), channel_id=1, source_target_pairs={{0,1},{1,0},{2,3},{3,2},{4,5},{5,4},{6,7},{7,6},{8,9},{9,8},{10,11... | collective-permute-start | bytes 393224 | tf_op jit(solution)/shard_map/ppermute | solution.py:290

commit v7 on v6

--- a/solution.py
+++ b/solution.py
@@ -123,12 +123,24 @@
     steps("own", proto_ref.shape[0], step)
 
 
-def first_pass(*refs, parts, scale, total):
+def first_pass(*refs, parts, by_core, scale, total):
     (_, centre_ref, column_ref), token_refs = refs[:3], refs[3 : 3 + parts]
     code_ref, out_ref, tok, acc, columns = refs[3 + parts :]
     n = token_refs[0].shape[0]
-    for i, t in enumerate(token_refs):
-        tok[i * n : (i + 1) * n, :] = normalize(t[...])
+    if by_core:
+        core = lax.rem(lax.axis_index("proto"), 2)
+        far, near, swapped_far, swapped_near = token_refs
+        tok[part(core, n), :] = normalize(near[...])
+        tok[part(1 - core, n), :] = normalize(swapped_near[...])
+        for c, t in enumerate((far, swapped_far)):
+
+            @pl.when(core == c)
+            def _():
+                tok[2 * n :, :] = normalize(t[...])
+
+    else:
+        for i, t in enumerate(token_refs[::-1]):
+            tok[i * n : (i + 1) * n, :] = normalize(t[...])
     acc[...] = jnp.zeros_like(acc)
     block = block_of("first", centre_ref.shape[0])
 
@@ -257,7 +269,7 @@
     (code_ref, centre_ref, tok_ref, scale_ref, logit_ref), packs = refs[:5], refs[5 : 5 + parts]
     out_ref, tok, weight, *slots = refs[5 + parts :]
     tokens, own = code_ref.shape[1], tok_ref.shape[0]
-    for i, pack in enumerate(packs):
+    for i, pack in enumerate(packs[::-1]):
         tok[i * own : (i + 1) * own, :] = pack[:own, :]
         pieces = pack[own:, :].astype(F32)
         count = own // 128
@@ -292,6 +304,18 @@
 
 def others_of(x, axis):
     return [swapped(x, axis, m) for m in range(lax.axis_size(axis) - 1, 0, -1)]
+
+
+def others_by_core(x):
+    dp, proto = lax.axis_size("dp"), lax.axis_size("proto")
+
+    def fetched(masks):
+        pairs = [
+            (i * proto + j, (i ^ masks[j % 2]) * proto + j) for i in range(dp) for j in range(proto)
+        ]
+        return lax.ppermute(x, ("dp", "proto"), pairs)
+
+    return [fetched((3, 0)), fetched((1, 2))]
 
 
 def proto_terms(x):
@@ -326,7 +350,8 @@
     pred_scale = log2e / d / PRED_TEMP
     acc = pltpu.VMEM((8, tokens), F32)
 
-    views = others_of(first_view, "dp")
+    by_core = lax.axis_size("dp") == 4
+    views = others_by_core(first_view) if by_core else others_of(first_view, "dp")
     code, centres, columns = run(
         functools.partial(own_codes, scale=code_scale),
         [shape(k, tokens), shape(k, d, dtype=BF16), shape(k, 128)],
@@ -335,13 +360,18 @@
         keep=(0, 1, 2),
         us=3,
     )
-    parts = len(views)
+    parts = lax.axis_size("dp") - 1
+    if by_core:
+        *views, columns = lax.optimization_barrier((*views, columns))
+        views = views + [swapped(v, "proto", 1) for v in views]
     code, sums = run(
-        functools.partial(first_pass, parts=parts, scale=code_scale, total=total),
+        functools.partial(
+            first_pass, parts=len(views), by_core=by_core, scale=code_scale, total=total
+        ),
         [shape(1, tokens)],
         [code, centres, columns] + views,
         [pltpu.VMEM((tokens - own, d), BF16), acc, pltpu.VMEM((k, 128), F32)],
-        resident=list(range(1, 3 + parts)),
+        resident=list(range(1, 3 + len(views))),
         keep=[0],
         thread=True,
         us=7,

time: 74.5 us -> 78.6 us (1.055)
  waiting for transfers between devices: 13 us -> 15.1 us
  starting transfers between devices: 26.3 us -> 28.1 us
    ppermute x0 -> x2, starting transfers between devices: none -> 6.53 us  [fetched(): return lax.ppermute(x, ('dp', 'proto'), pairs)]
    ppermute x23 -> x22, starting transfers between devices: 26.3 us -> 21.6 us  [swapped(): lax.ppermute(x, axis, [(i, i ^ mask) for i in range(lax.axis_size(axis))])]
    ppermute x0 -> x2, waiting for transfers between devices: none -> 1.46 us  [fetched(): return lax.ppermute(x, ('dp', 'proto'), pairs)]
    ppermute x23 -> x22, waiting for transfers between devices: 13 us -> 13.6 us  [swapped(): lax.ppermute(x, axis, [(i, i ^ mask) for i in range(lax.axis_size(axis))])]
  transfers between devices with their start and end apart: 23 -> 24, of which waited for: 12 -> 12; matrix products, arithmetic and copies ran while one was open for 0% -> 0% of each run, Pallas kernels for 23% -> 22%
where the time goes in v7:
time: 78.6 us; the launch traced here: 78.4 us
  Pallas kernels  33.6 us (43%)
  starting transfers between devices  28.1 us (36%)
  waiting for transfers between devices  15.1 us (19%)
  other arithmetic  0.82 us (1%)
    pallas_call x7, Pallas kernels, run(): pl.pallas_call(body, out_shape=tuple((pltpu.VMEM(s.shape, s.dtype) if i i...  33.6 us
    ppermute x22, starting transfers between devices, swapped(): lax.ppermute(x, axis, [(i, i ^ mask) for i in range(lax.axis_size(axis))])  21.6 us
    ppermute x22, waiting for transfers between devices, swapped(): lax.ppermute(x, axis, [(i, i ^ mask) for i in range(lax.axis_size(axis))])  13.6 us
    ppermute x2, starting transfers between devices, fetched(): return lax.ppermute(x, ('dp', 'proto'), pairs)  6.53 us
  transfers between devices with their start and end apart: 24, of which 12 were waited for; matrix products, arithmetic and copies ran while one was open for 0% of the time, Pallas kernels for 22%

profile of v7, /device:TPU:0, one launch (start us, length us, event | category | flops | bytes accessed | tf_op | source)
XLA Modules:
  0.0 78.4 jit_solution(17154967905419324565)
XLA Ops:
  0.6 5.9 %collective-permute-start = (bf16[512,128]{1,0:T(8,128)(2,1)}, bf16[512,128]{1,0:T(8,128)(2,1)S(1)}, u32[]{:S(2)}, u32[]{:S(2)}) collective-permute-start(bf16[512,128]{1,0:T(8,128)(2,1)} %token_ref.2), channel_id=1, source_target_pairs={{0,24},{1,1},{2,26},{3,3},{4,28},{5,5},{6,30},{7,7},{8,16},{9,9},{... | collective-permute-start | bytes 393224 | tf_op jit(solution)/shard_map/ppermute | solution.py:316
  7.2 3.2 %shard_map.50 = (f32[4096,2048]{1,0:T(8,128)S(1)}, bf16[4096,128]{1,0:T(8,128)(2,1)S(1)}, f32[4096,128]{1,0:T(8,128)S(1)}) custom-call(bf16[4096,128]{1,0:T(8,128)(2,1)} %proto_ref.1, bf16[512,128]{1,0:T(8,128)(2,1)} %token_ref.2), custom_call_target="tpu_custom_call" | custom-call | flops 3000000000 | bytes 1048576 | tf_op jit(solution)/shard_map/pallas_call | solution.py:36
  10.4 1.5 %collective-permute-done.1.refs_4_ = bf16[512,128]{1,0:T(8,128)(2,1)S(1)} collective-permute-done((bf16[512,128]{1,0:T(8,128)(2,1)}, bf16[512,128]{1,0:T(8,128)(2,1)S(1)}, u32[]{:S(2)}, u32[]{:S(2)}) %collective-permute-start.1) | collective-permute-done | bytes 131104 | tf_op jit(solution)/shard_map/ppermute | solution.py:316
  13.4 6.7 %shard_map.51 = (f32[4096,2048]{1,0:T(8,128)S(1)}, f32[1,2048]{1,0:T(1,128)S(1)}) custom-call(f32[4096,2048]{1,0:T(8,128)S(1)} %get-tuple-element.26.refs_0_, bf16[4096,128]{1,0:T(8,128)(2,1)S(1)} %get-tuple-element.27.refs_1_.centre_ref, f32[4096,128]{1,0:T(8,128)S(1)} %get-tuple-element.29.refs_2_, ...), custom_call_target="tpu_custom_call", output_to_operand_aliasing={{0}: (0, {})} | custom-call | flops 7000000000 | bytes 1048576 | tf_op jit(solution)/shard_map/pallas_call | solution.py:36
  21.4 3.7 %collective-permute-start.5 = (f32[1,2048]{1,0:T(1,128)S(1)}, f32[1,2048]{1,0:T(1,128)S(1)}, u32[]{:S(2)}, u32[]{:S(2)}) collective-permute-start(f32[1,2048]{1,0:T(1,128)S(1)} %add.21.refs_1_), channel_id=1, source_target_pairs={{0,6},{1,7},{2,4},{3,5},{4,2},{5,3},{6,0},{7,1},{8,14},{9,15},{10,... | collective-permute-start | bytes 24584 | tf_op jit(solution)/shard_map/ppermute | solution.py:302
  25.8 1.6 %shard_map.52 = (f32[4096,2048]{1,0:T(8,128)S(1)}, bf16[512,128]{1,0:T(8,128)(2,1)S(1)}, f32[1,512]{1,0:T(1,128)S(1)}) custom-call(f32[4096,2048]{1,0:T(8,128)S(1)} %get-tuple-element.32._, bf16[4096,128]{1,0:T(8,128)(2,1)S(1)} %get-tuple-element.27.refs_1_.centre_ref, bf16[512,128]{1,0:T(8,128)(2,1)S(1)} %copy-done), custom_call_target="tpu_custom_call", output_to_operand_aliasing={{0}: (0, {})} | custom-call | flops 2000000000 | bytes 1048576 | tf_op jit(solution)/shard_map/pallas_call | solution.py:36
  27.4 2.1 %collective-permute-done.6.refs_3_ = f32[1,2048]{1,0:T(1,128)S(1)} collective-permute-done((f32[1,2048]{1,0:T(1,128)S(1)}, f32[1,2048]{1,0:T(1,128)S(1)}, u32[]{:S(2)}, u32[]{:S(2)}) %collective-permute-start.6) | collective-permute-done | bytes 8224 | tf_op jit(solution)/shard_map/ppermute | solution.py:302
  29.6 4.5 %shard_map.53 = (f32[4096,2048]{1,0:T(8,128)S(1)}, f32[1,2560]{1,0:T(1,128)S(1)}) custom-call(f32[4096,2048]{1,0:T(8,128)S(1)} %get-tuple-element.33.refs_0_, f32[1,2048]{1,0:T(1,128)S(1)} %add.21.refs_1_, f32[1,2048]{1,0:T(1,128)S(1)} %collective-permute-done.5.refs_2_, ...), custom_call_target="tpu_custom_call", output_to_operand_aliasing={{0}: (0, {})} | custom-call | flops 5000000000 | bytes 1048576 | tf_op jit(solution)/shard_map/pallas_call | solution.py:36
  34.2 1.2 %collective-permute-done.8 = f32[1,2560]{1,0:T(1,128)S(1)} collective-permute-done((f32[1,2560]{1,0:T(1,128)S(1)}, f32[1,2560]{1,0:T(1,128)S(1)}, u32[]{:S(2)}, u32[]{:S(2)}) %collective-permute-start.8) | collective-permute-done | bytes 10272 | tf_op jit(solution)/shard_map/ppermute | solution.py:302
  35.4 3.5 %collective-permute-start.11 = (f32[1,2560]{1,0:T(1,128)S(1)}, f32[1,2560]{1,0:T(1,128)S(1)}, u32[]{:S(2)}, u32[]{:S(2)}) collective-permute-start(f32[1,2560]{1,0:T(1,128)S(1)} %add.22.refs_1_), channel_id=1, source_target_pairs={{0,6},{1,7},{2,4},{3,5},{4,2},{5,3},{6,0},{7,1},{8,14},{9,15},{10,... | collective-permute-start | bytes 30728 | tf_op jit(solution)/shard_map/ppermute | solution.py:302
  39.1 1.9 %collective-permute-done.11.refs_4_ = f32[1,2560]{1,0:T(1,128)S(1)} collective-permute-done((f32[1,2560]{1,0:T(1,128)S(1)}, f32[1,2560]{1,0:T(1,128)S(1)}, u32[]{:S(2)}, u32[]{:S(2)}) %collective-permute-start.11) | collective-permute-done | bytes 10272 | tf_op jit(solution)/shard_map/ppermute | solution.py:302
  41.0 2.4 %collective-permute-done.9.refs_2_ = f32[1,2560]{1,0:T(1,128)S(1)} collective-permute-done((f32[1,2560]{1,0:T(1,128)S(1)}, f32[1,2560]{1,0:T(1,128)S(1)}, u32[]{:S(2)}, u32[]{:S(2)}) %collective-permute-start.9) | collective-permute-done | bytes 10272 | tf_op jit(solution)/shard_map/ppermute | solution.py:302
  43.5 4.9 %shard_map.54 = (f32[4096,2048]{1,0:T(8,128)S(1)}, f32[1,2048]{1,0:T(1,128)S(1)}, f32[1,512]{1,0:T(1,128)S(1)}, bf16[528,128]{1,0:T(8,128)(2,1)S(1)}) custom-call(f32[4096,2048]{1,0:T(8,128)S(1)} %get-tuple-element.36.refs_0_, f32[1,2560]{1,0:T(1,128)S(1)} %add.22.refs_1_, ...), custom_call_target="tpu_custom_call", output_to_operand_aliasing={{0}: (0, {})} | custom-call | flops 5000000000 | bytes 1048576 | tf_op jit(solution)/shard_map/pallas_call | solution.py:36
  48.5 1.2 %collective-permute-done.12 = f32[1,2048]{1,0:T(1,128)S(1)} collective-permute-done((f32[1,2048]{1,0:T(1,128)S(1)}, f32[1,2048]{1,0:T(1,128)S(1)}, u32[]{:S(2)}, u32[]{:S(2)}) %collective-permute-start.12) | collective-permute-done | bytes 8224 | tf_op jit(solution)/shard_map/ppermute | solution.py:302
  49.7 1.0 %collective-permute-start.13 = (f32[1,2048]{1,0:T(1,128)S(1)}, f32[1,2048]{1,0:T(1,128)S(1)}, u32[]{:S(2)}, u32[]{:S(2)}) collective-permute-start(f32[1,2048]{1,0:T(1,128)S(1)} %add.23.refs_4_), channel_id=1, source_target_pairs={{0,6},{1,7},{2,4},{3,5},{4,2},{5,3},{6,0},{7,1},{8,14},{9,15},{10,... | collective-permute-start | bytes 24584 | tf_op jit(solution)/shard_map/ppermute | solution.py:302
  50.6 3.5 %collective-permute-start.15 = (f32[1,2048]{1,0:T(1,128)S(1)}, f32[1,2048]{1,0:T(1,128)S(1)}, u32[]{:S(2)}, u32[]{:S(2)}) collective-permute-start(f32[1,2048]{1,0:T(1,128)S(1)} %add.23.refs_4_), channel_id=1, source_target_pairs={{0,2},{1,3},{2,0},{3,1},{4,6},{5,7},{6,4},{7,5},{8,10},{9,11},{10,... | collective-permute-start | bytes 24584 | tf_op jit(solution)/shard_map/ppermute | solution.py:302
  54.1 1.3 %collective-permute-start.20 = (bf16[528,128]{1,0:T(8,128)(2,1)S(1)}, bf16[528,128]{1,0:T(8,128)(2,1)S(1)}, u32[]{:S(2)}, u32[]{:S(2)}) collective-permute-start(bf16[528,128]{1,0:T(8,128)(2,1)S(1)} %get-tuple-element.47), channel_id=1, source_target_pairs={{0,24},{8,16},{16,8},{24,0},{1,25},{9,17},{17,9},{25,1},{2,26},{10... | collective-permute-start | bytes 405512 | tf_op jit(solution)/shard_map/ppermute | solution.py:302
  55.4 1.5 %collective-permute-start.21 = (bf16[528,128]{1,0:T(8,128)(2,1)S(1)}, bf16[528,128]{1,0:T(8,128)(2,1)S(1)}, u32[]{:S(2)}, u32[]{:S(2)}) collective-permute-start(bf16[528,128]{1,0:T(8,128)(2,1)S(1)} %get-tuple-element.47), channel_id=1, source_target_pairs={{0,16},{8,24},{16,0},{24,8},{1,17},{9,25},{17,1},{25,9},{2,18},{10... | collective-permute-start | bytes 405512 | tf_op jit(solution)/shard_map/ppermute | solution.py:302
  57.6 2.7 %shard_map.55 = (f32[4096,2048]{1,0:T(8,128)S(1)}, f32[256,128]{1,0:T(8,128)S(1)}, f32[256,128]{1,0:T(8,128)S(1)}, f32[1,2048]{1,0:T(1,128)S(1)}, bf16[4096,512]{1,0:T(8,128)(2,1)S(1)}) custom-call(f32[4096,2048]{1,0:T(8,128)S(1)} %get-tuple-element.39.refs_0_, ...), custom_call_target="tpu_custom_call", output_to_operand_aliasing={{0}: (0, {})} | custom-call | flops 4000000000 | bytes 1048576 | tf_op jit(solution)/shard_map/pallas_call | solution.py:36
  60.4 1.3 %collective-permute-done.16 = f32[256,128]{1,0:T(8,128)S(1)} collective-permute-done((f32[256,128]{1,0:T(8,128)S(1)}, f32[256,128]{1,0:T(8,128)S(1)}, u32[]{:S(2)}, u32[]{:S(2)}) %collective-permute-start.16) | collective-permute-done | bytes 131104 | tf_op jit(solution)/shard_map/ppermute | solution.py:302
  61.7 1.0 %collective-permute-start.17 = (f32[256,128]{1,0:T(8,128)S(1)}, f32[256,128]{1,0:T(8,128)S(1)}, u32[]{:S(2)}, u32[]{:S(2)}) collective-permute-start(f32[256,128]{1,0:T(8,128)S(1)} %add.24), channel_id=1, source_target_pairs={{0,6},{1,7},{2,4},{3,5},{4,2},{5,3},{6,0},{7,1},{8,14},{9,15},{10,... | collective-permute-start | bytes 393224 | tf_op jit(solution)/shard_map/ppermute | solution.py:302
  63.4 2.8 %collective-permute-start.19 = (f32[256,128]{1,0:T(8,128)S(1)}, f32[256,128]{1,0:T(8,128)S(1)}, u32[]{:S(2)}, u32[]{:S(2)}) collective-permute-start(f32[256,128]{1,0:T(8,128)S(1)} %add.24), channel_id=1, source_target_pairs={{0,2},{1,3},{2,0},{3,1},{4,6},{5,7},{6,4},{7,5},{8,10},{9,11},{10,... | collective-permute-start | bytes 393224 | tf_op jit(solution)/shard_map/ppermute | solution.py:302
  66.2 10.0 %shard_map.56 = f32[4096,128]{1,0:T(8,128)} custom-call(f32[4096,2048]{1,0:T(8,128)S(1)} %get-tuple-element.44.refs_0_, bf16[4096,128]{1,0:T(8,128)(2,1)S(1)} %get-tuple-element.27.refs_1_.centre_ref, bf16[512,128]{1,0:T(8,128)(2,1)S(1)} %get-tuple-element.38.refs_5_.refs_2_, f32[1,2048]{1,0:T(1,128)S(1)} %get-tuple-element.45.refs_3_, ...), custom_call_target="tpu_custom_call" | custom-call | flops 10000000000 | bytes 1048576 | tf_op jit(solution)/shard_map/pallas_call | solution.py:36
  76.3 1.3 %collective-permute-done.23 = f32[256,128]{1,0:T(8,128)S(1)} collective-permute-done((f32[256,128]{1,0:T(8,128)S(1)}, f32[256,128]{1,0:T(8,128)S(1)}, u32[]{:S(2)}, u32[]{:S(2)}) %collective-permute-start.23) | collective-permute-done | bytes 131104 | tf_op jit(solution)/shard_map/ppermute | solution.py:302
  (39 shorter events, 7.0 us)
Async XLA Ops:
  0.6 9.7 %collective-permute-start = (bf16[512,128]{1,0:T(8,128)(2,1)}, bf16[512,128]{1,0:T(8,128)(2,1)S(1)}, u32[]{:S(2)}, u32[]{:S(2)}) collective-permute-start(bf16[512,128]{1,0:T(8,128)(2,1)} %token_ref.2), channel_id=1, source_target_pairs={{0,24},{1,1},{2,26},{3,3},{4,28},{5,5},{6,30},{7,7},{8,16},{9,9},{... | collective-permute-start | bytes 393224 | tf_op jit(solution)/shard_map/ppermute | solution.py:316
  6.6 5.2 %collective-permute-start.1 = (bf16[512,128]{1,0:T(8,128)(2,1)}, bf16[512,128]{1,0:T(8,128)(2,1)S(1)}, u32[]{:S(2)}, u32[]{:S(2)}) collective-permute-start(bf16[512,128]{1,0:T(8,128)(2,1)} %token_ref.2), channel_id=1, source_target_pairs={{0,8},{1,17},{2,10},{3,19},{4,12},{5,21},{6,14},{7,23},{8,0},{9,25... | collective-permute-start | bytes 393224 | tf_op jit(solution)/shard_map/ppermute | solution.py:316
  11.8 1.3 %collective-permute-start.2 = (bf16[512,128]{1,0:T(8,128)(2,1)S(1)}, bf16[512,128]{1,0:T(8,128)(2,1)S(1)}, u32[]{:S(2)}, u32[]{:S(2)}) collective-permute-start(bf16[512,128]{1,0:T(8,128)(2,1)S(1)} %collective-permute-done.refs_3_), channel_id=1, source_target_pairs={{0,1},{1,0},{2,3},{3,2},{4,5},{5,4},{6,7},{7,6},{8,9},{9,8},{10,11... | collective-permute-start | bytes 393224 | tf_op jit(solution)/shard_map/ppermute | solution.py:302
  11.8 1.5 %collective-permute-start.3 = (bf16[512,128]{1,0:T(8,128)(2,1)S(1)}, bf16[512,128]{1,0:T(8,128)(2,1)S(1)}, u32[]{:S(2)}, u32[]{:S(2)}) collective-permute-start(bf16[512,128]{1,0:T(8,128)(2,1)S(1)} %collective-permute-done.1.refs_4_), channel_id=1, source_target_pairs={{0,1},{1,0},{2,3},{3,2},{4,5},{5,4},{6,7},{7,6},{8,9},{9,8},{10,11... | collective-permute-start | bytes 393224 | tf_op jit(solution)/shard_map/ppermute | solution.py:302
  20.1 1.2 %collective-permute-start.4 = (f32[1,2048]{1,0:T(1,128)S(1)}, f32[1,2048]{1,0:T(1,128)S(1)}, u32[]{:S(2)}, u32[]{:S(2)}) collective-permute-start(f32[1,2048]{1,0:T(1,128)S(1)} %get-tuple-element.34), channel_id=1, source_target_pairs={{0,1},{1,0},{2,3},{3,2},{4,5},{5,4},{6,7},{7,6},{8,9},{9,8},{10,11... | collective-permute-start | bytes 24584 | tf_op jit(solution)/shard_map/ppermute | solution.py:302
  21.4 6.1 %collective-permute-start.5 = (f32[1,2048]{1,0:T(1,128)S(1)}, f32[1,2048]{1,0:T(1,128)S(1)}, u32[]{:S(2)}, u32[]{:S(2)}) collective-permute-start(f32[1,2048]{1,0:T(1,128)S(1)} %add.21.refs_1_), channel_id=1, source_target_pairs={{0,6},{1,7},{2,4},{3,5},{4,2},{5,3},{6,0},{7,1},{8,14},{9,15},{10,... | collective-permute-start | bytes 24584 | tf_op jit(solution)/shard_map/ppermute | solution.py:302
  25.0 4.5 %collective-permute-start.6 = (f32[1,2048]{1,0:T(1,128)S(1)}, f32[1,2048]{1,0:T(1,128)S(1)}, u32[]{:S(2)}, u32[]{:S(2)}) collective-permute-start(f32[1,2048]{1,0:T(1,128)S(1)} %add.21.refs_1_), channel_id=1, source_target_pairs={{0,4},{1,5},{2,6},{3,7},{4,0},{5,1},{6,2},{7,3},{8,12},{9,13},{10,... | collective-permute-start | bytes 24584 | tf_op jit(solution)/shard_map/ppermute | solution.py:302
  25.0 4.5 %collective-permute-start.7 = (f32[1,2048]{1,0:T(1,128)S(1)}, f32[1,2048]{1,0:T(1,128)S(1)}, u32[]{:S(2)}, u32[]{:S(2)}) collective-permute-start(f32[1,2048]{1,0:T(1,128)S(1)} %add.21.refs_1_), channel_id=1, source_target_pairs={{0,2},{1,3},{2,0},{3,1},{4,6},{5,7},{6,4},{7,5},{8,10},{9,11},{10,... | collective-permute-start | bytes 24584 | tf_op jit(solution)/shard_map/ppermute | solution.py:302
  34.1 1.2 %collective-permute-start.8 = (f32[1,2560]{1,0:T(1,128)S(1)}, f32[1,2560]{1,0:T(1,128)S(1)}, u32[]{:S(2)}, u32[]{:S(2)}) collective-permute-start(f32[1,2560]{1,0:T(1,128)S(1)} %get-tuple-element.37), channel_id=1, source_target_pairs={{0,1},{1,0},{2,3},{3,2},{4,5},{5,4},{6,7},{7,6},{8,9},{9,8},{10,11... | collective-permute-start | bytes 30728 | tf_op jit(solution)/shard_map/ppermute | solution.py:302
  35.3 3.7 %collective-permute-start.10 = (f32[1,2560]{1,0:T(1,128)S(1)}, f32[1,2560]{1,0:T(1,128)S(1)}, u32[]{:S(2)}, u32[]{:S(2)}) collective-permute-start(f32[1,2560]{1,0:T(1,128)S(1)} %add.22.refs_1_), channel_id=1, source_target_pairs={{0,2},{1,3},{2,0},{3,1},{4,6},{5,7},{6,4},{7,5},{8,10},{9,11},{10,... | collective-permute-start | bytes 30728 | tf_op jit(solution)/shard_map/ppermute | solution.py:302
  35.4 5.6 %collective-permute-start.11 = (f32[1,2560]{1,0:T(1,128)S(1)}, f32[1,2560]{1,0:T(1,128)S(1)}, u32[]{:S(2)}, u32[]{:S(2)}) collective-permute-start(f32[1,2560]{1,0:T(1,128)S(1)} %add.22.refs_1_), channel_id=1, source_target_pairs={{0,6},{1,7},{2,4},{3,5},{4,2},{5,3},{6,0},{7,1},{8,14},{9,15},{10,... | collective-permute-start | bytes 30728 | tf_op jit(solution)/shard_map/ppermute | solution.py:302
  38.9 4.6 %collective-permute-start.9 = (f32[1,2560]{1,0:T(1,128)S(1)}, f32[1,2560]{1,0:T(1,128)S(1)}, u32[]{:S(2)}, u32[]{:S(2)}) collective-permute-start(f32[1,2560]{1,0:T(1,128)S(1)} %add.22.refs_1_), channel_id=1, source_target_pairs={{0,4},{1,5},{2,6},{3,7},{4,0},{5,1},{6,2},{7,3},{8,12},{9,13},{10,... | collective-permute-start | bytes 30728 | tf_op jit(solution)/shard_map/ppermute | solution.py:302
  48.4 1.2 %collective-permute-start.12 = (f32[1,2048]{1,0:T(1,128)S(1)}, f32[1,2048]{1,0:T(1,128)S(1)}, u32[]{:S(2)}, u32[]{:S(2)}) collective-permute-start(f32[1,2048]{1,0:T(1,128)S(1)} %get-tuple-element.41), channel_id=1, source_target_pairs={{0,1},{1,0},{2,3},{3,2},{4,5},{5,4},{6,7},{7,6},{8,9},{9,8},{10,11... | collective-permute-start | bytes 24584 | tf_op jit(solution)/shard_map/ppermute | solution.py:302
  49.7 7.2 %collective-permute-start.13 = (f32[1,2048]{1,0:T(1,128)S(1)}, f32[1,2048]{1,0:T(1,128)S(1)}, u32[]{:S(2)}, u32[]{:S(2)}) collective-permute-start(f32[1,2048]{1,0:T(1,128)S(1)} %add.23.refs_4_), channel_id=1, source_target_pairs={{0,6},{1,7},{2,4},{3,5},{4,2},{5,3},{6,0},{7,1},{8,14},{9,15},{10,... | collective-permute-start | bytes 24584 | tf_op jit(solution)/shard_map/ppermute | solution.py:302
  50.6 7.0 %collective-permute-start.14 = (f32[1,2048]{1,0:T(1,128)S(1)}, f32[1,2048]{1,0:T(1,128)S(1)}, u32[]{:S(2)}, u32[]{:S(2)}) collective-permute-start(f32[1,2048]{1,0:T(1,128)S(1)} %add.23.refs_4_), channel_id=1, source_target_pairs={{0,4},{1,5},{2,6},{3,7},{4,0},{5,1},{6,2},{7,3},{8,12},{9,13},{10,... | collective-permute-start | bytes 24584 | tf_op jit(solution)/shard_map/ppermute | solution.py:302
  50.6 7.0 %collective-permute-start.15 = (f32[1,2048]{1,0:T(1,128)S(1)}, f32[1,2048]{1,0:T(1,128)S(1)}, u32[]{:S(2)}, u32[]{:S(2)}) collective-permute-start(f32[1,2048]{1,0:T(1,128)S(1)} %add.23.refs_4_), channel_id=1, source_target_pairs={{0,2},{1,3},{2,0},{3,1},{4,6},{5,7},{6,4},{7,5},{8,10},{9,11},{10,... | collective-permute-start | bytes 24584 | tf_op jit(solution)/shard_map/ppermute | solution.py:302
  54.1 9.3 %collective-permute-start.20 = (bf16[528,128]{1,0:T(8,128)(2,1)S(1)}, bf16[528,128]{1,0:T(8,128)(2,1)S(1)}, u32[]{:S(2)}, u32[]{:S(2)}) collective-permute-start(bf16[528,128]{1,0:T(8,128)(2,1)S(1)} %get-tuple-element.47), channel_id=1, source_target_pairs={{0,24},{8,16},{16,8},{24,0},{1,25},{9,17},{17,9},{25,1},{2,26},{10... | collective-permute-start | bytes 405512 | tf_op jit(solution)/shard_map/ppermute | solution.py:302
  55.4 10.8 %collective-permute-start.21 = (bf16[528,128]{1,0:T(8,128)(2,1)S(1)}, bf16[528,128]{1,0:T(8,128)(2,1)S(1)}, u32[]{:S(2)}, u32[]{:S(2)}) collective-permute-start(bf16[528,128]{1,0:T(8,128)(2,1)S(1)} %get-tuple-element.47), channel_id=1, source_target_pairs={{0,16},{8,24},{16,0},{24,8},{1,17},{9,25},{17,1},{25,9},{2,18},{10... | collective-permute-start | bytes 405512 | tf_op jit(solution)/shard_map/ppermute | solution.py:302
  56.9 9.3 %collective-permute-start.22 = (bf16[528,128]{1,0:T(8,128)(2,1)S(1)}, bf16[528,128]{1,0:T(8,128)(2,1)S(1)}, u32[]{:S(2)}, u32[]{:S(2)}) collective-permute-start(bf16[528,128]{1,0:T(8,128)(2,1)S(1)} %get-tuple-element.47), channel_id=1, source_target_pairs={{0,8},{8,0},{16,24},{24,16},{1,9},{9,1},{17,25},{25,17},{2,10},{10... | collective-permute-start | bytes 405512 | tf_op jit(solution)/shard_map/ppermute | solution.py:302
  60.3 1.4 %collective-permute-start.16 = (f32[256,128]{1,0:T(8,128)S(1)}, f32[256,128]{1,0:T(8,128)S(1)}, u32[]{:S(2)}, u32[]{:S(2)}) collective-permute-start(f32[256,128]{1,0:T(8,128)S(1)} %get-tuple-element.43), channel_id=1, source_target_pairs={{0,1},{1,0},{2,3},{3,2},{4,5},{5,4},{6,7},{7,6},{8,9},{9,8},{10,11... | collective-permute-start | bytes 393224 | tf_op jit(solution)/shard_map/ppermute | solution.py:302
  61.7 14.5 %collective-permute-start.17 = (f32[256,128]{1,0:T(8,128)S(1)}, f32[256,128]{1,0:T(8,128)S(1)}, u32[]{:S(2)}, u32[]{:S(2)}) collective-permute-start(f32[256,128]{1,0:T(8,128)S(1)} %add.24), channel_id=1, source_target_pairs={{0,6},{1,7},{2,4},{3,5},{4,2},{5,3},{6,0},{7,1},{8,14},{9,15},{10,... | collective-permute-start | bytes 393224 | tf_op jit(solution)/shard_map/ppermute | solution.py:302
  62.7 13.5 %collective-permute-start.18 = (f32[256,128]{1,0:T(8,128)S(1)}, f32[256,128]{1,0:T(8,128)S(1)}, u32[]{:S(2)}, u32[]{:S(2)}) collective-permute-start(f32[256,128]{1,0:T(8,128)S(1)} %add.24), channel_id=1, source_target_pairs={{0,4},{1,5},{2,6},{3,7},{4,0},{5,1},{6,2},{7,3},{8,12},{9,13},{10,... | collective-permute-start | bytes 393224 | tf_op jit(solution)/shard_map/ppermute | solution.py:302
  63.4 12.8 %collective-permute-start.19 = (f32[256,128]{1,0:T(8,128)S(1)}, f32[256,128]{1,0:T(8,128)S(1)}, u32[]{:S(2)}, u32[]{:S(2)}) collective-permute-start(f32[256,128]{1,0:T(8,128)S(1)} %add.24), channel_id=1, source_target_pairs={{0,2},{1,3},{2,0},{3,1},{4,6},{5,7},{6,4},{7,5},{8,10},{9,11},{10,... | collective-permute-start | bytes 393224 | tf_op jit(solution)/shard_map/ppermute | solution.py:302
  76.2 1.4 %collective-permute-start.23 = (f32[256,128]{1,0:T(8,128)S(1)}, f32[256,128]{1,0:T(8,128)S(1)}, u32[]{:S(2)}, u32[]{:S(2)}) collective-permute-start(f32[256,128]{1,0:T(8,128)S(1)} %add_add_fusion), channel_id=1, source_target_pairs={{0,1},{1,0},{2,3},{3,2},{4,5},{5,4},{6,7},{7,6},{8,9},{9,8},{10,11... | collective-permute-start | bytes 393224 | tf_op jit(solution)/shard_map/ppermute | solution.py:302
  (1 other events, 25.2 us)

commit v8 on v6

--- a/solution.py
+++ b/solution.py
@@ -16,6 +16,7 @@
 CHUNK = 256
 BLOCKS = {"own": 2048, "first": 1024, "den": 2048, "middle": 512, "token": 2048}
 SUBS = {"first": 1, "proto": 1}
+COPIES = 4
 SPLIT = 3
 TILE = 16
 
@@ -28,7 +29,7 @@
     return jax.ShapeDtypeStruct(dims, dtype)
 
 
-def run(body, outs, args, scratch, resident=(), keep=(), us=1.0, thread=False):
+def run(body, outs, args, scratch, resident=(), keep=(), us=1.0, thread=False, copied=()):
     if thread:
         outs = [shape(*args[0].shape, dtype=args[0].dtype)] + outs
         keep = [0] + [i + 1 for i in keep]
@@ -37,7 +38,9 @@
         body,
         out_shape=tuple(pltpu.VMEM(s.shape, s.dtype) if i in keep else s for i, s in enumerate(outs)),
         in_specs=[vmem_spec()] * len(args),
-        out_specs=tuple(vmem_spec() for _ in outs),
+        out_specs=tuple(
+            pl.BlockSpec(memory_space=pl.ANY) if i in copied else vmem_spec() for i in range(len(outs))
+        ),
         scratch_shapes=scratch,
         input_output_aliases={0: 0} if thread else {},
         compiler_params=pltpu.CompilerParams(vmem_limit_bytes=VMEM_LIMIT),
@@ -70,7 +73,7 @@
     return min(BLOCKS[name], size // 2)
 
 
-def pipelined(n, fill, work, subs=1):
+def pipelined(n, fill, work, subs=1, end=None):
     def both(i, slot):
         for m in range(subs):
             fill(i, slot, m)
@@ -89,8 +92,11 @@
     else:
         lax.fori_loop(0, n // 2 - 1, body, 0)
     both(n - 1, 1)
-    for m in range(subs):
-        work(n - 1, 1, m)
+    if end is not None:
+        end()
+    else:
+        for m in range(subs):
+            work(n - 1, 1, m)
 
 
 def part(i, size):
@@ -123,10 +129,23 @@
     steps("own", proto_ref.shape[0], step)
 
 
+def more_codes(_, centre_ref, column_ref, token_ref, code_ref, out_ref, *, scale):
+    own = token_ref.shape[0]
+    tok = normalize(token_ref[...])
+
+    def step(at):
+        code = jnp.exp2(similarity(centre_ref[at, :], tok) * scale)
+        code_ref[at, own : 2 * own] = code
+        out_ref[at, :] = column_ref[at, :] + lane_sums(code)
+
+    steps("own", centre_ref.shape[0], step)
+
+
 def first_pass(*refs, parts, scale, total):
     (_, centre_ref, column_ref), token_refs = refs[:3], refs[3 : 3 + parts]
     code_ref, out_ref, tok, acc, columns = refs[3 + parts :]
     n = token_refs[0].shape[0]
+    done = code_ref.shape[1] - parts * n
     for i, t in enumerate(token_refs):
         tok[i * n : (i + 1) * n, :] = normalize(t[...])
     acc[...] = jnp.zeros_like(acc)
@@ -141,7 +160,7 @@
     def fill(i, slot, m):
         at = rows(i, m)
         code = jnp.exp2(similarity(centre_ref[at, :], tok[...]) * scale)
-        code_ref[at, n:] = code
+        code_ref[at, done:] = code
         columns[at, :] = column_ref[at, :] + lane_sums(code)
 
     def work(i, slot, m):
@@ -255,7 +274,7 @@
 
 def proto_part(*refs, parts, scale):
     (code_ref, centre_ref, tok_ref, scale_ref, logit_ref), packs = refs[:5], refs[5 : 5 + parts]
-    out_ref, tok, weight, *slots = refs[5 + parts :]
+    result_ref, tok, weight, out_ref, sems, *slots = refs[5 + parts :]
     tokens, own = code_ref.shape[1], tok_ref.shape[0]
     for i, pack in enumerate(packs):
         tok[i * own : (i + 1) * own, :] = pack[:own, :]
@@ -282,8 +301,23 @@
         out_ref[r, :] += jnp.dot(slots[slot][r, :], tok[part(i, CHUNK), :], preferred_element_type=F32)
 
     out_ref[...] = jnp.dot(logit_ref[...], tok_ref[...], preferred_element_type=F32)
-    pipelined(parts * own // CHUNK, fill, work, subs)
-    out_ref[...] = out_ref[...] * tokens ** (-0.5)
+    count = parts * own // CHUNK
+    copies = []
+
+    def end():
+        rows = out_ref.shape[0] // COPIES
+        for j in range(COPIES):
+            r = slice(j * rows, (j + 1) * rows)
+            last = jnp.dot(slots[1][r, :], tok[part(count - 1, CHUNK), :], preferred_element_type=F32)
+            out_ref[r, :] = (out_ref[r, :] + last) * tokens ** (-0.5)
+            copies.append(
+                pltpu.make_async_copy(out_ref.at[pl.ds(j * rows, rows)], result_ref.at[pl.ds(j * rows, rows)], sems.at[j])
+            )
+            copies[-1].start()
+
+    pipelined(count, fill, work, subs, end)
+    for c in copies:
+        c.wait()
 
 
 def swapped(x, axis, mask):
@@ -336,12 +370,23 @@
         us=3,
     )
     parts = len(views)
+    code, columns = run(
+        functools.partial(more_codes, scale=code_scale),
+        [shape(k, 128)],
+        [code, centres, columns, views[0]],
+        [],
+        resident=[1, 2, 3],
+        keep=[0],
+        thread=True,
+        us=2,
+    )
+    views = views[1:]
     code, sums = run(
-        functools.partial(first_pass, parts=parts, scale=code_scale, total=total),
+        functools.partial(first_pass, parts=len(views), scale=code_scale, total=total),
         [shape(1, tokens)],
         [code, centres, columns] + views,
-        [pltpu.VMEM((tokens - own, d), BF16), acc, pltpu.VMEM((k, 128), F32)],
-        resident=list(range(1, 3 + parts)),
+        [pltpu.VMEM((len(views) * own, d), BF16), acc, pltpu.VMEM((k, 128), F32)],
+        resident=list(range(1, 3 + len(views))),
         keep=[0],
         thread=True,
         us=7,
@@ -398,8 +443,10 @@
         [shape(k, d)],
         [code, centres, tok, token_scale, logits] + packs,
         [pltpu.VMEM((tokens - own, d), BF16), pltpu.VMEM((1, tokens - own), F32)]
+        + [pltpu.VMEM((k, d), F32), pltpu.SemaphoreType.DMA((COPIES,))]
         + [pltpu.VMEM((k, CHUNK), BF16)] * 2,
         resident=range(5 + parts),
+        copied=[0],
         us=10,
     )
     mine, proto_grad = lax.optimization_barrier((mine, proto_grad))

time: 74.5 us -> 73 us (0.980)
  waiting for transfers between devices: 13 us -> 11.7 us
    ppermute x23, waiting for transfers between devices: 13 us -> 11.7 us  [swapped(): lax.ppermute(x, axis, [(i, i ^ mask) for i in range(lax.axis_size(axis))])]
    pallas_call x7 -> x8, Pallas kernels: 33.5 us -> 33.4 us  [run(): pl.pallas_call(body, out_shape=tuple((pltpu.VMEM(s.shape, s.dtype) if i i...]
  transfers between devices with their start and end apart: 23 -> 23, of which waited for: 12 -> 13; matrix products, arithmetic and copies ran while one was open for 0% -> 0% of each run, Pallas kernels for 23% -> 26%
where the time goes in v8:
time: 73 us; the launch traced here: 72.9 us
  Pallas kernels  33.4 us (46%)
  starting transfers between devices  26.3 us (36%)
  waiting for transfers between devices  11.7 us (16%)
  other arithmetic  0.82 us (1%)
  between operations  0.78 us (1%)
    pallas_call x8, Pallas kernels, run(): pl.pallas_call(body, out_shape=tuple((pltpu.VMEM(s.shape, s.dtype) if i i...  33.4 us
    ppermute x23, starting transfers between devices, swapped(): lax.ppermute(x, axis, [(i, i ^ mask) for i in range(lax.axis_size(axis))])  26.3 us
    ppermute x23, waiting for transfers between devices, swapped(): lax.ppermute(x, axis, [(i, i ^ mask) for i in range(lax.axis_size(axis))])  11.7 us
  transfers between devices with their start and end apart: 23, of which 13 were waited for; matrix products, arithmetic and copies ran while one was open for 0% of the time, Pallas kernels for 26%

profile of v8, /device:TPU:0, one launch (start us, length us, event | category | flops | bytes accessed | tf_op | source)
XLA Modules:
  0.0 72.9 jit_solution(16406904205601020755)
XLA Ops:
  0.6 4.0 %collective-permute-start = (bf16[512,128]{1,0:T(8,128)(2,1)}, bf16[512,128]{1,0:T(8,128)(2,1)S(1)}, u32[]{:S(2)}, u32[]{:S(2)}) collective-permute-start(bf16[512,128]{1,0:T(8,128)(2,1)} %token_ref.2), channel_id=1, source_target_pairs={{0,24},{8,16},{16,8},{24,0},{1,25},{9,17},{17,9},{25,1},{2,26},{10... | collective-permute-start | bytes 393224 | tf_op jit(solution)/shard_map/ppermute | solution.py:324
  5.2 3.2 %shard_map.50 = (f32[4096,2048]{1,0:T(8,128)S(1)}, bf16[4096,128]{1,0:T(8,128)(2,1)S(1)}, f32[4096,128]{1,0:T(8,128)S(1)}) custom-call(bf16[4096,128]{1,0:T(8,128)(2,1)} %proto_ref.1, bf16[512,128]{1,0:T(8,128)(2,1)} %token_ref.2), custom_call_target="tpu_custom_call" | custom-call | flops 3000000000 | bytes 1048576 | tf_op jit(solution)/shard_map/pallas_call | solution.py:37
  8.8 1.6 %shard_map.51 = (f32[4096,2048]{1,0:T(8,128)S(1)}, f32[4096,128]{1,0:T(8,128)S(1)}) custom-call(f32[4096,2048]{1,0:T(8,128)S(1)} %get-tuple-element.25._, bf16[4096,128]{1,0:T(8,128)(2,1)S(1)} %get-tuple-element.26.centre_ref.refs_1_, f32[4096,128]{1,0:T(8,128)S(1)} %get-tuple-element.27.column_ref, ...), custom_call_target="tpu_custom_call", output_to_operand_aliasing={{0}: (0, {})} | custom-call | flops 2000000000 | bytes 1048576 | tf_op jit(solution)/shard_map/pallas_call | solution.py:37
  11.4 5.1 %shard_map.52 = (f32[4096,2048]{1,0:T(8,128)S(1)}, f32[1,2048]{1,0:T(1,128)S(1)}) custom-call(f32[4096,2048]{1,0:T(8,128)S(1)} %get-tuple-element.28.refs_0_, bf16[4096,128]{1,0:T(8,128)(2,1)S(1)} %get-tuple-element.26.centre_ref.refs_1_, f32[4096,128]{1,0:T(8,128)S(1)} %get-tuple-element.29.refs_2_, ...), custom_call_target="tpu_custom_call", output_to_operand_aliasing={{0}: (0, {})} | custom-call | flops 7000000000 | bytes 1048576 | tf_op jit(solution)/shard_map/pallas_call | solution.py:37
  16.6 1.2 %collective-permute-done.3 = f32[1,2048]{1,0:T(1,128)S(1)} collective-permute-done((f32[1,2048]{1,0:T(1,128)S(1)}, f32[1,2048]{1,0:T(1,128)S(1)}, u32[]{:S(2)}, u32[]{:S(2)}) %collective-permute-start.3) | collective-permute-done | bytes 8224 | tf_op jit(solution)/shard_map/ppermute | solution.py:324
  17.7 3.7 %collective-permute-start.4 = (f32[1,2048]{1,0:T(1,128)S(1)}, f32[1,2048]{1,0:T(1,128)S(1)}, u32[]{:S(2)}, u32[]{:S(2)}) collective-permute-start(f32[1,2048]{1,0:T(1,128)S(1)} %add.21.refs_1_), channel_id=1, source_target_pairs={{0,6},{1,7},{2,4},{3,5},{4,2},{5,3},{6,0},{7,1},{8,14},{9,15},{10,... | collective-permute-start | bytes 24584 | tf_op jit(solution)/shard_map/ppermute | solution.py:324
  22.2 1.6 %shard_map.53 = (f32[4096,2048]{1,0:T(8,128)S(1)}, bf16[512,128]{1,0:T(8,128)(2,1)S(1)}, f32[1,512]{1,0:T(1,128)S(1)}) custom-call(f32[4096,2048]{1,0:T(8,128)S(1)} %get-tuple-element.30._, bf16[4096,128]{1,0:T(8,128)(2,1)S(1)} %get-tuple-element.26.centre_ref.refs_1_, bf16[512,128]{1,0:T(8,128)(2,1)S(1)} %copy-done), custom_call_target="tpu_custom_call", output_to_operand_aliasing={{0}: (0, {})} | custom-call | flops 2000000000 | bytes 1048576 | tf_op jit(solution)/shard_map/pallas_call | solution.py:37
  23.8 2.2 %collective-permute-done.5.refs_3_ = f32[1,2048]{1,0:T(1,128)S(1)} collective-permute-done((f32[1,2048]{1,0:T(1,128)S(1)}, f32[1,2048]{1,0:T(1,128)S(1)}, u32[]{:S(2)}, u32[]{:S(2)}) %collective-permute-start.5) | collective-permute-done | bytes 8224 | tf_op jit(solution)/shard_map/ppermute | solution.py:324
  25.9 4.5 %shard_map.54 = (f32[4096,2048]{1,0:T(8,128)S(1)}, f32[1,2560]{1,0:T(1,128)S(1)}) custom-call(f32[4096,2048]{1,0:T(8,128)S(1)} %get-tuple-element.31.refs_0_, f32[1,2048]{1,0:T(1,128)S(1)} %add.21.refs_1_, f32[1,2048]{1,0:T(1,128)S(1)} %collective-permute-done.4.refs_2_, ...), custom_call_target="tpu_custom_call", output_to_operand_aliasing={{0}: (0, {})} | custom-call | flops 5000000000 | bytes 1048576 | tf_op jit(solution)/shard_map/pallas_call | solution.py:37
  30.5 1.2 %collective-permute-done.7 = f32[1,2560]{1,0:T(1,128)S(1)} collective-permute-done((f32[1,2560]{1,0:T(1,128)S(1)}, f32[1,2560]{1,0:T(1,128)S(1)}, u32[]{:S(2)}, u32[]{:S(2)}) %collective-permute-start.7) | collective-permute-done | bytes 10272 | tf_op jit(solution)/shard_map/ppermute | solution.py:324
  31.7 1.5 %collective-permute-start.10 = (f32[1,2560]{1,0:T(1,128)S(1)}, f32[1,2560]{1,0:T(1,128)S(1)}, u32[]{:S(2)}, u32[]{:S(2)}) collective-permute-start(f32[1,2560]{1,0:T(1,128)S(1)} %add.22.refs_1_), channel_id=1, source_target_pairs={{0,6},{1,7},{2,4},{3,5},{4,2},{5,3},{6,0},{7,1},{8,14},{9,15},{10,... | collective-permute-start | bytes 30728 | tf_op jit(solution)/shard_map/ppermute | solution.py:324
  33.9 2.3 %collective-permute-start.9 = (f32[1,2560]{1,0:T(1,128)S(1)}, f32[1,2560]{1,0:T(1,128)S(1)}, u32[]{:S(2)}, u32[]{:S(2)}) collective-permute-start(f32[1,2560]{1,0:T(1,128)S(1)} %add.22.refs_1_), channel_id=1, source_target_pairs={{0,2},{1,3},{2,0},{3,1},{4,6},{5,7},{6,4},{7,5},{8,10},{9,11},{10,... | collective-permute-start | bytes 30728 | tf_op jit(solution)/shard_map/ppermute | solution.py:324
  36.2 1.1 %collective-permute-done.10.refs_4_ = f32[1,2560]{1,0:T(1,128)S(1)} collective-permute-done((f32[1,2560]{1,0:T(1,128)S(1)}, f32[1,2560]{1,0:T(1,128)S(1)}, u32[]{:S(2)}, u32[]{:S(2)}) %collective-permute-start.10) | collective-permute-done | bytes 10272 | tf_op jit(solution)/shard_map/ppermute | solution.py:324
  37.9 5.1 %shard_map.55 = (f32[4096,2048]{1,0:T(8,128)S(1)}, f32[1,2048]{1,0:T(1,128)S(1)}, f32[1,512]{1,0:T(1,128)S(1)}, bf16[528,128]{1,0:T(8,128)(2,1)S(1)}) custom-call(f32[4096,2048]{1,0:T(8,128)S(1)} %get-tuple-element.34.refs_0_, f32[1,2560]{1,0:T(1,128)S(1)} %add.22.refs_1_, ...), custom_call_target="tpu_custom_call", output_to_operand_aliasing={{0}: (0, {})} | custom-call | flops 5000000000 | bytes 1048576 | tf_op jit(solution)/shard_map/pallas_call | solution.py:37
  43.1 1.2 %collective-permute-done.11 = f32[1,2048]{1,0:T(1,128)S(1)} collective-permute-done((f32[1,2048]{1,0:T(1,128)S(1)}, f32[1,2048]{1,0:T(1,128)S(1)}, u32[]{:S(2)}, u32[]{:S(2)}) %collective-permute-start.11) | collective-permute-done | bytes 8224 | tf_op jit(solution)/shard_map/ppermute | solution.py:324
  44.3 2.5 %collective-permute-start.12 = (f32[1,2048]{1,0:T(1,128)S(1)}, f32[1,2048]{1,0:T(1,128)S(1)}, u32[]{:S(2)}, u32[]{:S(2)}) collective-permute-start(f32[1,2048]{1,0:T(1,128)S(1)} %add.23.refs_4_), channel_id=1, source_target_pairs={{0,6},{1,7},{2,4},{3,5},{4,2},{5,3},{6,0},{7,1},{8,14},{9,15},{10,... | collective-permute-start | bytes 24584 | tf_op jit(solution)/shard_map/ppermute | solution.py:324
  47.7 1.0 %collective-permute-start.14 = (f32[1,2048]{1,0:T(1,128)S(1)}, f32[1,2048]{1,0:T(1,128)S(1)}, u32[]{:S(2)}, u32[]{:S(2)}) collective-permute-start(f32[1,2048]{1,0:T(1,128)S(1)} %add.23.refs_4_), channel_id=1, source_target_pairs={{0,2},{1,3},{2,0},{3,1},{4,6},{5,7},{6,4},{7,5},{8,10},{9,11},{10,... | collective-permute-start | bytes 24584 | tf_op jit(solution)/shard_map/ppermute | solution.py:324
  48.8 2.3 %collective-permute-start.19 = (bf16[528,128]{1,0:T(8,128)(2,1)S(1)}, bf16[528,128]{1,0:T(8,128)(2,1)S(1)}, u32[]{:S(2)}, u32[]{:S(2)}) collective-permute-start(bf16[528,128]{1,0:T(8,128)(2,1)S(1)} %get-tuple-element.45), channel_id=1, source_target_pairs={{0,24},{8,16},{16,8},{24,0},{1,25},{9,17},{17,9},{25,1},{2,26},{10... | collective-permute-start | bytes 405512 | tf_op jit(solution)/shard_map/ppermute | solution.py:324
  52.3 2.5 %shard_map.56 = (f32[4096,2048]{1,0:T(8,128)S(1)}, f32[256,128]{1,0:T(8,128)S(1)}, f32[256,128]{1,0:T(8,128)S(1)}, f32[1,2048]{1,0:T(1,128)S(1)}, bf16[4096,512]{1,0:T(8,128)(2,1)S(1)}) custom-call(f32[4096,2048]{1,0:T(8,128)S(1)} %get-tuple-element.37.refs_0_, ...), custom_call_target="tpu_custom_call", output_to_operand_aliasing={{0}: (0, {})} | custom-call | flops 4000000000 | bytes 1048576 | tf_op jit(solution)/shard_map/pallas_call | solution.py:37
  54.8 1.3 %collective-permute-done.15 = f32[256,128]{1,0:T(8,128)S(1)} collective-permute-done((f32[256,128]{1,0:T(8,128)S(1)}, f32[256,128]{1,0:T(8,128)S(1)}, u32[]{:S(2)}, u32[]{:S(2)}) %collective-permute-start.15) | collective-permute-done | bytes 131104 | tf_op jit(solution)/shard_map/ppermute | solution.py:324
  56.2 2.5 %collective-permute-start.16 = (f32[256,128]{1,0:T(8,128)S(1)}, f32[256,128]{1,0:T(8,128)S(1)}, u32[]{:S(2)}, u32[]{:S(2)}) collective-permute-start(f32[256,128]{1,0:T(8,128)S(1)} %add.24), channel_id=1, source_target_pairs={{0,6},{1,7},{2,4},{3,5},{4,2},{5,3},{6,0},{7,1},{8,14},{9,15},{10,... | collective-permute-start | bytes 393224 | tf_op jit(solution)/shard_map/ppermute | solution.py:324
  58.7 1.9 %collective-permute-start.18 = (f32[256,128]{1,0:T(8,128)S(1)}, f32[256,128]{1,0:T(8,128)S(1)}, u32[]{:S(2)}, u32[]{:S(2)}) collective-permute-start(f32[256,128]{1,0:T(8,128)S(1)} %add.24), channel_id=1, source_target_pairs={{0,2},{1,3},{2,0},{3,1},{4,6},{5,7},{6,4},{7,5},{8,10},{9,11},{10,... | collective-permute-start | bytes 393224 | tf_op jit(solution)/shard_map/ppermute | solution.py:324
  60.6 9.8 %shard_map.57 = f32[4096,128]{1,0:T(8,128)} custom-call(f32[4096,2048]{1,0:T(8,128)S(1)} %get-tuple-element.42.refs_0_, bf16[4096,128]{1,0:T(8,128)(2,1)S(1)} %get-tuple-element.26.centre_ref.refs_1_, bf16[512,128]{1,0:T(8,128)(2,1)S(1)} %get-tuple-element.36.refs_5_.refs_2_, f32[1,2048]{1,0:T(1,128)S(1)} %get-tuple-element.43.refs_3_, ...), custom_call_target="tpu_custom_call" | custom-call | flops 10000000000 | bytes 1048576 | tf_op jit(solution)/shard_map/pallas_call | solution.py:37
  70.8 1.3 %collective-permute-done.22 = f32[256,128]{1,0:T(8,128)S(1)} collective-permute-done((f32[256,128]{1,0:T(8,128)S(1)}, f32[256,128]{1,0:T(8,128)S(1)}, u32[]{:S(2)}, u32[]{:S(2)}) %collective-permute-start.22) | collective-permute-done | bytes 131104 | tf_op jit(solution)/shard_map/ppermute | solution.py:324
  (38 shorter events, 7.5 us)
Async XLA Ops:
  0.6 8.2 %collective-permute-start = (bf16[512,128]{1,0:T(8,128)(2,1)}, bf16[512,128]{1,0:T(8,128)(2,1)S(1)}, u32[]{:S(2)}, u32[]{:S(2)}) collective-permute-start(bf16[512,128]{1,0:T(8,128)(2,1)} %token_ref.2), channel_id=1, source_target_pairs={{0,24},{8,16},{16,8},{24,0},{1,25},{9,17},{17,9},{25,1},{2,26},{10... | collective-permute-start | bytes 393224 | tf_op jit(solution)/shard_map/ppermute | solution.py:324
  4.6 6.5 %collective-permute-start.1 = (bf16[512,128]{1,0:T(8,128)(2,1)}, bf16[512,128]{1,0:T(8,128)(2,1)S(1)}, u32[]{:S(2)}, u32[]{:S(2)}) collective-permute-start(bf16[512,128]{1,0:T(8,128)(2,1)} %token_ref.2), channel_id=1, source_target_pairs={{0,16},{8,24},{16,0},{24,8},{1,17},{9,25},{17,1},{25,9},{2,18},{10... | collective-permute-start | bytes 393224 | tf_op jit(solution)/shard_map/ppermute | solution.py:324
  5.1 6.3 %collective-permute-start.2 = (bf16[512,128]{1,0:T(8,128)(2,1)}, bf16[512,128]{1,0:T(8,128)(2,1)S(1)}, u32[]{:S(2)}, u32[]{:S(2)}) collective-permute-start(bf16[512,128]{1,0:T(8,128)(2,1)} %token_ref.2), channel_id=1, source_target_pairs={{0,8},{8,0},{16,24},{24,16},{1,9},{9,1},{17,25},{25,17},{2,10},{10... | collective-permute-start | bytes 393224 | tf_op jit(solution)/shard_map/ppermute | solution.py:324
  8.8 13.4 %copy-start = (bf16[512,128]{1,0:T(8,128)(2,1)S(1)}, bf16[512,128]{1,0:T(8,128)(2,1)}, u32[]{:S(2)}) copy-start(bf16[512,128]{1,0:T(8,128)(2,1)} %token_ref.3) | copy-start | bytes 393220
  16.5 1.2 %collective-permute-start.3 = (f32[1,2048]{1,0:T(1,128)S(1)}, f32[1,2048]{1,0:T(1,128)S(1)}, u32[]{:S(2)}, u32[]{:S(2)}) collective-permute-start(f32[1,2048]{1,0:T(1,128)S(1)} %get-tuple-element.32), channel_id=1, source_target_pairs={{0,1},{1,0},{2,3},{3,2},{4,5},{5,4},{6,7},{7,6},{8,9},{9,8},{10,11... | collective-permute-start | bytes 24584 | tf_op jit(solution)/shard_map/ppermute | solution.py:324
  17.7 6.1 %collective-permute-start.4 = (f32[1,2048]{1,0:T(1,128)S(1)}, f32[1,2048]{1,0:T(1,128)S(1)}, u32[]{:S(2)}, u32[]{:S(2)}) collective-permute-start(f32[1,2048]{1,0:T(1,128)S(1)} %add.21.refs_1_), channel_id=1, source_target_pairs={{0,6},{1,7},{2,4},{3,5},{4,2},{5,3},{6,0},{7,1},{8,14},{9,15},{10,... | collective-permute-start | bytes 24584 | tf_op jit(solution)/shard_map/ppermute | solution.py:324
  21.4 4.5 %collective-permute-start.5 = (f32[1,2048]{1,0:T(1,128)S(1)}, f32[1,2048]{1,0:T(1,128)S(1)}, u32[]{:S(2)}, u32[]{:S(2)}) collective-permute-start(f32[1,2048]{1,0:T(1,128)S(1)} %add.21.refs_1_), channel_id=1, source_target_pairs={{0,4},{1,5},{2,6},{3,7},{4,0},{5,1},{6,2},{7,3},{8,12},{9,13},{10,... | collective-permute-start | bytes 24584 | tf_op jit(solution)/shard_map/ppermute | solution.py:324
  21.4 4.5 %collective-permute-start.6 = (f32[1,2048]{1,0:T(1,128)S(1)}, f32[1,2048]{1,0:T(1,128)S(1)}, u32[]{:S(2)}, u32[]{:S(2)}) collective-permute-start(f32[1,2048]{1,0:T(1,128)S(1)} %add.21.refs_1_), channel_id=1, source_target_pairs={{0,2},{1,3},{2,0},{3,1},{4,6},{5,7},{6,4},{7,5},{8,10},{9,11},{10,... | collective-permute-start | bytes 24584 | tf_op jit(solution)/shard_map/ppermute | solution.py:324
  30.5 1.2 %collective-permute-start.7 = (f32[1,2560]{1,0:T(1,128)S(1)}, f32[1,2560]{1,0:T(1,128)S(1)}, u32[]{:S(2)}, u32[]{:S(2)}) collective-permute-start(f32[1,2560]{1,0:T(1,128)S(1)} %get-tuple-element.35), channel_id=1, source_target_pairs={{0,1},{1,0},{2,3},{3,2},{4,5},{5,4},{6,7},{7,6},{8,9},{9,8},{10,11... | collective-permute-start | bytes 30728 | tf_op jit(solution)/shard_map/ppermute | solution.py:324
  31.7 5.6 %collective-permute-start.10 = (f32[1,2560]{1,0:T(1,128)S(1)}, f32[1,2560]{1,0:T(1,128)S(1)}, u32[]{:S(2)}, u32[]{:S(2)}) collective-permute-start(f32[1,2560]{1,0:T(1,128)S(1)} %add.22.refs_1_), channel_id=1, source_target_pairs={{0,6},{1,7},{2,4},{3,5},{4,2},{5,3},{6,0},{7,1},{8,14},{9,15},{10,... | collective-permute-start | bytes 30728 | tf_op jit(solution)/shard_map/ppermute | solution.py:324
  33.2 4.6 %collective-permute-start.8 = (f32[1,2560]{1,0:T(1,128)S(1)}, f32[1,2560]{1,0:T(1,128)S(1)}, u32[]{:S(2)}, u32[]{:S(2)}) collective-permute-start(f32[1,2560]{1,0:T(1,128)S(1)} %add.22.refs_1_), channel_id=1, source_target_pairs={{0,4},{1,5},{2,6},{3,7},{4,0},{5,1},{6,2},{7,3},{8,12},{9,13},{10,... | collective-permute-start | bytes 30728 | tf_op jit(solution)/shard_map/ppermute | solution.py:324
  33.9 4.0 %collective-permute-start.9 = (f32[1,2560]{1,0:T(1,128)S(1)}, f32[1,2560]{1,0:T(1,128)S(1)}, u32[]{:S(2)}, u32[]{:S(2)}) collective-permute-start(f32[1,2560]{1,0:T(1,128)S(1)} %add.22.refs_1_), channel_id=1, source_target_pairs={{0,2},{1,3},{2,0},{3,1},{4,6},{5,7},{6,4},{7,5},{8,10},{9,11},{10,... | collective-permute-start | bytes 30728 | tf_op jit(solution)/shard_map/ppermute | solution.py:324
  43.1 1.2 %collective-permute-start.11 = (f32[1,2048]{1,0:T(1,128)S(1)}, f32[1,2048]{1,0:T(1,128)S(1)}, u32[]{:S(2)}, u32[]{:S(2)}) collective-permute-start(f32[1,2048]{1,0:T(1,128)S(1)} %get-tuple-element.39), channel_id=1, source_target_pairs={{0,1},{1,0},{2,3},{3,2},{4,5},{5,4},{6,7},{7,6},{8,9},{9,8},{10,11... | collective-permute-start | bytes 24584 | tf_op jit(solution)/shard_map/ppermute | solution.py:324
  44.3 7.5 %collective-permute-start.12 = (f32[1,2048]{1,0:T(1,128)S(1)}, f32[1,2048]{1,0:T(1,128)S(1)}, u32[]{:S(2)}, u32[]{:S(2)}) collective-permute-start(f32[1,2048]{1,0:T(1,128)S(1)} %add.23.refs_4_), channel_id=1, source_target_pairs={{0,6},{1,7},{2,4},{3,5},{4,2},{5,3},{6,0},{7,1},{8,14},{9,15},{10,... | collective-permute-start | bytes 24584 | tf_op jit(solution)/shard_map/ppermute | solution.py:324
  46.8 5.4 %collective-permute-start.13 = (f32[1,2048]{1,0:T(1,128)S(1)}, f32[1,2048]{1,0:T(1,128)S(1)}, u32[]{:S(2)}, u32[]{:S(2)}) collective-permute-start(f32[1,2048]{1,0:T(1,128)S(1)} %add.23.refs_4_), channel_id=1, source_target_pairs={{0,4},{1,5},{2,6},{3,7},{4,0},{5,1},{6,2},{7,3},{8,12},{9,13},{10,... | collective-permute-start | bytes 24584 | tf_op jit(solution)/shard_map/ppermute | solution.py:324
  47.7 4.5 %collective-permute-start.14 = (f32[1,2048]{1,0:T(1,128)S(1)}, f32[1,2048]{1,0:T(1,128)S(1)}, u32[]{:S(2)}, u32[]{:S(2)}) collective-permute-start(f32[1,2048]{1,0:T(1,128)S(1)} %add.23.refs_4_), channel_id=1, source_target_pairs={{0,2},{1,3},{2,0},{3,1},{4,6},{5,7},{6,4},{7,5},{8,10},{9,11},{10,... | collective-permute-start | bytes 24584 | tf_op jit(solution)/shard_map/ppermute | solution.py:324
  48.8 10.0 %collective-permute-start.19 = (bf16[528,128]{1,0:T(8,128)(2,1)S(1)}, bf16[528,128]{1,0:T(8,128)(2,1)S(1)}, u32[]{:S(2)}, u32[]{:S(2)}) collective-permute-start(bf16[528,128]{1,0:T(8,128)(2,1)S(1)} %get-tuple-element.45), channel_id=1, source_target_pairs={{0,24},{8,16},{16,8},{24,0},{1,25},{9,17},{17,9},{25,1},{2,26},{10... | collective-permute-start | bytes 405512 | tf_op jit(solution)/shard_map/ppermute | solution.py:324
  51.1 9.5 %collective-permute-start.20 = (bf16[528,128]{1,0:T(8,128)(2,1)S(1)}, bf16[528,128]{1,0:T(8,128)(2,1)S(1)}, u32[]{:S(2)}, u32[]{:S(2)}) collective-permute-start(bf16[528,128]{1,0:T(8,128)(2,1)S(1)} %get-tuple-element.45), channel_id=1, source_target_pairs={{0,16},{8,24},{16,0},{24,8},{1,17},{9,25},{17,1},{25,9},{2,18},{10... | collective-permute-start | bytes 405512 | tf_op jit(solution)/shard_map/ppermute | solution.py:324
  51.8 8.9 %collective-permute-start.21 = (bf16[528,128]{1,0:T(8,128)(2,1)S(1)}, bf16[528,128]{1,0:T(8,128)(2,1)S(1)}, u32[]{:S(2)}, u32[]{:S(2)}) collective-permute-start(bf16[528,128]{1,0:T(8,128)(2,1)S(1)} %get-tuple-element.45), channel_id=1, source_target_pairs={{0,8},{8,0},{16,24},{24,16},{1,9},{9,1},{17,25},{25,17},{2,10},{10... | collective-permute-start | bytes 405512 | tf_op jit(solution)/shard_map/ppermute | solution.py:324
  54.7 1.4 %collective-permute-start.15 = (f32[256,128]{1,0:T(8,128)S(1)}, f32[256,128]{1,0:T(8,128)S(1)}, u32[]{:S(2)}, u32[]{:S(2)}) collective-permute-start(f32[256,128]{1,0:T(8,128)S(1)} %get-tuple-element.41), channel_id=1, source_target_pairs={{0,1},{1,0},{2,3},{3,2},{4,5},{5,4},{6,7},{7,6},{8,9},{9,8},{10,11... | collective-permute-start | bytes 393224 | tf_op jit(solution)/shard_map/ppermute | solution.py:324
  56.2 14.3 %collective-permute-start.16 = (f32[256,128]{1,0:T(8,128)S(1)}, f32[256,128]{1,0:T(8,128)S(1)}, u32[]{:S(2)}, u32[]{:S(2)}) collective-permute-start(f32[256,128]{1,0:T(8,128)S(1)} %add.24), channel_id=1, source_target_pairs={{0,6},{1,7},{2,4},{3,5},{4,2},{5,3},{6,0},{7,1},{8,14},{9,15},{10,... | collective-permute-start | bytes 393224 | tf_op jit(solution)/shard_map/ppermute | solution.py:324
  58.7 12.0 %collective-permute-start.17 = (f32[256,128]{1,0:T(8,128)S(1)}, f32[256,128]{1,0:T(8,128)S(1)}, u32[]{:S(2)}, u32[]{:S(2)}) collective-permute-start(f32[256,128]{1,0:T(8,128)S(1)} %add.24), channel_id=1, source_target_pairs={{0,4},{1,5},{2,6},{3,7},{4,0},{5,1},{6,2},{7,3},{8,12},{9,13},{10,... | collective-permute-start | bytes 393224 | tf_op jit(solution)/shard_map/ppermute | solution.py:324
  58.7 11.9 %collective-permute-start.18 = (f32[256,128]{1,0:T(8,128)S(1)}, f32[256,128]{1,0:T(8,128)S(1)}, u32[]{:S(2)}, u32[]{:S(2)}) collective-permute-start(f32[256,128]{1,0:T(8,128)S(1)} %add.24), channel_id=1, source_target_pairs={{0,2},{1,3},{2,0},{3,1},{4,6},{5,7},{6,4},{7,5},{8,10},{9,11},{10,... | collective-permute-start | bytes 393224 | tf_op jit(solution)/shard_map/ppermute | solution.py:324
  70.7 1.4 %collective-permute-start.22 = (f32[256,128]{1,0:T(8,128)S(1)}, f32[256,128]{1,0:T(8,128)S(1)}, u32[]{:S(2)}, u32[]{:S(2)}) collective-permute-start(f32[256,128]{1,0:T(8,128)S(1)} %add_add_fusion), channel_id=1, source_target_pairs={{0,1},{1,0},{2,3},{3,2},{4,5},{5,4},{6,7},{7,6},{8,9},{9,8},{10,11... | collective-permute-start | bytes 393224 | tf_op jit(solution)/shard_map/ppermute | solution.py:324

commit v9 on v8

--- a/solution.py
+++ b/solution.py
@@ -238,22 +238,23 @@
     return (pred - code * token_scale).astype(BF16)
 
 
-def token_part(*refs, parts, scale, total):
-    centre_ref, tok_ref, weight_ref = refs[1:4]
-    code_ref, mine_ref, other_ref, scale_ref, logit_ref, acc = refs[4 + parts :]
-    own = tok_ref.shape[0]
+def token_half(code_ref, centre_ref, tok_ref, weight_ref, scale_ref, grad_ref, logit_ref, acc, *, scale, total, other):
+    half = tok_ref.shape[0] // 2
     core = lax.rem(lax.axis_index("proto"), 2)
-    scale_ref[...] = total / term_sum(refs[4 : 4 + parts])
+    at_half = part(1 - core if other else core, half)
+    block = block_of("token", code_ref.shape[0])
     acc[...] = jnp.zeros_like(acc)
-    block = block_of("token", code_ref.shape[0])
 
     def fill(i, slot, m):
         at = part(i, block)
-        for c in range(0, own, CHUNK):
-            c = slice(c, min(c + CHUNK, own))
-            logit_ref[at, c] = logit(
-                centre_ref[at, :], tok_ref[c, :], code_ref[at, c], scale_ref[:, c], weight_ref[:, c], scale
-            )
+        logit_ref[at, :] = logit(
+            centre_ref[at, :],
+            tok_ref[at_half, :],
+            code_ref[at, at_half],
+            scale_ref[:, at_half],
+            weight_ref[:, at_half],
+            scale,
+        )
 
     def work(i, slot, m):
         at = part(i, block)
@@ -262,19 +263,30 @@
         )
 
     pipelined(code_ref.shape[0] // block, fill, work)
-    acc[...] = acc[...] * total ** (-0.5)
-    half = own // 2
-    for c in range(2):
-
-        @pl.when(core == c)
-        def _():
-            mine_ref[...] = acc[:, c * half : (c + 1) * half].T
-            other_ref[...] = acc[:, (1 - c) * half : (2 - c) * half].T
+    grad_ref[...] = acc[...].T * total ** (-0.5)
+
+
+def other_half(*refs, parts, scale, total):
+    _, centre_ref, tok_ref, weight_ref = refs[:4]
+    code_ref, grad_ref, logit_ref, scale_ref, acc = refs[4 + parts :]
+    scale_ref[...] = total / term_sum(refs[4 : 4 + parts])
+    token_half(
+        code_ref, centre_ref, tok_ref, weight_ref, scale_ref, grad_ref, logit_ref, acc,
+        scale=scale, total=total, other=True,
+    )
+
+
+def kept_half(_, centre_ref, tok_ref, weight_ref, scale_ref, code_ref, grad_ref, logit_ref, acc, *, scale, total):
+    token_half(
+        code_ref, centre_ref, tok_ref, weight_ref, scale_ref, grad_ref, logit_ref, acc,
+        scale=scale, total=total, other=False,
+    )
 
 
 def proto_part(*refs, parts, scale):
-    (code_ref, centre_ref, tok_ref, scale_ref, logit_ref), packs = refs[:5], refs[5 : 5 + parts]
-    result_ref, tok, weight, out_ref, sems, *slots = refs[5 + parts :]
+    code_ref, centre_ref, tok_ref, scale_ref, kept_ref, other_ref = refs[:6]
+    packs = refs[6 : 6 + parts]
+    result_ref, tok, weight, out_ref, sems, *slots = refs[6 + parts :]
     tokens, own = code_ref.shape[1], tok_ref.shape[0]
     for i, pack in enumerate(packs):
         tok[i * own : (i + 1) * own, :] = pack[:own, :]
@@ -300,7 +312,11 @@
         r = slice(m * size, (m + 1) * size)
         out_ref[r, :] += jnp.dot(slots[slot][r, :], tok[part(i, CHUNK), :], preferred_element_type=F32)
 
-    out_ref[...] = jnp.dot(logit_ref[...], tok_ref[...], preferred_element_type=F32)
+    core = lax.rem(lax.axis_index("proto"), 2)
+    out_ref[...] = sum(
+        jnp.dot(ref[...], tok_ref[part(half, own // 2), :], preferred_element_type=F32)
+        for ref, half in ((kept_ref, core), (other_ref, 1 - core))
+    )
     count = parts * own // CHUNK
     copies = []
 
@@ -427,25 +443,35 @@
     )
     terms = proto_terms(sums)
     packs = others_of(pack, "dp")
-    code, mine, other, token_scale, logits = run(
-        functools.partial(token_part, parts=len(terms), scale=pred_scale, total=total),
-        [shape(own // 2, d), shape(own // 2, d), shape(1, tokens), shape(k, own, dtype=BF16)],
+    code, other, other_logits, token_scale = run(
+        functools.partial(other_half, parts=len(terms), scale=pred_scale, total=total),
+        [shape(own // 2, d), shape(k, own // 2, dtype=BF16), shape(1, tokens)],
         [code, centres, tok, weight] + terms,
-        [pltpu.VMEM((d, own), F32)],
+        [pltpu.VMEM((d, own // 2), F32)],
         resident=list(range(1, 4 + len(terms))),
-        keep=[0, 1, 2, 3],
-        thread=True,
-        us=4,
+        keep=[0, 1, 2],
+        thread=True,
+        us=2,
+    )
+    code, mine, kept_logits = run(
+        functools.partial(kept_half, scale=pred_scale, total=total),
+        [shape(own // 2, d), shape(k, own // 2, dtype=BF16)],
+        [code, centres, tok, weight, token_scale],
+        [pltpu.VMEM((d, own // 2), F32)],
+        resident=list(range(1, 5)),
+        keep=[0, 1],
+        thread=True,
+        us=2,
     )
     mine = chip_sum(mine + swapped(other, "proto", 1))
     (proto_grad,) = run(
         functools.partial(proto_part, parts=parts, scale=pred_scale),
         [shape(k, d)],
-        [code, centres, tok, token_scale, logits] + packs,
+        [code, centres, tok, token_scale, kept_logits, other_logits] + packs,
         [pltpu.VMEM((tokens - own, d), BF16), pltpu.VMEM((1, tokens - own), F32)]
         + [pltpu.VMEM((k, d), F32), pltpu.SemaphoreType.DMA((COPIES,))]
         + [pltpu.VMEM((k, CHUNK), BF16)] * 2,
-        resident=range(5 + parts),
+        resident=range(6 + parts),
         copied=[0],
         us=10,
     )

time: 73 us -> 72.3 us (level)
  waiting for transfers between devices: 11.7 us -> 10.6 us
    ppermute x23, waiting for transfers between devices: 11.7 us -> 10.6 us  [swapped(): lax.ppermute(x, axis, [(i, i ^ mask) for i in range(lax.axis_size(axis))])]
    pallas_call x8 -> x9, Pallas kernels: 33.4 us -> 33.6 us  [run(): pl.pallas_call(body, out_shape=tuple((pltpu.VMEM(s.shape, s.dtype) if i i...]
  transfers between devices with their start and end apart: 23 -> 23, of which waited for: 13 -> 12; matrix products, arithmetic and copies ran while one was open for 0% -> 0% of each run, Pallas kernels for 26% -> 26%
where the time goes in v9:
time: 72.3 us; the launch traced here: 72.1 us
  Pallas kernels  33.6 us (46%)
  starting transfers between devices  26.3 us (36%)
  waiting for transfers between devices  10.6 us (15%)
  other arithmetic  0.8 us (1%)
  between operations  0.8 us (1%)
    pallas_call x9, Pallas kernels, run(): pl.pallas_call(body, out_shape=tuple((pltpu.VMEM(s.shape, s.dtype) if i i...  33.6 us
    ppermute x23, starting transfers between devices, swapped(): lax.ppermute(x, axis, [(i, i ^ mask) for i in range(lax.axis_size(axis))])  26.3 us
    ppermute x23, waiting for transfers between devices, swapped(): lax.ppermute(x, axis, [(i, i ^ mask) for i in range(lax.axis_size(axis))])  10.6 us
  transfers between devices with their start and end apart: 23, of which 12 were waited for; matrix products, arithmetic and copies ran while one was open for 0% of the time, Pallas kernels for 26%

profile of v9, /device:TPU:0, one launch (start us, length us, event | category | flops | bytes accessed | tf_op | source)
XLA Modules:
  0.0 72.1 jit_solution(9602621686657171988)
XLA Ops:
  0.6 4.0 %collective-permute-start = (bf16[512,128]{1,0:T(8,128)(2,1)}, bf16[512,128]{1,0:T(8,128)(2,1)S(1)}, u32[]{:S(2)}, u32[]{:S(2)}) collective-permute-start(bf16[512,128]{1,0:T(8,128)(2,1)} %token_ref.2), channel_id=1, source_target_pairs={{0,24},{8,16},{16,8},{24,0},{1,25},{9,17},{17,9},{25,1},{2,26},{10... | collective-permute-start | bytes 393224 | tf_op jit(solution)/shard_map/ppermute | solution.py:340
  5.2 3.2 %shard_map.50 = (f32[4096,2048]{1,0:T(8,128)S(1)}, bf16[4096,128]{1,0:T(8,128)(2,1)S(1)}, f32[4096,128]{1,0:T(8,128)S(1)}) custom-call(bf16[4096,128]{1,0:T(8,128)(2,1)} %proto_ref.1, bf16[512,128]{1,0:T(8,128)(2,1)} %token_ref.2), custom_call_target="tpu_custom_call" | custom-call | flops 3000000000 | bytes 1048576 | tf_op jit(solution)/shard_map/pallas_call | solution.py:37
  8.8 1.6 %shard_map.51 = (f32[4096,2048]{1,0:T(8,128)S(1)}, f32[4096,128]{1,0:T(8,128)S(1)}) custom-call(f32[4096,2048]{1,0:T(8,128)S(1)} %get-tuple-element.27._, bf16[4096,128]{1,0:T(8,128)(2,1)S(1)} %get-tuple-element.28.centre_ref.refs_1_, f32[4096,128]{1,0:T(8,128)S(1)} %get-tuple-element.29.column_ref, ...), custom_call_target="tpu_custom_call", output_to_operand_aliasing={{0}: (0, {})} | custom-call | flops 2000000000 | bytes 1048576 | tf_op jit(solution)/shard_map/pallas_call | solution.py:37
  11.4 5.1 %shard_map.52 = (f32[4096,2048]{1,0:T(8,128)S(1)}, f32[1,2048]{1,0:T(1,128)S(1)}) custom-call(f32[4096,2048]{1,0:T(8,128)S(1)} %get-tuple-element.30.refs_0_, bf16[4096,128]{1,0:T(8,128)(2,1)S(1)} %get-tuple-element.28.centre_ref.refs_1_, f32[4096,128]{1,0:T(8,128)S(1)} %get-tuple-element.31.refs_2_, ...), custom_call_target="tpu_custom_call", output_to_operand_aliasing={{0}: (0, {})} | custom-call | flops 7000000000 | bytes 1048576 | tf_op jit(solution)/shard_map/pallas_call | solution.py:37
  16.6 1.2 %collective-permute-done.3 = f32[1,2048]{1,0:T(1,128)S(1)} collective-permute-done((f32[1,2048]{1,0:T(1,128)S(1)}, f32[1,2048]{1,0:T(1,128)S(1)}, u32[]{:S(2)}, u32[]{:S(2)}) %collective-permute-start.3) | collective-permute-done | bytes 8224 | tf_op jit(solution)/shard_map/ppermute | solution.py:340
  17.7 3.7 %collective-permute-start.4 = (f32[1,2048]{1,0:T(1,128)S(1)}, f32[1,2048]{1,0:T(1,128)S(1)}, u32[]{:S(2)}, u32[]{:S(2)}) collective-permute-start(f32[1,2048]{1,0:T(1,128)S(1)} %add.21.refs_1_), channel_id=1, source_target_pairs={{0,6},{1,7},{2,4},{3,5},{4,2},{5,3},{6,0},{7,1},{8,14},{9,15},{10,... | collective-permute-start | bytes 24584 | tf_op jit(solution)/shard_map/ppermute | solution.py:340
  22.2 1.6 %shard_map.53 = (f32[4096,2048]{1,0:T(8,128)S(1)}, bf16[512,128]{1,0:T(8,128)(2,1)S(1)}, f32[1,512]{1,0:T(1,128)S(1)}) custom-call(f32[4096,2048]{1,0:T(8,128)S(1)} %get-tuple-element.32._, bf16[4096,128]{1,0:T(8,128)(2,1)S(1)} %get-tuple-element.28.centre_ref.refs_1_, bf16[512,128]{1,0:T(8,128)(2,1)S(1)} %copy-done), custom_call_target="tpu_custom_call", output_to_operand_aliasing={{0}: (0, {})} | custom-call | flops 2000000000 | bytes 1048576 | tf_op jit(solution)/shard_map/pallas_call | solution.py:37
  23.8 2.2 %collective-permute-done.5.refs_3_ = f32[1,2048]{1,0:T(1,128)S(1)} collective-permute-done((f32[1,2048]{1,0:T(1,128)S(1)}, f32[1,2048]{1,0:T(1,128)S(1)}, u32[]{:S(2)}, u32[]{:S(2)}) %collective-permute-start.5) | collective-permute-done | bytes 8224 | tf_op jit(solution)/shard_map/ppermute | solution.py:340
  25.9 4.5 %shard_map.54 = (f32[4096,2048]{1,0:T(8,128)S(1)}, f32[1,2560]{1,0:T(1,128)S(1)}) custom-call(f32[4096,2048]{1,0:T(8,128)S(1)} %get-tuple-element.33.refs_0_, f32[1,2048]{1,0:T(1,128)S(1)} %add.21.refs_1_, f32[1,2048]{1,0:T(1,128)S(1)} %collective-permute-done.4.refs_2_, ...), custom_call_target="tpu_custom_call", output_to_operand_aliasing={{0}: (0, {})} | custom-call | flops 5000000000 | bytes 1048576 | tf_op jit(solution)/shard_map/pallas_call | solution.py:37
  30.5 1.2 %collective-permute-done.7 = f32[1,2560]{1,0:T(1,128)S(1)} collective-permute-done((f32[1,2560]{1,0:T(1,128)S(1)}, f32[1,2560]{1,0:T(1,128)S(1)}, u32[]{:S(2)}, u32[]{:S(2)}) %collective-permute-start.7) | collective-permute-done | bytes 10272 | tf_op jit(solution)/shard_map/ppermute | solution.py:340
  31.7 1.5 %collective-permute-start.10 = (f32[1,2560]{1,0:T(1,128)S(1)}, f32[1,2560]{1,0:T(1,128)S(1)}, u32[]{:S(2)}, u32[]{:S(2)}) collective-permute-start(f32[1,2560]{1,0:T(1,128)S(1)} %add.22.refs_1_), channel_id=1, source_target_pairs={{0,6},{1,7},{2,4},{3,5},{4,2},{5,3},{6,0},{7,1},{8,14},{9,15},{10,... | collective-permute-start | bytes 30728 | tf_op jit(solution)/shard_map/ppermute | solution.py:340
  33.9 2.3 %collective-permute-start.9 = (f32[1,2560]{1,0:T(1,128)S(1)}, f32[1,2560]{1,0:T(1,128)S(1)}, u32[]{:S(2)}, u32[]{:S(2)}) collective-permute-start(f32[1,2560]{1,0:T(1,128)S(1)} %add.22.refs_1_), channel_id=1, source_target_pairs={{0,2},{1,3},{2,0},{3,1},{4,6},{5,7},{6,4},{7,5},{8,10},{9,11},{10,... | collective-permute-start | bytes 30728 | tf_op jit(solution)/shard_map/ppermute | solution.py:340
  36.2 1.1 %collective-permute-done.10.refs_4_ = f32[1,2560]{1,0:T(1,128)S(1)} collective-permute-done((f32[1,2560]{1,0:T(1,128)S(1)}, f32[1,2560]{1,0:T(1,128)S(1)}, u32[]{:S(2)}, u32[]{:S(2)}) %collective-permute-start.10) | collective-permute-done | bytes 10272 | tf_op jit(solution)/shard_map/ppermute | solution.py:340
  37.9 5.1 %shard_map.55 = (f32[4096,2048]{1,0:T(8,128)S(1)}, f32[1,2048]{1,0:T(1,128)S(1)}, f32[1,512]{1,0:T(1,128)S(1)}, bf16[528,128]{1,0:T(8,128)(2,1)S(1)}) custom-call(f32[4096,2048]{1,0:T(8,128)S(1)} %get-tuple-element.36.refs_0_, f32[1,2560]{1,0:T(1,128)S(1)} %add.22.refs_1_, ...), custom_call_target="tpu_custom_call", output_to_operand_aliasing={{0}: (0, {})} | custom-call | flops 5000000000 | bytes 1048576 | tf_op jit(solution)/shard_map/pallas_call | solution.py:37
  43.1 1.2 %collective-permute-done.11 = f32[1,2048]{1,0:T(1,128)S(1)} collective-permute-done((f32[1,2048]{1,0:T(1,128)S(1)}, f32[1,2048]{1,0:T(1,128)S(1)}, u32[]{:S(2)}, u32[]{:S(2)}) %collective-permute-start.11) | collective-permute-done | bytes 8224 | tf_op jit(solution)/shard_map/ppermute | solution.py:340
  44.3 2.5 %collective-permute-start.12 = (f32[1,2048]{1,0:T(1,128)S(1)}, f32[1,2048]{1,0:T(1,128)S(1)}, u32[]{:S(2)}, u32[]{:S(2)}) collective-permute-start(f32[1,2048]{1,0:T(1,128)S(1)} %add.23.refs_4_), channel_id=1, source_target_pairs={{0,6},{1,7},{2,4},{3,5},{4,2},{5,3},{6,0},{7,1},{8,14},{9,15},{10,... | collective-permute-start | bytes 24584 | tf_op jit(solution)/shard_map/ppermute | solution.py:340
  47.7 1.0 %collective-permute-start.14 = (f32[1,2048]{1,0:T(1,128)S(1)}, f32[1,2048]{1,0:T(1,128)S(1)}, u32[]{:S(2)}, u32[]{:S(2)}) collective-permute-start(f32[1,2048]{1,0:T(1,128)S(1)} %add.23.refs_4_), channel_id=1, source_target_pairs={{0,2},{1,3},{2,0},{3,1},{4,6},{5,7},{6,4},{7,5},{8,10},{9,11},{10,... | collective-permute-start | bytes 24584 | tf_op jit(solution)/shard_map/ppermute | solution.py:340
  48.8 2.3 %collective-permute-start.19 = (bf16[528,128]{1,0:T(8,128)(2,1)S(1)}, bf16[528,128]{1,0:T(8,128)(2,1)S(1)}, u32[]{:S(2)}, u32[]{:S(2)}) collective-permute-start(bf16[528,128]{1,0:T(8,128)(2,1)S(1)} %get-tuple-element.49), channel_id=1, source_target_pairs={{0,24},{8,16},{16,8},{24,0},{1,25},{9,17},{17,9},{25,1},{2,26},{10... | collective-permute-start | bytes 405512 | tf_op jit(solution)/shard_map/ppermute | solution.py:340
  52.3 1.4 %shard_map.56 = (f32[4096,2048]{1,0:T(8,128)S(1)}, f32[256,128]{1,0:T(8,128)S(1)}, bf16[4096,256]{1,0:T(8,128)(2,1)S(1)}, f32[1,2048]{1,0:T(1,128)S(1)}) custom-call(f32[4096,2048]{1,0:T(8,128)S(1)} %get-tuple-element.39.refs_0_, bf16[4096,128]{1,0:T(8,128)(2,1)S(1)} %get-tuple-element.28.centre_ref.refs_1_, ...), custom_call_target="tpu_custom_call", output_to_operand_aliasing={{0}: (0, {})} | custom-call | flops 2000000000 | bytes 1048576 | tf_op jit(solution)/shard_map/pallas_call | solution.py:37
  53.7 1.4 %shard_map.57 = (f32[4096,2048]{1,0:T(8,128)S(1)}, f32[256,128]{1,0:T(8,128)S(1)}, bf16[4096,256]{1,0:T(8,128)(2,1)S(1)}) custom-call(f32[4096,2048]{1,0:T(8,128)S(1)} %get-tuple-element.42._, bf16[4096,128]{1,0:T(8,128)(2,1)S(1)} %get-tuple-element.28.centre_ref.refs_1_, ...), custom_call_target="tpu_custom_call", output_to_operand_aliasing={{0}: (0, {})} | custom-call | flops 2000000000 | bytes 1048576 | tf_op jit(solution)/shard_map/pallas_call | solution.py:37
  55.2 2.5 %collective-permute-start.16 = (f32[256,128]{1,0:T(8,128)S(1)}, f32[256,128]{1,0:T(8,128)S(1)}, u32[]{:S(2)}, u32[]{:S(2)}) collective-permute-start(f32[256,128]{1,0:T(8,128)S(1)} %add.24), channel_id=1, source_target_pairs={{0,6},{1,7},{2,4},{3,5},{4,2},{5,3},{6,0},{7,1},{8,14},{9,15},{10,... | collective-permute-start | bytes 393224 | tf_op jit(solution)/shard_map/ppermute | solution.py:340
  57.7 1.9 %collective-permute-start.18 = (f32[256,128]{1,0:T(8,128)S(1)}, f32[256,128]{1,0:T(8,128)S(1)}, u32[]{:S(2)}, u32[]{:S(2)}) collective-permute-start(f32[256,128]{1,0:T(8,128)S(1)} %add.24), channel_id=1, source_target_pairs={{0,2},{1,3},{2,0},{3,1},{4,6},{5,7},{6,4},{7,5},{8,10},{9,11},{10,... | collective-permute-start | bytes 393224 | tf_op jit(solution)/shard_map/ppermute | solution.py:340
  59.6 9.8 %shard_map.58 = f32[4096,128]{1,0:T(8,128)} custom-call(f32[4096,2048]{1,0:T(8,128)S(1)} %get-tuple-element.46.refs_0_, bf16[4096,128]{1,0:T(8,128)(2,1)S(1)} %get-tuple-element.28.centre_ref.refs_1_, bf16[512,128]{1,0:T(8,128)(2,1)S(1)} %get-tuple-element.38.refs_5_.refs_2_.tok_ref, f32[1,2048]{1,0:T(1,128)S(1)} %get-tuple-element.43.scale_ref.refs_3_, ...), custom_call_target="tpu_custom_call" | custom-call | flops 10000000000 | bytes 1048576 | tf_op jit(solution)/shard_map/pallas_call | solution.py:37
  70.1 1.3 %collective-permute-done.22 = f32[256,128]{1,0:T(8,128)S(1)} collective-permute-done((f32[256,128]{1,0:T(8,128)S(1)}, f32[256,128]{1,0:T(8,128)S(1)}, u32[]{:S(2)}, u32[]{:S(2)}) %collective-permute-start.22) | collective-permute-done | bytes 131104 | tf_op jit(solution)/shard_map/ppermute | solution.py:340
  (39 shorter events, 7.8 us)
Async XLA Ops:
  0.6 8.2 %collective-permute-start = (bf16[512,128]{1,0:T(8,128)(2,1)}, bf16[512,128]{1,0:T(8,128)(2,1)S(1)}, u32[]{:S(2)}, u32[]{:S(2)}) collective-permute-start(bf16[512,128]{1,0:T(8,128)(2,1)} %token_ref.2), channel_id=1, source_target_pairs={{0,24},{8,16},{16,8},{24,0},{1,25},{9,17},{17,9},{25,1},{2,26},{10... | collective-permute-start | bytes 393224 | tf_op jit(solution)/shard_map/ppermute | solution.py:340
  4.6 6.5 %collective-permute-start.1 = (bf16[512,128]{1,0:T(8,128)(2,1)}, bf16[512,128]{1,0:T(8,128)(2,1)S(1)}, u32[]{:S(2)}, u32[]{:S(2)}) collective-permute-start(bf16[512,128]{1,0:T(8,128)(2,1)} %token_ref.2), channel_id=1, source_target_pairs={{0,16},{8,24},{16,0},{24,8},{1,17},{9,25},{17,1},{25,9},{2,18},{10... | collective-permute-start | bytes 393224 | tf_op jit(solution)/shard_map/ppermute | solution.py:340
  5.1 6.3 %collective-permute-start.2 = (bf16[512,128]{1,0:T(8,128)(2,1)}, bf16[512,128]{1,0:T(8,128)(2,1)S(1)}, u32[]{:S(2)}, u32[]{:S(2)}) collective-permute-start(bf16[512,128]{1,0:T(8,128)(2,1)} %token_ref.2), channel_id=1, source_target_pairs={{0,8},{8,0},{16,24},{24,16},{1,9},{9,1},{17,25},{25,17},{2,10},{10... | collective-permute-start | bytes 393224 | tf_op jit(solution)/shard_map/ppermute | solution.py:340
  8.8 13.4 %copy-start = (bf16[512,128]{1,0:T(8,128)(2,1)S(1)}, bf16[512,128]{1,0:T(8,128)(2,1)}, u32[]{:S(2)}) copy-start(bf16[512,128]{1,0:T(8,128)(2,1)} %token_ref.3) | copy-start | bytes 393220
  16.5 1.2 %collective-permute-start.3 = (f32[1,2048]{1,0:T(1,128)S(1)}, f32[1,2048]{1,0:T(1,128)S(1)}, u32[]{:S(2)}, u32[]{:S(2)}) collective-permute-start(f32[1,2048]{1,0:T(1,128)S(1)} %get-tuple-element.34), channel_id=1, source_target_pairs={{0,1},{1,0},{2,3},{3,2},{4,5},{5,4},{6,7},{7,6},{8,9},{9,8},{10,11... | collective-permute-start | bytes 24584 | tf_op jit(solution)/shard_map/ppermute | solution.py:340
  17.7 6.1 %collective-permute-start.4 = (f32[1,2048]{1,0:T(1,128)S(1)}, f32[1,2048]{1,0:T(1,128)S(1)}, u32[]{:S(2)}, u32[]{:S(2)}) collective-permute-start(f32[1,2048]{1,0:T(1,128)S(1)} %add.21.refs_1_), channel_id=1, source_target_pairs={{0,6},{1,7},{2,4},{3,5},{4,2},{5,3},{6,0},{7,1},{8,14},{9,15},{10,... | collective-permute-start | bytes 24584 | tf_op jit(solution)/shard_map/ppermute | solution.py:340
  21.4 4.5 %collective-permute-start.5 = (f32[1,2048]{1,0:T(1,128)S(1)}, f32[1,2048]{1,0:T(1,128)S(1)}, u32[]{:S(2)}, u32[]{:S(2)}) collective-permute-start(f32[1,2048]{1,0:T(1,128)S(1)} %add.21.refs_1_), channel_id=1, source_target_pairs={{0,4},{1,5},{2,6},{3,7},{4,0},{5,1},{6,2},{7,3},{8,12},{9,13},{10,... | collective-permute-start | bytes 24584 | tf_op jit(solution)/shard_map/ppermute | solution.py:340
  21.4 4.5 %collective-permute-start.6 = (f32[1,2048]{1,0:T(1,128)S(1)}, f32[1,2048]{1,0:T(1,128)S(1)}, u32[]{:S(2)}, u32[]{:S(2)}) collective-permute-start(f32[1,2048]{1,0:T(1,128)S(1)} %add.21.refs_1_), channel_id=1, source_target_pairs={{0,2},{1,3},{2,0},{3,1},{4,6},{5,7},{6,4},{7,5},{8,10},{9,11},{10,... | collective-permute-start | bytes 24584 | tf_op jit(solution)/shard_map/ppermute | solution.py:340
  30.5 1.2 %collective-permute-start.7 = (f32[1,2560]{1,0:T(1,128)S(1)}, f32[1,2560]{1,0:T(1,128)S(1)}, u32[]{:S(2)}, u32[]{:S(2)}) collective-permute-start(f32[1,2560]{1,0:T(1,128)S(1)} %get-tuple-element.37), channel_id=1, source_target_pairs={{0,1},{1,0},{2,3},{3,2},{4,5},{5,4},{6,7},{7,6},{8,9},{9,8},{10,11... | collective-permute-start | bytes 30728 | tf_op jit(solution)/shard_map/ppermute | solution.py:340
  31.7 5.6 %collective-permute-start.10 = (f32[1,2560]{1,0:T(1,128)S(1)}, f32[1,2560]{1,0:T(1,128)S(1)}, u32[]{:S(2)}, u32[]{:S(2)}) collective-permute-start(f32[1,2560]{1,0:T(1,128)S(1)} %add.22.refs_1_), channel_id=1, source_target_pairs={{0,6},{1,7},{2,4},{3,5},{4,2},{5,3},{6,0},{7,1},{8,14},{9,15},{10,... | collective-permute-start | bytes 30728 | tf_op jit(solution)/shard_map/ppermute | solution.py:340
  33.2 4.6 %collective-permute-start.8 = (f32[1,2560]{1,0:T(1,128)S(1)}, f32[1,2560]{1,0:T(1,128)S(1)}, u32[]{:S(2)}, u32[]{:S(2)}) collective-permute-start(f32[1,2560]{1,0:T(1,128)S(1)} %add.22.refs_1_), channel_id=1, source_target_pairs={{0,4},{1,5},{2,6},{3,7},{4,0},{5,1},{6,2},{7,3},{8,12},{9,13},{10,... | collective-permute-start | bytes 30728 | tf_op jit(solution)/shard_map/ppermute | solution.py:340
  33.9 4.0 %collective-permute-start.9 = (f32[1,2560]{1,0:T(1,128)S(1)}, f32[1,2560]{1,0:T(1,128)S(1)}, u32[]{:S(2)}, u32[]{:S(2)}) collective-permute-start(f32[1,2560]{1,0:T(1,128)S(1)} %add.22.refs_1_), channel_id=1, source_target_pairs={{0,2},{1,3},{2,0},{3,1},{4,6},{5,7},{6,4},{7,5},{8,10},{9,11},{10,... | collective-permute-start | bytes 30728 | tf_op jit(solution)/shard_map/ppermute | solution.py:340
  43.1 1.2 %collective-permute-start.11 = (f32[1,2048]{1,0:T(1,128)S(1)}, f32[1,2048]{1,0:T(1,128)S(1)}, u32[]{:S(2)}, u32[]{:S(2)}) collective-permute-start(f32[1,2048]{1,0:T(1,128)S(1)} %get-tuple-element.41), channel_id=1, source_target_pairs={{0,1},{1,0},{2,3},{3,2},{4,5},{5,4},{6,7},{7,6},{8,9},{9,8},{10,11... | collective-permute-start | bytes 24584 | tf_op jit(solution)/shard_map/ppermute | solution.py:340
  44.3 7.5 %collective-permute-start.12 = (f32[1,2048]{1,0:T(1,128)S(1)}, f32[1,2048]{1,0:T(1,128)S(1)}, u32[]{:S(2)}, u32[]{:S(2)}) collective-permute-start(f32[1,2048]{1,0:T(1,128)S(1)} %add.23.refs_4_), channel_id=1, source_target_pairs={{0,6},{1,7},{2,4},{3,5},{4,2},{5,3},{6,0},{7,1},{8,14},{9,15},{10,... | collective-permute-start | bytes 24584 | tf_op jit(solution)/shard_map/ppermute | solution.py:340
  46.8 5.4 %collective-permute-start.13 = (f32[1,2048]{1,0:T(1,128)S(1)}, f32[1,2048]{1,0:T(1,128)S(1)}, u32[]{:S(2)}, u32[]{:S(2)}) collective-permute-start(f32[1,2048]{1,0:T(1,128)S(1)} %add.23.refs_4_), channel_id=1, source_target_pairs={{0,4},{1,5},{2,6},{3,7},{4,0},{5,1},{6,2},{7,3},{8,12},{9,13},{10,... | collective-permute-start | bytes 24584 | tf_op jit(solution)/shard_map/ppermute | solution.py:340
  47.7 4.5 %collective-permute-start.14 = (f32[1,2048]{1,0:T(1,128)S(1)}, f32[1,2048]{1,0:T(1,128)S(1)}, u32[]{:S(2)}, u32[]{:S(2)}) collective-permute-start(f32[1,2048]{1,0:T(1,128)S(1)} %add.23.refs_4_), channel_id=1, source_target_pairs={{0,2},{1,3},{2,0},{3,1},{4,6},{5,7},{6,4},{7,5},{8,10},{9,11},{10,... | collective-permute-start | bytes 24584 | tf_op jit(solution)/shard_map/ppermute | solution.py:340
  48.8 8.9 %collective-permute-start.19 = (bf16[528,128]{1,0:T(8,128)(2,1)S(1)}, bf16[528,128]{1,0:T(8,128)(2,1)S(1)}, u32[]{:S(2)}, u32[]{:S(2)}) collective-permute-start(bf16[528,128]{1,0:T(8,128)(2,1)S(1)} %get-tuple-element.49), channel_id=1, source_target_pairs={{0,24},{8,16},{16,8},{24,0},{1,25},{9,17},{17,9},{25,1},{2,26},{10... | collective-permute-start | bytes 405512 | tf_op jit(solution)/shard_map/ppermute | solution.py:340
  51.1 8.5 %collective-permute-start.20 = (bf16[528,128]{1,0:T(8,128)(2,1)S(1)}, bf16[528,128]{1,0:T(8,128)(2,1)S(1)}, u32[]{:S(2)}, u32[]{:S(2)}) collective-permute-start(bf16[528,128]{1,0:T(8,128)(2,1)S(1)} %get-tuple-element.49), channel_id=1, source_target_pairs={{0,16},{8,24},{16,0},{24,8},{1,17},{9,25},{17,1},{25,9},{2,18},{10... | collective-permute-start | bytes 405512 | tf_op jit(solution)/shard_map/ppermute | solution.py:340
  51.8 7.8 %collective-permute-start.21 = (bf16[528,128]{1,0:T(8,128)(2,1)S(1)}, bf16[528,128]{1,0:T(8,128)(2,1)S(1)}, u32[]{:S(2)}, u32[]{:S(2)}) collective-permute-start(bf16[528,128]{1,0:T(8,128)(2,1)S(1)} %get-tuple-element.49), channel_id=1, source_target_pairs={{0,8},{8,0},{16,24},{24,16},{1,9},{9,1},{17,25},{25,17},{2,10},{10... | collective-permute-start | bytes 405512 | tf_op jit(solution)/shard_map/ppermute | solution.py:340
  53.6 1.5 %collective-permute-start.15 = (f32[256,128]{1,0:T(8,128)S(1)}, f32[256,128]{1,0:T(8,128)S(1)}, u32[]{:S(2)}, u32[]{:S(2)}) collective-permute-start(f32[256,128]{1,0:T(8,128)S(1)} %get-tuple-element.45), channel_id=1, source_target_pairs={{0,1},{1,0},{2,3},{3,2},{4,5},{5,4},{6,7},{7,6},{8,9},{9,8},{10,11... | collective-permute-start | bytes 393224 | tf_op jit(solution)/shard_map/ppermute | solution.py:340
  55.2 14.3 %collective-permute-start.16 = (f32[256,128]{1,0:T(8,128)S(1)}, f32[256,128]{1,0:T(8,128)S(1)}, u32[]{:S(2)}, u32[]{:S(2)}) collective-permute-start(f32[256,128]{1,0:T(8,128)S(1)} %add.24), channel_id=1, source_target_pairs={{0,6},{1,7},{2,4},{3,5},{4,2},{5,3},{6,0},{7,1},{8,14},{9,15},{10,... | collective-permute-start | bytes 393224 | tf_op jit(solution)/shard_map/ppermute | solution.py:340
  57.7 12.3 %collective-permute-start.17 = (f32[256,128]{1,0:T(8,128)S(1)}, f32[256,128]{1,0:T(8,128)S(1)}, u32[]{:S(2)}, u32[]{:S(2)}) collective-permute-start(f32[256,128]{1,0:T(8,128)S(1)} %add.24), channel_id=1, source_target_pairs={{0,4},{1,5},{2,6},{3,7},{4,0},{5,1},{6,2},{7,3},{8,12},{9,13},{10,... | collective-permute-start | bytes 393224 | tf_op jit(solution)/shard_map/ppermute | solution.py:340
  57.7 12.3 %collective-permute-start.18 = (f32[256,128]{1,0:T(8,128)S(1)}, f32[256,128]{1,0:T(8,128)S(1)}, u32[]{:S(2)}, u32[]{:S(2)}) collective-permute-start(f32[256,128]{1,0:T(8,128)S(1)} %add.24), channel_id=1, source_target_pairs={{0,2},{1,3},{2,0},{3,1},{4,6},{5,7},{6,4},{7,5},{8,10},{9,11},{10,... | collective-permute-start | bytes 393224 | tf_op jit(solution)/shard_map/ppermute | solution.py:340
  70.0 1.4 %collective-permute-start.22 = (f32[256,128]{1,0:T(8,128)S(1)}, f32[256,128]{1,0:T(8,128)S(1)}, u32[]{:S(2)}, u32[]{:S(2)}) collective-permute-start(f32[256,128]{1,0:T(8,128)S(1)} %add_add_fusion), channel_id=1, source_target_pairs={{0,1},{1,0},{2,3},{3,2},{4,5},{5,4},{6,7},{7,6},{8,9},{9,8},{10,11... | collective-permute-start | bytes 393224 | tf_op jit(solution)/shard_map/ppermute | solution.py:340

commit v10 on v9

--- a/solution.py
+++ b/solution.py
@@ -397,6 +397,16 @@
         us=2,
     )
     views = views[1:]
+    code, tok, den = run(
+        functools.partial(denominators, scale=pred_scale),
+        [shape(own, d, dtype=BF16), shape(1, own)],
+        [code, centres, alternate_augmentation],
+        [pltpu.VMEM((8, own), F32)],
+        resident=[1],
+        keep=[0, 1],
+        thread=True,
+        us=2,
+    )
     code, sums = run(
         functools.partial(first_pass, parts=len(views), scale=code_scale, total=total),
         [shape(1, tokens)],
@@ -408,16 +418,6 @@
         us=7,
     )
     terms = proto_terms(sums)
-    code, tok, den = run(
-        functools.partial(denominators, scale=pred_scale),
-        [shape(own, d, dtype=BF16), shape(1, own)],
-        [code, centres, alternate_augmentation],
-        [pltpu.VMEM((8, own), F32)],
-        resident=[1],
-        keep=[0, 1],
-        thread=True,
-        us=2,
-    )
     code, sums = run(
         functools.partial(middle_pass, parts=len(terms), total=total),
         [shape(1, tokens + own)],

time: 72.3 us -> 73.3 us (1.014)
  transfers between devices with their start and end apart: 23 -> 23, of which waited for: 12 -> 11; matrix products, arithmetic and copies ran while one was open for 0% -> 0% of each run, Pallas kernels for 26% -> 26%
where the time goes in v10:
time: 73.3 us; the launch traced here: 73.2 us
  Pallas kernels  33.6 us (46%)
  starting transfers between devices  26.6 us (36%)
  waiting for transfers between devices  11.3 us (15%)
  between operations  0.82 us (1%)
  other arithmetic  0.8 us (1%)
    pallas_call x9, Pallas kernels, run(): pl.pallas_call(body, out_shape=tuple((pltpu.VMEM(s.shape, s.dtype) if i i...  33.6 us
    ppermute x23, starting transfers between devices, swapped(): lax.ppermute(x, axis, [(i, i ^ mask) for i in range(lax.axis_size(axis))])  26.6 us
    ppermute x23, waiting for transfers between devices, swapped(): lax.ppermute(x, axis, [(i, i ^ mask) for i in range(lax.axis_size(axis))])  11.3 us
  transfers between devices with their start and end apart: 23, of which 11 were waited for; matrix products, arithmetic and copies ran while one was open for 0% of the time, Pallas kernels for 26%

profile of v10, /device:TPU:0, one launch (start us, length us, event | category | flops | bytes accessed | tf_op | source)
XLA Modules:
  0.0 73.2 jit_solution(7682383532383174448)
XLA Ops:
  0.6 4.0 %collective-permute-start = (bf16[512,128]{1,0:T(8,128)(2,1)}, bf16[512,128]{1,0:T(8,128)(2,1)S(1)}, u32[]{:S(2)}, u32[]{:S(2)}) collective-permute-start(bf16[512,128]{1,0:T(8,128)(2,1)} %token_ref.2), channel_id=1, source_target_pairs={{0,24},{8,16},{16,8},{24,0},{1,25},{9,17},{17,9},{25,1},{2,26},{10... | collective-permute-start | bytes 393224 | tf_op jit(solution)/shard_map/ppermute | solution.py:340
  5.2 3.2 %shard_map.50 = (f32[4096,2048]{1,0:T(8,128)S(1)}, bf16[4096,128]{1,0:T(8,128)(2,1)S(1)}, f32[4096,128]{1,0:T(8,128)S(1)}) custom-call(bf16[4096,128]{1,0:T(8,128)(2,1)} %proto_ref.1, bf16[512,128]{1,0:T(8,128)(2,1)} %token_ref.2), custom_call_target="tpu_custom_call" | custom-call | flops 3000000000 | bytes 1048576 | tf_op jit(solution)/shard_map/pallas_call | solution.py:37
  8.8 1.6 %shard_map.51 = (f32[4096,2048]{1,0:T(8,128)S(1)}, f32[4096,128]{1,0:T(8,128)S(1)}) custom-call(f32[4096,2048]{1,0:T(8,128)S(1)} %get-tuple-element.27._, bf16[4096,128]{1,0:T(8,128)(2,1)S(1)} %get-tuple-element.28.centre_ref.refs_1_, f32[4096,128]{1,0:T(8,128)S(1)} %get-tuple-element.29.column_ref, ...), custom_call_target="tpu_custom_call", output_to_operand_aliasing={{0}: (0, {})} | custom-call | flops 2000000000 | bytes 1048576 | tf_op jit(solution)/shard_map/pallas_call | solution.py:37
  10.4 1.6 %shard_map.52 = (f32[4096,2048]{1,0:T(8,128)S(1)}, bf16[512,128]{1,0:T(8,128)(2,1)S(1)}, f32[1,512]{1,0:T(1,128)S(1)}) custom-call(f32[4096,2048]{1,0:T(8,128)S(1)} %get-tuple-element.30._, bf16[4096,128]{1,0:T(8,128)(2,1)S(1)} %get-tuple-element.28.centre_ref.refs_1_, bf16[512,128]{1,0:T(8,128)(2,1)S(1)} %copy-done), custom_call_target="tpu_custom_call", output_to_operand_aliasing={{0}: (0, {})} | custom-call | flops 2000000000 | bytes 1048576 | tf_op jit(solution)/shard_map/pallas_call | solution.py:37
  12.0 5.1 %shard_map.53 = (f32[4096,2048]{1,0:T(8,128)S(1)}, f32[1,2048]{1,0:T(1,128)S(1)}) custom-call(f32[4096,2048]{1,0:T(8,128)S(1)} %get-tuple-element.31.refs_0_, bf16[4096,128]{1,0:T(8,128)(2,1)S(1)} %get-tuple-element.28.centre_ref.refs_1_, f32[4096,128]{1,0:T(8,128)S(1)} %get-tuple-element.32.refs_2_, ...), custom_call_target="tpu_custom_call", output_to_operand_aliasing={{0}: (0, {})} | custom-call | flops 7000000000 | bytes 1048576 | tf_op jit(solution)/shard_map/pallas_call | solution.py:37
  17.2 1.2 %collective-permute-done.3 = f32[1,2048]{1,0:T(1,128)S(1)} collective-permute-done((f32[1,2048]{1,0:T(1,128)S(1)}, f32[1,2048]{1,0:T(1,128)S(1)}, u32[]{:S(2)}, u32[]{:S(2)}) %collective-permute-start.3) | collective-permute-done | bytes 8224 | tf_op jit(solution)/shard_map/ppermute | solution.py:340
  18.4 3.7 %collective-permute-start.4 = (f32[1,2048]{1,0:T(1,128)S(1)}, f32[1,2048]{1,0:T(1,128)S(1)}, u32[]{:S(2)}, u32[]{:S(2)}) collective-permute-start(f32[1,2048]{1,0:T(1,128)S(1)} %add.21.refs_1_), channel_id=1, source_target_pairs={{0,6},{1,7},{2,4},{3,5},{4,2},{5,3},{6,0},{7,1},{8,14},{9,15},{10,... | collective-permute-start | bytes 24584 | tf_op jit(solution)/shard_map/ppermute | solution.py:340
  22.9 1.1 %collective-permute-done.4.refs_2_ = f32[1,2048]{1,0:T(1,128)S(1)} collective-permute-done((f32[1,2048]{1,0:T(1,128)S(1)}, f32[1,2048]{1,0:T(1,128)S(1)}, u32[]{:S(2)}, u32[]{:S(2)}) %collective-permute-start.4) | collective-permute-done | bytes 8224 | tf_op jit(solution)/shard_map/ppermute | solution.py:340
  23.9 2.7 %collective-permute-done.5.refs_3_ = f32[1,2048]{1,0:T(1,128)S(1)} collective-permute-done((f32[1,2048]{1,0:T(1,128)S(1)}, f32[1,2048]{1,0:T(1,128)S(1)}, u32[]{:S(2)}, u32[]{:S(2)}) %collective-permute-start.5) | collective-permute-done | bytes 8224 | tf_op jit(solution)/shard_map/ppermute | solution.py:340
  26.6 4.5 %shard_map.54 = (f32[4096,2048]{1,0:T(8,128)S(1)}, f32[1,2560]{1,0:T(1,128)S(1)}) custom-call(f32[4096,2048]{1,0:T(8,128)S(1)} %get-tuple-element.33.refs_0_, f32[1,2048]{1,0:T(1,128)S(1)} %add.21.refs_1_, f32[1,2048]{1,0:T(1,128)S(1)} %collective-permute-done.4.refs_2_, ...), custom_call_target="tpu_custom_call", output_to_operand_aliasing={{0}: (0, {})} | custom-call | flops 5000000000 | bytes 1048576 | tf_op jit(solution)/shard_map/pallas_call | solution.py:37
  31.2 1.2 %collective-permute-done.7 = f32[1,2560]{1,0:T(1,128)S(1)} collective-permute-done((f32[1,2560]{1,0:T(1,128)S(1)}, f32[1,2560]{1,0:T(1,128)S(1)}, u32[]{:S(2)}, u32[]{:S(2)}) %collective-permute-start.7) | collective-permute-done | bytes 10272 | tf_op jit(solution)/shard_map/ppermute | solution.py:340
  32.4 1.5 %collective-permute-start.10 = (f32[1,2560]{1,0:T(1,128)S(1)}, f32[1,2560]{1,0:T(1,128)S(1)}, u32[]{:S(2)}, u32[]{:S(2)}) collective-permute-start(f32[1,2560]{1,0:T(1,128)S(1)} %add.22.refs_1_), channel_id=1, source_target_pairs={{0,6},{1,7},{2,4},{3,5},{4,2},{5,3},{6,0},{7,1},{8,14},{9,15},{10,... | collective-permute-start | bytes 30728 | tf_op jit(solution)/shard_map/ppermute | solution.py:340
  34.6 2.3 %collective-permute-start.9 = (f32[1,2560]{1,0:T(1,128)S(1)}, f32[1,2560]{1,0:T(1,128)S(1)}, u32[]{:S(2)}, u32[]{:S(2)}) collective-permute-start(f32[1,2560]{1,0:T(1,128)S(1)} %add.22.refs_1_), channel_id=1, source_target_pairs={{0,2},{1,3},{2,0},{3,1},{4,6},{5,7},{6,4},{7,5},{8,10},{9,11},{10,... | collective-permute-start | bytes 30728 | tf_op jit(solution)/shard_map/ppermute | solution.py:340
  36.9 1.1 %collective-permute-done.10.refs_4_ = f32[1,2560]{1,0:T(1,128)S(1)} collective-permute-done((f32[1,2560]{1,0:T(1,128)S(1)}, f32[1,2560]{1,0:T(1,128)S(1)}, u32[]{:S(2)}, u32[]{:S(2)}) %collective-permute-start.10) | collective-permute-done | bytes 10272 | tf_op jit(solution)/shard_map/ppermute | solution.py:340
  38.6 5.1 %shard_map.55 = (f32[4096,2048]{1,0:T(8,128)S(1)}, f32[1,2048]{1,0:T(1,128)S(1)}, f32[1,512]{1,0:T(1,128)S(1)}, bf16[528,128]{1,0:T(8,128)(2,1)S(1)}) custom-call(f32[4096,2048]{1,0:T(8,128)S(1)} %get-tuple-element.36.refs_0_, f32[1,2560]{1,0:T(1,128)S(1)} %add.22.refs_1_, ...), custom_call_target="tpu_custom_call", output_to_operand_aliasing={{0}: (0, {})} | custom-call | flops 5000000000 | bytes 1048576 | tf_op jit(solution)/shard_map/pallas_call | solution.py:37
  43.8 1.2 %collective-permute-done.11 = f32[1,2048]{1,0:T(1,128)S(1)} collective-permute-done((f32[1,2048]{1,0:T(1,128)S(1)}, f32[1,2048]{1,0:T(1,128)S(1)}, u32[]{:S(2)}, u32[]{:S(2)}) %collective-permute-start.11) | collective-permute-done | bytes 8224 | tf_op jit(solution)/shard_map/ppermute | solution.py:340
  45.0 2.5 %collective-permute-start.12 = (f32[1,2048]{1,0:T(1,128)S(1)}, f32[1,2048]{1,0:T(1,128)S(1)}, u32[]{:S(2)}, u32[]{:S(2)}) collective-permute-start(f32[1,2048]{1,0:T(1,128)S(1)} %add.23.refs_4_), channel_id=1, source_target_pairs={{0,6},{1,7},{2,4},{3,5},{4,2},{5,3},{6,0},{7,1},{8,14},{9,15},{10,... | collective-permute-start | bytes 24584 | tf_op jit(solution)/shard_map/ppermute | solution.py:340
  49.4 3.3 %collective-permute-start.19 = (bf16[528,128]{1,0:T(8,128)(2,1)S(1)}, bf16[528,128]{1,0:T(8,128)(2,1)S(1)}, u32[]{:S(2)}, u32[]{:S(2)}) collective-permute-start(bf16[528,128]{1,0:T(8,128)(2,1)S(1)} %get-tuple-element.49), channel_id=1, source_target_pairs={{0,24},{8,16},{16,8},{24,0},{1,25},{9,17},{17,9},{25,1},{2,26},{10... | collective-permute-start | bytes 405512 | tf_op jit(solution)/shard_map/ppermute | solution.py:340
  53.3 1.4 %shard_map.56 = (f32[4096,2048]{1,0:T(8,128)S(1)}, f32[256,128]{1,0:T(8,128)S(1)}, bf16[4096,256]{1,0:T(8,128)(2,1)S(1)}, f32[1,2048]{1,0:T(1,128)S(1)}) custom-call(f32[4096,2048]{1,0:T(8,128)S(1)} %get-tuple-element.39.refs_0_, bf16[4096,128]{1,0:T(8,128)(2,1)S(1)} %get-tuple-element.28.centre_ref.refs_1_, ...), custom_call_target="tpu_custom_call", output_to_operand_aliasing={{0}: (0, {})} | custom-call | flops 2000000000 | bytes 1048576 | tf_op jit(solution)/shard_map/pallas_call | solution.py:37
  54.8 1.4 %shard_map.57 = (f32[4096,2048]{1,0:T(8,128)S(1)}, f32[256,128]{1,0:T(8,128)S(1)}, bf16[4096,256]{1,0:T(8,128)(2,1)S(1)}) custom-call(f32[4096,2048]{1,0:T(8,128)S(1)} %get-tuple-element.42._, bf16[4096,128]{1,0:T(8,128)(2,1)S(1)} %get-tuple-element.28.centre_ref.refs_1_, ...), custom_call_target="tpu_custom_call", output_to_operand_aliasing={{0}: (0, {})} | custom-call | flops 2000000000 | bytes 1048576 | tf_op jit(solution)/shard_map/pallas_call | solution.py:37
  56.2 2.6 %collective-permute-start.16 = (f32[256,128]{1,0:T(8,128)S(1)}, f32[256,128]{1,0:T(8,128)S(1)}, u32[]{:S(2)}, u32[]{:S(2)}) collective-permute-start(f32[256,128]{1,0:T(8,128)S(1)} %add.24), channel_id=1, source_target_pairs={{0,6},{1,7},{2,4},{3,5},{4,2},{5,3},{6,0},{7,1},{8,14},{9,15},{10,... | collective-permute-start | bytes 393224 | tf_op jit(solution)/shard_map/ppermute | solution.py:340
  58.7 1.9 %collective-permute-start.18 = (f32[256,128]{1,0:T(8,128)S(1)}, f32[256,128]{1,0:T(8,128)S(1)}, u32[]{:S(2)}, u32[]{:S(2)}) collective-permute-start(f32[256,128]{1,0:T(8,128)S(1)} %add.24), channel_id=1, source_target_pairs={{0,2},{1,3},{2,0},{3,1},{4,6},{5,7},{6,4},{7,5},{8,10},{9,11},{10,... | collective-permute-start | bytes 393224 | tf_op jit(solution)/shard_map/ppermute | solution.py:340
  60.6 9.8 %shard_map.58 = f32[4096,128]{1,0:T(8,128)} custom-call(f32[4096,2048]{1,0:T(8,128)S(1)} %get-tuple-element.46.refs_0_, bf16[4096,128]{1,0:T(8,128)(2,1)S(1)} %get-tuple-element.28.centre_ref.refs_1_, bf16[512,128]{1,0:T(8,128)(2,1)S(1)} %get-tuple-element.38.refs_5_.refs_2_.tok_ref, f32[1,2048]{1,0:T(1,128)S(1)} %get-tuple-element.43.scale_ref.refs_3_, ...), custom_call_target="tpu_custom_call" | custom-call | flops 10000000000 | bytes 1048576 | tf_op jit(solution)/shard_map/pallas_call | solution.py:37
  71.1 1.3 %collective-permute-done.22 = f32[256,128]{1,0:T(8,128)S(1)} collective-permute-done((f32[256,128]{1,0:T(8,128)S(1)}, f32[256,128]{1,0:T(8,128)S(1)}, u32[]{:S(2)}, u32[]{:S(2)}) %collective-permute-start.22) | collective-permute-done | bytes 131104 | tf_op jit(solution)/shard_map/ppermute | solution.py:340
  (39 shorter events, 7.3 us)
Async XLA Ops:
  0.6 9.8 %copy-start = (bf16[512,128]{1,0:T(8,128)(2,1)S(1)}, bf16[512,128]{1,0:T(8,128)(2,1)}, u32[]{:S(2)}) copy-start(bf16[512,128]{1,0:T(8,128)(2,1)} %token_ref.3) | copy-start | bytes 393220
  0.6 8.2 %collective-permute-start = (bf16[512,128]{1,0:T(8,128)(2,1)}, bf16[512,128]{1,0:T(8,128)(2,1)S(1)}, u32[]{:S(2)}, u32[]{:S(2)}) collective-permute-start(bf16[512,128]{1,0:T(8,128)(2,1)} %token_ref.2), channel_id=1, source_target_pairs={{0,24},{8,16},{16,8},{24,0},{1,25},{9,17},{17,9},{25,1},{2,26},{10... | collective-permute-start | bytes 393224 | tf_op jit(solution)/shard_map/ppermute | solution.py:340
  4.6 7.4 %collective-permute-start.1 = (bf16[512,128]{1,0:T(8,128)(2,1)}, bf16[512,128]{1,0:T(8,128)(2,1)S(1)}, u32[]{:S(2)}, u32[]{:S(2)}) collective-permute-start(bf16[512,128]{1,0:T(8,128)(2,1)} %token_ref.2), channel_id=1, source_target_pairs={{0,16},{8,24},{16,0},{24,8},{1,17},{9,25},{17,1},{25,9},{2,18},{10... | collective-permute-start | bytes 393224 | tf_op jit(solution)/shard_map/ppermute | solution.py:340
  5.1 6.9 %collective-permute-start.2 = (bf16[512,128]{1,0:T(8,128)(2,1)}, bf16[512,128]{1,0:T(8,128)(2,1)S(1)}, u32[]{:S(2)}, u32[]{:S(2)}) collective-permute-start(bf16[512,128]{1,0:T(8,128)(2,1)} %token_ref.2), channel_id=1, source_target_pairs={{0,8},{8,0},{16,24},{24,16},{1,9},{9,1},{17,25},{25,17},{2,10},{10... | collective-permute-start | bytes 393224 | tf_op jit(solution)/shard_map/ppermute | solution.py:340
  17.2 1.2 %collective-permute-start.3 = (f32[1,2048]{1,0:T(1,128)S(1)}, f32[1,2048]{1,0:T(1,128)S(1)}, u32[]{:S(2)}, u32[]{:S(2)}) collective-permute-start(f32[1,2048]{1,0:T(1,128)S(1)} %get-tuple-element.34), channel_id=1, source_target_pairs={{0,1},{1,0},{2,3},{3,2},{4,5},{5,4},{6,7},{7,6},{8,9},{9,8},{10,11... | collective-permute-start | bytes 24584 | tf_op jit(solution)/shard_map/ppermute | solution.py:340
  18.4 5.5 %collective-permute-start.4 = (f32[1,2048]{1,0:T(1,128)S(1)}, f32[1,2048]{1,0:T(1,128)S(1)}, u32[]{:S(2)}, u32[]{:S(2)}) collective-permute-start(f32[1,2048]{1,0:T(1,128)S(1)} %add.21.refs_1_), channel_id=1, source_target_pairs={{0,6},{1,7},{2,4},{3,5},{4,2},{5,3},{6,0},{7,1},{8,14},{9,15},{10,... | collective-permute-start | bytes 24584 | tf_op jit(solution)/shard_map/ppermute | solution.py:340
  22.1 4.5 %collective-permute-start.5 = (f32[1,2048]{1,0:T(1,128)S(1)}, f32[1,2048]{1,0:T(1,128)S(1)}, u32[]{:S(2)}, u32[]{:S(2)}) collective-permute-start(f32[1,2048]{1,0:T(1,128)S(1)} %add.21.refs_1_), channel_id=1, source_target_pairs={{0,4},{1,5},{2,6},{3,7},{4,0},{5,1},{6,2},{7,3},{8,12},{9,13},{10,... | collective-permute-start | bytes 24584 | tf_op jit(solution)/shard_map/ppermute | solution.py:340
  22.1 4.5 %collective-permute-start.6 = (f32[1,2048]{1,0:T(1,128)S(1)}, f32[1,2048]{1,0:T(1,128)S(1)}, u32[]{:S(2)}, u32[]{:S(2)}) collective-permute-start(f32[1,2048]{1,0:T(1,128)S(1)} %add.21.refs_1_), channel_id=1, source_target_pairs={{0,2},{1,3},{2,0},{3,1},{4,6},{5,7},{6,4},{7,5},{8,10},{9,11},{10,... | collective-permute-start | bytes 24584 | tf_op jit(solution)/shard_map/ppermute | solution.py:340
  31.1 1.2 %collective-permute-start.7 = (f32[1,2560]{1,0:T(1,128)S(1)}, f32[1,2560]{1,0:T(1,128)S(1)}, u32[]{:S(2)}, u32[]{:S(2)}) collective-permute-start(f32[1,2560]{1,0:T(1,128)S(1)} %get-tuple-element.37), channel_id=1, source_target_pairs={{0,1},{1,0},{2,3},{3,2},{4,5},{5,4},{6,7},{7,6},{8,9},{9,8},{10,11... | collective-permute-start | bytes 30728 | tf_op jit(solution)/shard_map/ppermute | solution.py:340
  32.4 5.6 %collective-permute-start.10 = (f32[1,2560]{1,0:T(1,128)S(1)}, f32[1,2560]{1,0:T(1,128)S(1)}, u32[]{:S(2)}, u32[]{:S(2)}) collective-permute-start(f32[1,2560]{1,0:T(1,128)S(1)} %add.22.refs_1_), channel_id=1, source_target_pairs={{0,6},{1,7},{2,4},{3,5},{4,2},{5,3},{6,0},{7,1},{8,14},{9,15},{10,... | collective-permute-start | bytes 30728 | tf_op jit(solution)/shard_map/ppermute | solution.py:340
  33.9 4.6 %collective-permute-start.8 = (f32[1,2560]{1,0:T(1,128)S(1)}, f32[1,2560]{1,0:T(1,128)S(1)}, u32[]{:S(2)}, u32[]{:S(2)}) collective-permute-start(f32[1,2560]{1,0:T(1,128)S(1)} %add.22.refs_1_), channel_id=1, source_target_pairs={{0,4},{1,5},{2,6},{3,7},{4,0},{5,1},{6,2},{7,3},{8,12},{9,13},{10,... | collective-permute-start | bytes 30728 | tf_op jit(solution)/shard_map/ppermute | solution.py:340
  34.6 4.0 %collective-permute-start.9 = (f32[1,2560]{1,0:T(1,128)S(1)}, f32[1,2560]{1,0:T(1,128)S(1)}, u32[]{:S(2)}, u32[]{:S(2)}) collective-permute-start(f32[1,2560]{1,0:T(1,128)S(1)} %add.22.refs_1_), channel_id=1, source_target_pairs={{0,2},{1,3},{2,0},{3,1},{4,6},{5,7},{6,4},{7,5},{8,10},{9,11},{10,... | collective-permute-start | bytes 30728 | tf_op jit(solution)/shard_map/ppermute | solution.py:340
  43.7 1.2 %collective-permute-start.11 = (f32[1,2048]{1,0:T(1,128)S(1)}, f32[1,2048]{1,0:T(1,128)S(1)}, u32[]{:S(2)}, u32[]{:S(2)}) collective-permute-start(f32[1,2048]{1,0:T(1,128)S(1)} %get-tuple-element.41), channel_id=1, source_target_pairs={{0,1},{1,0},{2,3},{3,2},{4,5},{5,4},{6,7},{7,6},{8,9},{9,8},{10,11... | collective-permute-start | bytes 24584 | tf_op jit(solution)/shard_map/ppermute | solution.py:340
  45.0 8.2 %collective-permute-start.12 = (f32[1,2048]{1,0:T(1,128)S(1)}, f32[1,2048]{1,0:T(1,128)S(1)}, u32[]{:S(2)}, u32[]{:S(2)}) collective-permute-start(f32[1,2048]{1,0:T(1,128)S(1)} %add.23.refs_4_), channel_id=1, source_target_pairs={{0,6},{1,7},{2,4},{3,5},{4,2},{5,3},{6,0},{7,1},{8,14},{9,15},{10,... | collective-permute-start | bytes 24584 | tf_op jit(solution)/shard_map/ppermute | solution.py:340
  47.5 5.8 %collective-permute-start.13 = (f32[1,2048]{1,0:T(1,128)S(1)}, f32[1,2048]{1,0:T(1,128)S(1)}, u32[]{:S(2)}, u32[]{:S(2)}) collective-permute-start(f32[1,2048]{1,0:T(1,128)S(1)} %add.23.refs_4_), channel_id=1, source_target_pairs={{0,4},{1,5},{2,6},{3,7},{4,0},{5,1},{6,2},{7,3},{8,12},{9,13},{10,... | collective-permute-start | bytes 24584 | tf_op jit(solution)/shard_map/ppermute | solution.py:340
  48.4 4.9 %collective-permute-start.14 = (f32[1,2048]{1,0:T(1,128)S(1)}, f32[1,2048]{1,0:T(1,128)S(1)}, u32[]{:S(2)}, u32[]{:S(2)}) collective-permute-start(f32[1,2048]{1,0:T(1,128)S(1)} %add.23.refs_4_), channel_id=1, source_target_pairs={{0,2},{1,3},{2,0},{3,1},{4,6},{5,7},{6,4},{7,5},{8,10},{9,11},{10,... | collective-permute-start | bytes 24584 | tf_op jit(solution)/shard_map/ppermute | solution.py:340
  49.4 9.3 %collective-permute-start.19 = (bf16[528,128]{1,0:T(8,128)(2,1)S(1)}, bf16[528,128]{1,0:T(8,128)(2,1)S(1)}, u32[]{:S(2)}, u32[]{:S(2)}) collective-permute-start(bf16[528,128]{1,0:T(8,128)(2,1)S(1)} %get-tuple-element.49), channel_id=1, source_target_pairs={{0,24},{8,16},{16,8},{24,0},{1,25},{9,17},{17,9},{25,1},{2,26},{10... | collective-permute-start | bytes 405512 | tf_op jit(solution)/shard_map/ppermute | solution.py:340
  52.7 7.9 %collective-permute-start.20 = (bf16[528,128]{1,0:T(8,128)(2,1)S(1)}, bf16[528,128]{1,0:T(8,128)(2,1)S(1)}, u32[]{:S(2)}, u32[]{:S(2)}) collective-permute-start(bf16[528,128]{1,0:T(8,128)(2,1)S(1)} %get-tuple-element.49), channel_id=1, source_target_pairs={{0,16},{8,24},{16,0},{24,8},{1,17},{9,25},{17,1},{25,9},{2,18},{10... | collective-permute-start | bytes 405512 | tf_op jit(solution)/shard_map/ppermute | solution.py:340
  53.2 7.4 %collective-permute-start.21 = (bf16[528,128]{1,0:T(8,128)(2,1)S(1)}, bf16[528,128]{1,0:T(8,128)(2,1)S(1)}, u32[]{:S(2)}, u32[]{:S(2)}) collective-permute-start(bf16[528,128]{1,0:T(8,128)(2,1)S(1)} %get-tuple-element.49), channel_id=1, source_target_pairs={{0,8},{8,0},{16,24},{24,16},{1,9},{9,1},{17,25},{25,17},{2,10},{10... | collective-permute-start | bytes 405512 | tf_op jit(solution)/shard_map/ppermute | solution.py:340
  54.7 1.5 %collective-permute-start.15 = (f32[256,128]{1,0:T(8,128)S(1)}, f32[256,128]{1,0:T(8,128)S(1)}, u32[]{:S(2)}, u32[]{:S(2)}) collective-permute-start(f32[256,128]{1,0:T(8,128)S(1)} %get-tuple-element.45), channel_id=1, source_target_pairs={{0,1},{1,0},{2,3},{3,2},{4,5},{5,4},{6,7},{7,6},{8,9},{9,8},{10,11... | collective-permute-start | bytes 393224 | tf_op jit(solution)/shard_map/ppermute | solution.py:340
  56.2 14.3 %collective-permute-start.16 = (f32[256,128]{1,0:T(8,128)S(1)}, f32[256,128]{1,0:T(8,128)S(1)}, u32[]{:S(2)}, u32[]{:S(2)}) collective-permute-start(f32[256,128]{1,0:T(8,128)S(1)} %add.24), channel_id=1, source_target_pairs={{0,6},{1,7},{2,4},{3,5},{4,2},{5,3},{6,0},{7,1},{8,14},{9,15},{10,... | collective-permute-start | bytes 393224 | tf_op jit(solution)/shard_map/ppermute | solution.py:340
  58.7 12.3 %collective-permute-start.17 = (f32[256,128]{1,0:T(8,128)S(1)}, f32[256,128]{1,0:T(8,128)S(1)}, u32[]{:S(2)}, u32[]{:S(2)}) collective-permute-start(f32[256,128]{1,0:T(8,128)S(1)} %add.24), channel_id=1, source_target_pairs={{0,4},{1,5},{2,6},{3,7},{4,0},{5,1},{6,2},{7,3},{8,12},{9,13},{10,... | collective-permute-start | bytes 393224 | tf_op jit(solution)/shard_map/ppermute | solution.py:340
  58.7 12.3 %collective-permute-start.18 = (f32[256,128]{1,0:T(8,128)S(1)}, f32[256,128]{1,0:T(8,128)S(1)}, u32[]{:S(2)}, u32[]{:S(2)}) collective-permute-start(f32[256,128]{1,0:T(8,128)S(1)} %add.24), channel_id=1, source_target_pairs={{0,2},{1,3},{2,0},{3,1},{4,6},{5,7},{6,4},{7,5},{8,10},{9,11},{10,... | collective-permute-start | bytes 393224 | tf_op jit(solution)/shard_map/ppermute | solution.py:340
  71.0 1.4 %collective-permute-start.22 = (f32[256,128]{1,0:T(8,128)S(1)}, f32[256,128]{1,0:T(8,128)S(1)}, u32[]{:S(2)}, u32[]{:S(2)}) collective-permute-start(f32[256,128]{1,0:T(8,128)S(1)} %add_add_fusion), channel_id=1, source_target_pairs={{0,1},{1,0},{2,3},{3,2},{4,5},{5,4},{6,7},{7,6},{8,9},{9,8},{10,11... | collective-permute-start | bytes 393224 | tf_op jit(solution)/shard_map/ppermute | solution.py:340
